TPU v7x, 256 devices: a whole 4x4x8 slice. The times are simulated.
256 devices in a mesh: lat: 16 (over y_hi, x, core), lon: 16 (over z, y_lo).
Axes of the slice: x: 4, y: 4 (y_hi: 2, y_lo: 2; y = y_hi * 2 + y_lo), z: 8, core: 2. Of those that a mesh axis runs over, the one named last changes fastest.
Arguments:
- tokens: bfloat16 [2, 192, 384, 192], P(None, 'lat', 'lon'), may hold values from -6 to 6
- w_qkv: bfloat16 [192, 576], replicated, may hold values from -0.4375 to 0.4375
- w_proj: bfloat16 [192, 192], replicated, may hold values from -0.4375 to 0.4375
- w_up: bfloat16 [192, 768], replicated, may hold values from -0.4375 to 0.4375
- w_down: bfloat16 [768, 192], replicated, may hold values from -0.21875 to 0.21875
- earth_bias: float32 [16, 1, 6, 24, 552], P('lat'), may hold values from -2 to 400
- cotangent: bfloat16 [2, 192, 384, 192], P(None, 'lat', 'lon'), may hold values from -6 to 6
Outputs:
- result: bfloat16 [2, 192, 384, 192], P(None, 'lat', 'lon')
- grad_tokens: bfloat16 [2, 192, 384, 192], P(None, 'lat', 'lon')
- grad_qkv: float32 [192, 576], replicated
- grad_proj: float32 [192, 192], replicated
- grad_up: float32 [192, 768], replicated
- grad_down: float32 [768, 192], replicated
- grad_bias: float32 [16, 1, 6, 24, 552], P('lat')
All inputs are finite; a program needn't handle non-finite values.
Results may differ from a plain program's by a relative error of at most 0.029.
Values may be sent and summed in bfloat16 or wider, within the bound.
No kernel may reach another device: no remote copies, remote signals or barrier semaphores. Data moves between devices by JAX's collectives and lax.ppermute only.
A program may use at most 128 MiB of HBM per device.

v0:
```python
from functools import partial
import math

import jax
import jax.numpy as jnp
from jax import lax
from jax.sharding import PartitionSpec as P

WZ = 2
WA = 12
WO = 12


def shifted(block, axis, distance):
    devices = range(lax.axis_size(axis))
    route = [((i - distance) % len(devices), i) for i in devices]
    return lax.ppermute(block, axis, route)


def normalize(values):
    average = jnp.mean(values, axis=-1, keepdims=True)
    centred = values - average
    variance = jnp.mean(centred * centred, axis=-1, keepdims=True)
    return centred * lax.rsqrt(variance + 1e-05)


def exact_gelu(values):
    return jax.nn.gelu(values, approximate=False)


def offset_table(window):
    row_index = jnp.arange(window)[:, None, None]
    col_index = jnp.arange(window)[None, :, None]
    offsets = jnp.arange(2 * window - 1)[None, None, :]
    return (offsets == row_index - col_index + window - 1).astype(jnp.float32)


def region_codes(band, bands, levwins, depth_count, row_count, col_count):
    level_win = jnp.arange(levwins)[:, None, None, None]
    level_pos = jnp.arange(depth_count)[None, :, None, None]
    row_pos = jnp.arange(row_count)[None, None, :, None]
    zone_level = jnp.where(level_win == levwins - 1, level_pos + 1, 0)
    zone_row = jnp.where(band == bands - 1, (row_pos >= row_count // 2).astype(jnp.int32) + 1, 0)
    codes = zone_level * 3 + zone_row + jnp.zeros((1, 1, 1, col_count), jnp.int32)
    return codes.reshape(levwins, depth_count * row_count * col_count)


def window_core(packed, table, region):
    levwins, lonwins, window_len, triple = packed.shape
    width = triple // 3
    heads_count = table.shape[1]
    head_size = width // heads_count
    positions = table.shape[2]
    spread = table.shape[3] // positions
    parts = packed.reshape(levwins, lonwins, window_len, 3, heads_count, head_size)
    queries = parts[:, :, :, 0]
    key_rows = parts[:, :, :, 1]
    value_rows = parts[:, :, :, 2]
    scores = jnp.einsum(
        "lnihd,lnjhd->lnhij", queries, key_rows, preferred_element_type=jnp.float32
    ) * head_size ** (-0.5)
    biases = jnp.einsum(
        "lhpqs,abs->lhpaqb",
        table.reshape(levwins, heads_count, positions, positions, spread),
        offset_table((spread + 1) // 2),
        precision=lax.Precision.HIGHEST,
    )
    scores = scores + biases.reshape(levwins, heads_count, window_len, window_len)[:, None]
    same_region = region[:, :, None] == region[:, None, :]
    scores = jnp.where(same_region[:, None, None], scores, -1e30)
    maxima = lax.stop_gradient(jnp.max(scores, axis=-1, keepdims=True))
    exponent = jnp.exp(scores - maxima)
    probability = (exponent / jnp.sum(exponent, axis=-1, keepdims=True)).astype(jnp.bfloat16)
    attended = jnp.einsum(
        "lnhij,lnjhd->lnihd", probability, value_rows, preferred_element_type=jnp.float32
    )
    return attended.reshape(levwins, lonwins, window_len, width).astype(jnp.bfloat16)


def to_windows(block):
    levels, row_count, col_count, width = block.shape
    shaped = block.reshape(levels // WZ, WZ, row_count, col_count // WO, WO, width)
    return shaped.transpose(0, 3, 1, 2, 4, 5).reshape(
        levels // WZ, col_count // WO, WZ * row_count * WO, width
    )


def from_windows(windows, levels, col_count):
    width = windows.shape[-1]
    shaped = windows.reshape(levels // WZ, col_count // WO, WZ, WA, WO, width)
    return shaped.transpose(0, 2, 3, 1, 4, 5).reshape(levels, WA, col_count, width)


def roll_forward(stacked):
    half_row = WA // 2
    half_col = WO // 2
    arrived = shifted(stacked[:, :, :half_row], "lat", -1)
    stacked = jnp.concatenate([stacked[:, :, half_row:], arrived], axis=2)
    arrived = shifted(stacked[:, :, :, :half_col], "lon", -1)
    stacked = jnp.concatenate([stacked[:, :, :, half_col:], arrived], axis=3)
    return jnp.roll(stacked, -1, axis=1)


def roll_back(stacked):
    half_row = WA // 2
    half_col = WO // 2
    arrived = shifted(stacked[:, :, -half_row:], "lat", 1)
    stacked = jnp.concatenate([arrived, stacked[:, :, :-half_row]], axis=2)
    arrived = shifted(stacked[:, :, :, -half_col:], "lon", 1)
    stacked = jnp.concatenate([arrived, stacked[:, :, :, :-half_col]], axis=3)
    return jnp.roll(stacked, 1, axis=1)


def on_device(tokens, w_qkv, w_proj, w_up, w_down, earth_bias, cotangent):
    band = lax.axis_index("lat")
    bands = lax.axis_size("lat")
    levels, row_count, col_count, width = tokens.shape
    hidden_width = w_up.shape[1]
    table = earth_bias[0]
    region = region_codes(band, bands, levels // WZ, WZ, row_count, WO)
    inputs = tokens.astype(jnp.float32)
    normed = normalize(inputs).astype(jnp.bfloat16)
    rolled = roll_forward(normed[None])[0]
    windows = to_windows(rolled)
    packed = jnp.dot(windows, w_qkv, preferred_element_type=jnp.float32).astype(jnp.bfloat16)
    attended, core_back = jax.vjp(partial(window_core, region=region), packed, table)
    mixed = jnp.dot(attended, w_proj, preferred_element_type=jnp.float32).astype(jnp.bfloat16)
    placed = from_windows(mixed, levels, col_count)
    placed = roll_back(placed[None])[0]
    residual = inputs + placed.astype(jnp.float32)
    normed_two = normalize(residual).astype(jnp.bfloat16)
    upper = jnp.dot(normed_two, w_up, preferred_element_type=jnp.float32)
    activated, gelu_back = jax.vjp(exact_gelu, upper)
    activated = activated.astype(jnp.bfloat16)
    result = (residual + jnp.dot(activated, w_down, preferred_element_type=jnp.float32)).astype(
        jnp.bfloat16
    )
    grad_down = jnp.dot(
        activated.reshape(-1, hidden_width).T,
        cotangent.reshape(-1, width),
        preferred_element_type=jnp.float32,
    )
    grad_act = jnp.dot(cotangent, w_down.T, preferred_element_type=jnp.float32).astype(jnp.bfloat16)
    grad_upper = gelu_back(grad_act.astype(jnp.float32))[0].astype(jnp.bfloat16)
    grad_up = jnp.dot(
        normed_two.reshape(-1, width).T,
        grad_upper.reshape(-1, hidden_width),
        preferred_element_type=jnp.float32,
    )
    grad_normed_two = jnp.dot(grad_upper, w_up.T, preferred_element_type=jnp.float32).astype(
        jnp.bfloat16
    )
    grad_residual = (
        cotangent.astype(jnp.float32)
        + jax.vjp(normalize, residual)[1](grad_normed_two.astype(jnp.float32))[0]
    )
    grad_placed = grad_residual.astype(jnp.bfloat16)
    grad_placed = roll_forward(grad_placed[None])[0]
    grad_mixed = to_windows(grad_placed)
    grad_proj = jnp.dot(
        attended.reshape(-1, width).T,
        grad_mixed.reshape(-1, width),
        preferred_element_type=jnp.float32,
    )
    grad_attended = jnp.dot(grad_mixed, w_proj.T, preferred_element_type=jnp.float32).astype(
        jnp.bfloat16
    )
    grad_packed, grad_table = core_back(grad_attended)
    grad_qkv = jnp.dot(
        windows.reshape(-1, width).T,
        grad_packed.reshape(-1, 3 * width),
        preferred_element_type=jnp.float32,
    )
    grad_windows = jnp.dot(grad_packed, w_qkv.T, preferred_element_type=jnp.float32).astype(
        jnp.bfloat16
    )
    grad_normed = from_windows(grad_windows, levels, col_count)
    grad_normed = roll_back(grad_normed[None])[0]
    grad_tokens = (
        grad_residual + jax.vjp(normalize, inputs)[1](grad_normed.astype(jnp.float32))[0]
    ).astype(jnp.bfloat16)
    qkv_sum, proj_sum, up_sum, down_sum = lax.psum(
        (grad_qkv, grad_proj, grad_up, grad_down), ("lat", "lon")
    )
    table_sum = lax.psum(grad_table.astype(jnp.bfloat16), "lon").astype(jnp.float32)
    square_total = (
        jnp.sum(qkv_sum * qkv_sum)
        + jnp.sum(proj_sum * proj_sum)
        + jnp.sum(up_sum * up_sum)
        + jnp.sum(down_sum * down_sum)
    )
    count = w_qkv.size + w_proj.size + w_up.size + w_down.size + table.size * bands
    factor = jnp.minimum(1.0, math.sqrt(count) / (jnp.sqrt(square_total) + 1e-06))
    return (
        result,
        grad_tokens,
        qkv_sum * factor,
        proj_sum * factor,
        up_sum * factor,
        down_sum * factor,
        (table_sum * factor)[None],
    )


def solution(mesh):
    placed = (
        P(None, "lat", "lon", None),
        P(),
        P(),
        P(),
        P(),
        P("lat", None, None, None, None),
        P(None, "lat", "lon", None),
    )
    return jax.shard_map(
        on_device,
        mesh=mesh,
        in_specs=placed,
        out_specs=(
            P(None, "lat", "lon", None),
            P(None, "lat", "lon", None),
            P(),
            P(),
            P(),
            P(),
            P("lat", None, None, None, None),
        ),
        check_vma=False,
    )
```

profile of v0, /device:TPU:2, one launch (start us, length us, event | category | flops | bytes accessed | tf_op | source)
XLA Modules:
  0.0 565.6 jit_solution(7304966259573341744)
XLA Ops:
  12.6 8.8 %convolution_bitcast_fusion = f32[1,6,24,12,24,12]{4,5,2,1,3,0:T(8,128)} fusion(f32[6,24,24,23,1]{3,2,1,0,4:T(8,128)S(1)} %reshape.385, s32[12,12]{1,0:T(8,128)S(1)} %subtract_add_fusion), kind=kOutput, calls=%fused_computation.3 | convolution fusion | flops 137358576 | bytes 2309184 | tf_op jit(solution)/shard_map/jvp(lhpqs,abs->lhpaqb)/dot_general | solution.py:62
  21.5 26.3 %copy.105 = f32[1,6,24,12,24,12]{3,2,5,4,1,0:T(8,128)} copy(f32[1,6,24,12,24,12]{4,5,2,1,3,0:T(8,128)} %convolution_bitcast_fusion) | data formatting | bytes 3981312 | tf_op jit(solution)/shard_map/jvp()/add | solution.py:68
  47.9 14.1 %reshape.393 = f32[6,288,288]{1,2,0:T(8,128)} reshape(f32[1,6,24,12,24,12]{3,2,5,4,1,0:T(8,128)} %copy.105) | data formatting | bytes 3981312 | tf_op jit(solution)/shard_map/jvp()/add | solution.py:68
  62.0 7.1 %collective-permute-start.1 = (bf16[1,2,12,6,192]{4,3,2,1,0:T(8,128)(2,1)S(1)}, bf16[1,2,12,6,192]{4,3,2,1,0:T(8,128)(2,1)S(1)}, u32[]{:S(2)}, u32[]{:S(2)}) collective-permute-start(bf16[1,2,12,6,192]{4,3,2,1,0:T(8,128)(2,1)S(1)} %pad_maximum_fusion.5), channel_id=1, source_target_pairs={{1,0},{2,1},{3,2},{4,3},{5,4},{6,5},{7,6},{8,7},{9,8},{10,9},{11,1... | collective-permute-start | bytes 165896 | tf_op jit(solution)/shard_map/ppermute | solution.py:17
  69.2 2.6 collective-permute-done.1
  73.9 6.5 %fusion.111 = (f32[2,6,288]{2,1,0:T(8,128)S(1)}, f32[2,6,288,288]{2,3,1,0:T(8,128)}) fusion(f32[6,288,288]{1,2,0:T(8,128)} %reshape.393, pred[288,288]{0,1:T(8,128)(4,1)S(1)} %broadcast_compare_fusion, bf16[1,2,288,3,6,32]{2,5,4,3,1,0:T(8,128)(2,1)S(1)} %bitcast.206), kind=kOutput, calls=%fused_computation.189 | convolution fusion | flops 68677920 | bytes 6686208 | tf_op jit(solution)/shard_map/jvp()/sub | solution.py:72
  80.4 2.9 divide_convert_fusion
  83.4 1.5 convolution_convert_fusion.8
  86.2 4.6 collective-permute-done.2
  93.9 1.8 reshape_reshape.6
  96.7 1.9 convert_element_type.192
  98.6 1.3 collective-permute-done.3
  103.3 4.0 multiply_convert_fusion
  108.7 1.6 convolution_bitcast_fusion.2
  113.7 1.4 collective-permute-done.4
  115.1 4.0 collective-permute-start.5
  119.2 2.6 collective-permute-done.5
  123.9 1.6 fusion.43
  125.6 1.5 fusion.46
  130.0 2.8 fusion.103
  138.1 1.9 fusion.113
  139.9 2.3 copy.89
  142.3 11.1 %broadcast_in_dim.99 = f32[1,6,24,12,24,12]{5,4,3,2,1,0:T(8,128)} reshape(f32[6,288,288]{2,1,0:T(8,128)S(1)} %copy.89) | data formatting | bytes 3981312 | tf_op jit(solution)/shard_map/transpose(jvp())/reshape;transpose(jvp())/broadcast_in_dim | solution.py:68
  154.7 15.6 %bitcast_convert_fusion = bf16[6,24,24,23]{3,2,1,0:T(8,128)(2,1)S(1)} fusion(f32[1,6,24,12,24,12]{5,4,3,2,1,0:T(8,128)} %broadcast_in_dim.99, s32[12,12]{1,0:T(8,128)S(1)} %copy-done.43), kind=kOutput, calls=%fused_computation.42 | convolution fusion | flops 137438064 | bytes 2150208 | tf_op jit(solution)/shard_map/transpose(jvp(lhpqs,abs->lhpaqb))/dot_general | solution.py:62
  172.5 1.5 add_convert_fusion
  174.0 247.5 %all-reduce.9.cloned.1.call-done = (f32[192,576]{1,0:T(8,128)}, f32[192,192]{1,0:T(8,128)}, f32[192,768]{1,0:T(8,128)}, f32[768,192]{0,1:T(8,128)}) async-done(((f32[192,576]{1,0:T(8,128)}, f32[192,192]{1,0:T(8,128)}, f32[192,768]{1,0:T(8,128)}, f32[768,192]{0,1:T(8,128)}), (f32[192,576]{1,0:T(8,128)}, f32[192,192]{1,0:T(8,128)}, f32[192,768]{1,0:T(8,128)}, ...) | async-done | bytes 1769488 | tf_op jit(solution)/shard_map/psum | solution.py:182
  421.6 1.8 multiply_reduce_fusion.4
  423.4 1.6 multiply_reduce_fusion.5
  425.1 1.8 multiply_reduce_fusion.1
  426.9 1.8 multiply_reduce_fusion
  434.7 122.2 %all-reduce.7.cloned.1.call-done = bf16[1,6,24,552]{3,2,1,0:T(8,128)(2,1)} async-done(((bf16[1,6,24,552]{3,2,1,0:T(8,128)(2,1)}), bf16[1,6,24,552]{3,2,1,0:T(8,128)(2,1)}) %all-reduce.7.cloned.1.call-update) | async-done | bytes 158992 | tf_op jit(solution)/shard_map/psum | solution.py:185
  556.9 1.7 multiply_bitcast_fusion
  (191 shorter events, 37.6 us)
Async XLA Ops:
  7.2 95.2 %copy-start = (bf16[192,768]{1,0:T(8,128)(2,1)S(1)}, bf16[192,768]{1,0:T(8,128)(2,1)}, u32[]{:S(2)}) copy-start(bf16[192,768]{1,0:T(8,128)(2,1)} %param.10) | copy-start | bytes 884740
  7.2 4.5 copy-start.27
  7.2 414.4 %all-reduce.9.cloned.1.call-start = ((), (), s32[]{:S(2)}) async-start(), calls=%async_computation.1 | async-start | bytes 3735552 | tf_op jit(solution)/shard_map/psum | solution.py:182
  11.5 50.4 %collective-permute-start = (bf16[1,2,6,24,192]{4,3,2,1,0:T(8,128)(2,1)S(1)}, bf16[1,2,6,24,192]{4,3,2,1,0:T(8,128)(2,1)S(1)}, u32[]{:S(2)}, u32[]{:S(2)}) collective-permute-start(bf16[1,2,6,24,192]{4,3,2,1,0:T(8,128)(2,1)S(1)} %get-tuple-element.24), channel_id=1, source_target_pairs={{16,0},{32,16},{48,32},{64,48},{80,64},{96,80},{112,96},{128,112},... | collective-permute-start | bytes 331784 | tf_op jit(solution)/shard_map/ppermute | solution.py:17
  11.6 9.8 %copy-start.42 = (s32[12,12]{1,0:T(8,128)}, s32[12,12]{1,0:T(8,128)S(1)}, u32[]{:S(2)}) copy-start(s32[12,12]{1,0:T(8,128)S(1)} %subtract_add_fusion) | copy-start | bytes 1732
  21.5 52.4 %copy-start.23 = (pred[288,288]{0,1:T(8,128)(4,1)}, pred[288,288]{0,1:T(8,128)(4,1)S(1)}, u32[]{:S(2)}) copy-start(pred[288,288]{0,1:T(8,128)(4,1)S(1)} %broadcast_compare_fusion) | copy-start | bytes 248836
  61.9 11.0 %copy-start.17 = (bf16[192,576]{1,0:T(8,128)(2,1)S(1)}, bf16[192,576]{1,0:T(8,128)(2,1)}, u32[]{:S(2)}) copy-start(bf16[192,576]{1,0:T(8,128)(2,1)} %param.8) | copy-start | bytes 663556
  62.0 9.8 %collective-permute-start.1 = (bf16[1,2,12,6,192]{4,3,2,1,0:T(8,128)(2,1)S(1)}, bf16[1,2,12,6,192]{4,3,2,1,0:T(8,128)(2,1)S(1)}, u32[]{:S(2)}, u32[]{:S(2)}) collective-permute-start(bf16[1,2,12,6,192]{4,3,2,1,0:T(8,128)(2,1)S(1)} %pad_maximum_fusion.5), channel_id=1, source_target_pairs={{1,0},{2,1},{3,2},{4,3},{5,4},{6,5},{7,6},{8,7},{9,8},{10,9},{11,1... | collective-permute-start | bytes 165896 | tf_op jit(solution)/shard_map/ppermute | solution.py:17
  73.9 6.5 %copy-start.9 = (bf16[2,288,576]{1,2,0:T(8,128)(2,1)}, bf16[2,288,576]{1,2,0:T(8,128)(2,1)S(1)}, u32[]{:S(2)}) copy-start(bf16[2,288,576]{1,2,0:T(8,128)(2,1)S(1)} %copy.61) | copy-start | bytes 1990660
  85.0 7.5 %copy-start.35 = (f32[2,6,288]{2,1,0:T(8,128)S(1)}, f32[2,6,288]{2,1,0:T(8,128)}, u32[]{:S(2)}) copy-start(f32[2,6,288]{2,1,0:T(8,128)} %copy-done.34) | copy-start | bytes 41476
  85.0 8.1 %copy-start.8 = (bf16[1,2,12,24,192]{4,1,3,2,0:T(2,128)(2,1)S(1)}, bf16[1,2,12,24,192]{4,1,3,2,0:T(2,128)(2,1)}, u32[]{:S(2)}) copy-start(bf16[1,2,12,24,192]{4,1,3,2,0:T(2,128)(2,1)} %copy-done.7) | copy-start | bytes 663556
  86.2 4.6 collective-permute-start.2
  90.8 10.1 %copy-start.2 = (bf16[2,12,24,192]{3,2,1,0:T(8,128)(2,1)S(1)}, bf16[2,12,24,192]{3,2,1,0:T(8,128)(2,1)}, u32[]{:S(2)}) copy-start(bf16[2,12,24,192]{3,2,1,0:T(8,128)(2,1)} %param.7) | copy-start | bytes 663556
  92.2 7.7 %collective-permute-start.3 = (bf16[1,2,12,6,192]{4,3,2,1,0:T(8,128)(2,1)}, bf16[1,2,12,6,192]{4,3,2,1,0:T(8,128)(2,1)}, u32[]{:S(2)}, u32[]{:S(2)}) collective-permute-start(bf16[1,2,12,6,192]{4,3,2,1,0:T(8,128)(2,1)} %slice.123), channel_id=1, source_target_pairs={{15,0},{0,1},{1,2},{2,3},{3,4},{4,5},{5,6},{6,7},{7,8},{8,9},{9,10... | collective-permute-start | bytes 165896 | tf_op jit(solution)/shard_map/ppermute | solution.py:17
  102.4 9.5 %copy-start.30 = (f32[2,12,24]{2,1,0:T(8,128)}, f32[2,12,24]{2,1,0:T(8,128)S(1)}, u32[]{:S(2)}) copy-start(f32[2,12,24]{2,1,0:T(8,128)S(1)} %fusion.95) | copy-start | bytes 6916
  103.2 4.0 copy-start.5
  103.3 4.0 copy-start.44
  108.7 14.2 %slice-start = ((s8[5308416]{0:T(1024)(128)(4,1)}), s8[4194304]{0:T(1024)(128)(4,1)S(1)}, s32[]{:S(2)}) async-start(s8[5308416]{0:T(1024)(128)(4,1)} %bitcast.191), calls=%async_computation.2 | async-start | bytes 8388608
  111.4 11.5 %slice-start.1 = ((s8[5308416]{0:T(1024)(128)(4,1)}), s8[1114112]{0:T(1024)(128)(4,1)S(1)}, s32[]{:S(2)}) async-start(s8[5308416]{0:T(1024)(128)(4,1)} %bitcast.191), calls=%async_computation.3 | async-start | bytes 2228224
  112.3 2.8 collective-permute-start.4
  115.1 7.5 %copy-start.26 = (bf16[192,192]{1,0:T(8,128)(2,1)S(1)}, bf16[192,192]{1,0:T(8,128)(2,1)}, u32[]{:S(2)}) copy-start(bf16[192,192]{1,0:T(8,128)(2,1)} %param.9) | copy-start | bytes 221188
  115.1 6.8 %collective-permute-start.5 = (bf16[1,2,12,6,192]{4,3,2,1,0:T(8,128)(2,1)S(1)}, bf16[1,2,12,6,192]{4,3,2,1,0:T(8,128)(2,1)S(1)}, u32[]{:S(2)}, u32[]{:S(2)}) collective-permute-start(bf16[1,2,12,6,192]{4,3,2,1,0:T(8,128)(2,1)S(1)} %pad_maximum_fusion.4), channel_id=1, source_target_pairs={{1,0},{2,1},{3,2},{4,3},{5,4},{6,5},{7,6},{8,7},{9,8},{10,9},{11,1... | collective-permute-start | bytes 165896 | tf_op jit(solution)/shard_map/ppermute | solution.py:17
  119.2 3.7 copy-start.10
  119.2 3.7 copy-start.41
  135.5 18.0 %collective-permute-start.6 = (bf16[1,2,6,24,192]{4,3,2,1,0:T(8,128)(2,1)}, bf16[1,2,6,24,192]{4,3,2,1,0:T(8,128)(2,1)}, u32[]{:S(2)}, u32[]{:S(2)}) collective-permute-start(bf16[1,2,6,24,192]{4,3,2,1,0:T(8,128)(2,1)} %copy.112), channel_id=1, source_target_pairs={{240,0},{0,16},{16,32},{32,48},{48,64},{64,80},{80,96},{96,112},{1... | collective-permute-start | bytes 331784 | tf_op jit(solution)/shard_map/ppermute | solution.py:17
  153.4 403.5 %all-reduce.7.cloned.1.call-start = ((), (), s32[]{:S(2)}) async-start(), calls=%async_computation | async-start | bytes 368640 | tf_op jit(solution)/shard_map/psum | solution.py:185
  154.5 17.1 %collective-permute-start.7 = (bf16[1,2,12,6,192]{4,3,2,1,0:T(8,128)(2,1)S(1)}, bf16[1,2,12,6,192]{4,3,2,1,0:T(8,128)(2,1)S(1)}, u32[]{:S(2)}, u32[]{:S(2)}) collective-permute-start(bf16[1,2,12,6,192]{4,3,2,1,0:T(8,128)(2,1)S(1)} %slice.135), channel_id=1, source_target_pairs={{15,0},{0,1},{1,2},{2,3},{3,4},{4,5},{5,6},{6,7},{7,8},{8,9},{9,10... | collective-permute-start | bytes 165896 | tf_op jit(solution)/shard_map/ppermute | solution.py:17
  421.6 9.9 %copy-start.14 = (f32[192,576]{1,0:T(8,128)S(1)}, f32[192,576]{1,0:T(8,128)}, u32[]{:S(2)}) copy-start(f32[192,576]{1,0:T(8,128)} %get-tuple-element.9) | copy-start | bytes 1327108
  421.6 10.7 %copy-start.13 = (f32[192,768]{1,0:T(8,128)S(1)}, f32[192,768]{1,0:T(8,128)}, u32[]{:S(2)}) copy-start(f32[192,768]{1,0:T(8,128)} %get-tuple-element.11) | copy-start | bytes 1769476
  423.4 9.7 %copy-start.12 = (f32[768,192]{0,1:T(8,128)S(1)}, f32[768,192]{0,1:T(8,128)}, u32[]{:S(2)}) copy-start(f32[768,192]{0,1:T(8,128)} %get-tuple-element.12) | copy-start | bytes 1769476
  428.7 5.3 copy-start.19
  431.4 127.1 %copy-start.1 = (bf16[192,768]{1,0:T(8,128)(2,1)S(1)}, bf16[192,768]{1,0:T(8,128)(2,1)}, u32[]{:S(2)}) copy-start(bf16[192,768]{1,0:T(8,128)(2,1)} %param.10) | copy-start | bytes 884740
  (25 other events, 46.2 us)
Sparse Core Ops, SparseCore 0:
  153.5 268.0 all-reduce.8
  424.8 132.0 all-reduce.6
where the time goes:
time: 573 us; the launch traced here: 566 us
  waiting for transfers between devices  382 us (67%)
  local copies, waits for them, and re-layouts  72.3 us (13%)
  matrix products  48.1 us (8%)
  other arithmetic  32.4 us (6%)
  between operations  18.1 us (3%)
  starting transfers between devices  12.5 us (2%)
    psum x1, waiting for transfers between devices, on_device(): lax.psum((grad_qkv, grad_proj, grad_up, grad_down), ('lat', 'lon'))  248 us
    psum x1, waiting for transfers between devices, on_device(): lax.psum(grad_table.astype(jnp.bfloat16), 'lon').astype(jnp.float32)  122 us
    add x2, local copies, waits for them, and re-layouts, window_core(): scores + biases.reshape(levwins, heads_count, window_len, window_len)[:,...  40.4 us
    dot_general x2, matrix products, window_core(): jnp.einsum('lhpqs,abs->lhpaqb', table.reshape(levwins, heads_count, posit...  24.3 us
    ppermute x8, waiting for transfers between devices, shifted(): return lax.ppermute(block, axis, route)  12.5 us
    ppermute x8, starting transfers between devices, shifted(): return lax.ppermute(block, axis, route)  12.4 us
  transfers between devices with their start and end apart: 10, of which 7 were waited for; matrix products, arithmetic and copies ran while one was open for 19% of the time, Pallas kernels for 0%

commit v1 on v0

v1 whole, which is shorter than its diff:
```python
import functools
import math

import jax
import jax.numpy as jnp
import numpy as np
from jax import lax
from jax.experimental import pallas as pl
from jax.experimental.pallas import tpu as pltpu
from jax.sharding import PartitionSpec as P

WA = 12
WO = 12
HALF = 6
HEADS = 6
HEAD = 32
WIN = WA * WO
SPAN = 2 * WO - 1
CUT = WA * SPAN
WIDE = 384
LANES = 128
C = 192
HID = 768
TOKENS = 576
PARTS = 4
PACKED = 1792
EPS = 1e-05
SCALE = HEAD ** (-0.5)
VMEM = 48 * 1024 * 1024
BF = jnp.bfloat16
F32 = jnp.float32


def table_order():
    lane = np.arange(CUT)
    order = np.zeros((CUT, WIDE), np.float32)
    order[(lane % WA) * SPAN + SPAN - 1 - lane // WA, lane] = 1.0
    return order


def table_back():
    back = np.zeros((2, WIDE, 2 * CUT), np.float32)
    for level in range(2):
        back[level, :, level * CUT : (level + 1) * CUT] = table_order().T
    return back


def dot(a, b):
    return jnp.dot(a, b, preferred_element_type=F32)


def dot_rt(a, b):
    return lax.dot_general(a, b, (((1,), (1,)), ((), ())), preferred_element_type=F32)


def dot_lt(a, b):
    return lax.dot_general(a, b, (((0,), (0,)), ((), ())), preferred_element_type=F32)


def normal(values):
    centred = values - jnp.mean(values, axis=-1, keepdims=True)
    variance = jnp.mean(centred * centred, axis=-1, keepdims=True)
    inverse = lax.rsqrt(variance + EPS)
    return centred * inverse, inverse


def normal_back(unit, inverse, grad):
    first = jnp.mean(grad, axis=-1, keepdims=True)
    second = jnp.mean(grad * unit, axis=-1, keepdims=True)
    return inverse * (grad - first - unit * second)


def bias_kernel(last_ref, table_ref, order_ref, bias_ref):
    order = order_ref[...]
    table = table_ref[...]
    high = table.astype(BF)
    rest = table - high.astype(F32)
    middle = rest.astype(BF)
    low = (rest - middle.astype(F32)).astype(BF)
    wide = dot(high, order) + (dot(middle, order) + dot(low, order))
    row = lax.broadcasted_iota(jnp.int32, (2 * WA, WIDE), 0)
    row_i = lax.broadcasted_iota(jnp.int32, (2 * WA, WIN), 0) % WA
    row_j = lax.broadcasted_iota(jnp.int32, (2 * WA, WIN), 1) % WA
    split = (row_i >= HALF) != (row_j >= HALF)
    split = jnp.logical_and(split, last_ref[0] == 1)
    for level in range(2):
        for head in range(HEADS):
            at = (level * HEADS + head) * 2 * WA
            both = wide[at : at + 2 * WA]
            both = jnp.where(row < WA, pltpu.roll(both, WIDE - WA, 1), both)
            for pair in range(WO // 2):
                turn = (WO - 2 - 2 * pair) * WA
                block = pltpu.roll(both, (WIDE - turn) % WIDE, 1)[:, :WIN]
                start = head * WIN + pair * 2 * WA
                bias_ref[level, start : start + 2 * WA, :] = jnp.where(split, -1e30, block)


def block_kernel(
    core_ref, x_ref, cot_ref, wq_ref, wk_ref, wv_ref, proj_ref, up_ref, down_ref, bias_ref,
    result_ref, gtok_ref, mine_ref, other_ref, gbias_ref,
    normed_ref, q_ref, k_ref, v_ref, prob_ref, att_ref, res_ref, two_ref, upper_ref, gact_ref, act_ref,
    gup_ref, gres_ref, gmix_ref, gatt_ref, dq_ref, dk_ref, dv_ref, ds_ref,
):
    lane = lax.broadcasted_iota(jnp.int32, (1, C), 1) // HEAD
    masks = [(lane == head).astype(F32) for head in range(HEADS)]
    half_masks = [mask.astype(BF) for mask in masks]

    def rows_of(part):
        return pl.ds(pl.multiple_of(part * WIN, WIN), WIN)

    def first_norm(part, carry):
        rows = rows_of(part)
        unit, _ = normal(x_ref[rows, :].astype(F32))
        normed_ref[rows, :] = unit.astype(BF)
        return carry

    lax.fori_loop(0, PARTS, first_norm, 0)
    normed = normed_ref[...]
    q_ref[...] = dot(normed, wq_ref[...]).astype(BF)
    k_ref[...] = dot(normed, wk_ref[...]).astype(BF)
    v_ref[...] = dot(normed, wv_ref[...]).astype(BF)

    def attend(part, carry):
        rows = rows_of(part)
        query, key, value = q_ref[rows, :], k_ref[rows, :], v_ref[rows, :]
        level = part % 2
        total = jnp.zeros((WIN, C), F32)
        for head in range(HEADS):
            chunk = slice(head * WIN, (head + 1) * WIN)
            scores = dot_rt(query * half_masks[head], key) * SCALE + bias_ref[level, chunk, :]
            exponent = jnp.exp(scores - jnp.max(scores, axis=-1, keepdims=True))
            prob = exponent / jnp.sum(exponent, axis=-1, keepdims=True)
            prob = prob.astype(BF)
            prob_ref[part, chunk, :] = prob
            total = total + dot(prob, value) * masks[head]
        att_ref[rows, :] = total.astype(BF)
        return carry

    lax.fori_loop(0, PARTS, attend, 0)
    res_ref[...] = dot(att_ref[...], proj_ref[...])

    def second_norm(part, carry):
        rows = rows_of(part)
        residual = x_ref[rows, :].astype(F32) + res_ref[rows, :].astype(BF).astype(F32)
        res_ref[rows, :] = residual
        unit, _ = normal(residual)
        two_ref[rows, :] = unit.astype(BF)
        return carry

    lax.fori_loop(0, PARTS, second_norm, 0)
    upper_ref[...] = dot(two_ref[...], up_ref[...])
    gact_ref[...] = dot_rt(cot_ref[...], down_ref[...]).astype(BF)
    step = 32

    def gelu(chunk, carry):
        rows = pl.ds(pl.multiple_of(chunk * step, step), step)
        upper = upper_ref[rows, :]
        cdf = 0.5 + 0.5 * lax.erf(upper * math.sqrt(0.5))
        pdf = jnp.exp(upper * upper * -0.5) * (1.0 / math.sqrt(2.0 * math.pi))
        act_ref[rows, :] = (upper * cdf).astype(BF)
        gup_ref[rows, :] = (gact_ref[rows, :].astype(F32) * (cdf + upper * pdf)).astype(BF)
        return carry

    lax.fori_loop(0, TOKENS // step, gelu, 0)
    result_ref[...] = (res_ref[...] + dot(act_ref[...], down_ref[...])).astype(BF)
    gres_ref[...] = dot_rt(gup_ref[...], up_ref[...])

    def second_back(part, carry):
        rows = rows_of(part)
        unit, inverse = normal(res_ref[rows, :])
        grad = gres_ref[rows, :].astype(BF).astype(F32)
        grad = cot_ref[rows, :].astype(F32) + normal_back(unit, inverse, grad)
        gres_ref[rows, :] = grad
        gmix_ref[rows, :] = grad.astype(BF)
        return carry

    lax.fori_loop(0, PARTS, second_back, 0)
    gatt_ref[...] = dot_rt(gmix_ref[...], proj_ref[...]).astype(BF)
    ds_ref[...] = jnp.zeros(ds_ref.shape, F32)

    def attend_back(part, carry):
        rows = rows_of(part)
        query, key, value = q_ref[rows, :], k_ref[rows, :], v_ref[rows, :]
        gatt = gatt_ref[rows, :]
        level = part % 2
        gquery = jnp.zeros((WIN, C), F32)
        gkey = jnp.zeros((WIN, C), F32)
        gvalue = jnp.zeros((WIN, C), F32)
        for head in range(HEADS):
            chunk = slice(head * WIN, (head + 1) * WIN)
            prob = prob_ref[part, chunk, :]
            own = gatt * half_masks[head]
            gprob = dot_rt(own, value)
            weight = prob.astype(F32)
            gscore = weight * (gprob - jnp.sum(weight * gprob, axis=-1, keepdims=True))
            ds_ref[level, chunk, :WIN] += gscore
            gscore = (gscore * SCALE).astype(BF)
            gquery = gquery + dot(gscore, key) * masks[head]
            gkey = gkey + dot_lt(gscore, query * half_masks[head])
            gvalue = gvalue + dot_lt(prob, own)
        dq_ref[rows, :] = gquery.astype(BF)
        dk_ref[rows, :] = gkey.astype(BF)
        dv_ref[rows, :] = gvalue.astype(BF)
        return carry

    lax.fori_loop(0, PARTS, attend_back, 0)
    normed_grad = dot_rt(dq_ref[...], wq_ref[...])
    normed_grad = normed_grad + dot_rt(dk_ref[...], wk_ref[...])
    res_ref[...] = normed_grad + dot_rt(dv_ref[...], wv_ref[...])

    def first_back(part, carry):
        rows = rows_of(part)
        unit, inverse = normal(x_ref[rows, :].astype(F32))
        grad = res_ref[rows, :].astype(BF).astype(F32)
        gtok_ref[rows, :] = (gres_ref[rows, :] + normal_back(unit, inverse, grad)).astype(BF)
        return carry

    lax.fori_loop(0, PARTS, first_back, 0)
    first = core_ref[0] == 0

    def put(start, zero, one):
        rows = slice(start, start + zero.shape[0])
        mine_ref[rows, :] = jnp.where(first, zero, one)
        other_ref[rows, :] = jnp.where(first, one, zero).astype(BF)

    gup = dot_lt(two_ref[...], gup_ref[...])
    gdown = dot_lt(act_ref[...], cot_ref[...])
    for chunk in range(4):
        put(chunk * C, gup[:, chunk * LANES : (chunk + 1) * LANES], gdown[chunk * C : (chunk + 1) * C, :LANES])
    for chunk in range(4, 6):
        left = (chunk - 4) * C
        pair = jnp.concatenate([gdown[left : left + C, LANES:], gdown[2 * C + left : 3 * C + left, LANES:]], axis=1)
        put(chunk * C, gup[:, chunk * LANES : (chunk + 1) * LANES], pair)
    normed = normed_ref[...]
    gq = dot_lt(normed, dq_ref[...])
    gk = dot_lt(normed, dk_ref[...])
    gv = dot_lt(normed, dv_ref[...])
    gproj = dot_lt(att_ref[...], gmix_ref[...])
    put(6 * C, gq[:, :LANES], gproj[:, :LANES])
    put(7 * C, gk[:, :LANES], jnp.concatenate([gq[:, LANES:], gk[:, LANES:]], axis=1))
    put(8 * C, gv[:, :LANES], jnp.concatenate([gv[:, LANES:], gproj[:, LANES:]], axis=1))
    mine_ref[9 * C :, :] = jnp.zeros((PACKED - 9 * C, LANES), F32)
    other_ref[9 * C :, :] = jnp.zeros((PACKED - 9 * C, LANES), BF)

    row = lax.broadcasted_iota(jnp.int32, (2 * WA, WIDE), 0)
    for level in range(2):
        for head in range(HEADS):
            total = jnp.zeros((2 * WA, WIDE), F32)
            for pair in range(WO // 2):
                start = head * WIN + pair * 2 * WA
                turn = (WO - 2 - 2 * pair) * WA
                block = ds_ref[level, start : start + 2 * WA, :]
                total = total + (pltpu.roll(block, turn, 1) if turn else block)
            total = jnp.where(row < WA, pltpu.roll(total, WA, 1), total)
            total = total + pltpu.roll(total, WA, 0)
            gbias_ref[level * HEADS + head] = total[:16].astype(BF)
    gbias_ref[2 * HEADS :] = jnp.zeros((16 - 2 * HEADS, 16, WIDE), BF)


def final_kernel(
    count, core_ref, mine_ref, other_ref, gbias_ref, back_ref,
    qkv_ref, proj_ref, up_ref, down_ref, bias_ref,
):
    first = core_ref[0] == 0
    mine = mine_ref[...].astype(F32)
    other = other_ref[...].astype(F32)
    total = jnp.sum(mine * mine) + jnp.sum(other * other)
    factor = jnp.minimum(1.0, math.sqrt(count) / (jnp.sqrt(jnp.full((8, LANES), total)) + 1e-06))[:1]
    zero = jnp.where(first, mine, other) * factor
    one = jnp.where(first, other, mine) * factor

    def chunk(half, place):
        return half[place * C : (place + 1) * C]

    for place in range(6):
        up_ref[:, place * LANES : (place + 1) * LANES] = chunk(zero, place)
    down_ref[:, :LANES] = one[: 4 * C]
    down_ref[: 2 * C, LANES:] = one[4 * C : 6 * C, : C - LANES]
    down_ref[2 * C :, LANES:] = one[4 * C : 6 * C, C - LANES :]
    last = C - LANES
    left, right = chunk(one, 7), chunk(one, 8)
    qkv_ref[:, :C] = jnp.concatenate([chunk(zero, 6), left[:, :last]], axis=1)
    qkv_ref[:, C : 2 * C] = jnp.concatenate([chunk(zero, 7), left[:, last:]], axis=1)
    qkv_ref[:, 2 * C :] = jnp.concatenate([chunk(zero, 8), right[:, :last]], axis=1)
    proj_ref[...] = jnp.concatenate([chunk(one, 6), right[:, last:]], axis=1)
    for level in range(2):
        rows = gbias_ref[level * HEADS : (level + 1) * HEADS].reshape(HEADS * 16, WIDE)
        table = dot(rows, back_ref[level]) * factor[:, :1]
        for head in range(HEADS):
            bias_ref[head, level * WA : (level + 1) * WA, :] = table[head * 16 : head * 16 + WA]


def call(kernel, outs, scalars, arrays, scratch=()):
    spaces = [pl.BlockSpec(memory_space=pltpu.SMEM)] * scalars
    spaces += [pl.BlockSpec(memory_space=pltpu.VMEM)] * arrays
    return pl.pallas_call(
        kernel,
        out_shape=outs,
        in_specs=spaces,
        out_specs=[pl.BlockSpec(memory_space=pltpu.VMEM)] * len(outs),
        scratch_shapes=scratch,
        compiler_params=pltpu.CompilerParams(vmem_limit_bytes=VMEM),
    )


def shape(*sizes, kind=F32):
    return jax.ShapeDtypeStruct(sizes, kind)


def from_next(block, axes, distance):
    sizes = [lax.axis_size(axis) for axis in axes]
    route = []
    for place in np.ndindex(*sizes):
        source = [(i + distance) % size for i, size in zip(place, sizes)]
        route.append((int(np.ravel_multi_index(source, sizes)), int(np.ravel_multi_index(place, sizes))))
    return lax.ppermute(block, tuple(axes), route)


def rolled_windows(pair):
    own, beside = pair[:, :, HALF:, HALF:], pair[:, :, HALF:, :HALF]
    below, corner = pair[:, :, :HALF, HALF:], pair[:, :, :HALF, :HALF]
    below = from_next(below, ["lat"], 1)
    beside = from_next(beside, ["lon"], 1)
    corner = from_next(corner, ["lat", "lon"], 1)
    upper = jnp.concatenate([own, beside], axis=3)
    lower = jnp.concatenate([below, corner], axis=3)
    whole = jnp.concatenate([upper, lower], axis=2)[:, ::-1]
    whole = whole.reshape(2, 2, WA, 2, WO, C).transpose(0, 3, 1, 4, 2, 5)
    return whole.reshape(2, TOKENS, C)


def rolled_back(pair):
    whole = pair.reshape(2, 2, 2, WO, WA, C).transpose(0, 2, 4, 1, 3, 5)
    whole = whole.reshape(2, 2, WA, 2 * WO, C)[:, ::-1]
    cut = 2 * WO - HALF
    own, beside = whole[:, :, :HALF, :cut], whole[:, :, :HALF, cut:]
    above, corner = whole[:, :, HALF:, :cut], whole[:, :, HALF:, cut:]
    above = from_next(above, ["lat"], -1)
    beside = from_next(beside, ["lon"], -1)
    corner = from_next(corner, ["lat", "lon"], -1)
    upper = jnp.concatenate([corner, above], axis=3)
    lower = jnp.concatenate([beside, own], axis=3)
    return jnp.concatenate([upper, lower], axis=2)


def weight_sums(mine, other):
    lat, lon = lax.axis_size("lat"), lax.axis_size("lon")
    half, depth = lat // 2, lon // 2
    pairs = [(i, i ^ 1) for i in range(lat)]
    planes = [
        [(2 * i + core) * lon + 2 * z + low for i in range(half) for low in range(2)]
        for core in range(2)
        for z in range(depth)
    ]
    columns = [[2 * z + low for z in range(depth)] for low in range(2)]
    mine = mine + lax.ppermute(other, "lat", pairs).astype(F32)
    mine = mine.astype(BF).reshape(lat, PACKED // lat, LANES)
    got = lax.all_to_all(mine, ("lat", "lon"), 0, 0, axis_index_groups=planes)
    part = jnp.sum(got.astype(F32), axis=0).astype(BF)
    got = lax.all_to_all(jnp.broadcast_to(part, (depth,) + part.shape), "lon", 0, 0, axis_index_groups=columns)
    part = jnp.sum(got.astype(F32), axis=0).astype(BF)
    part = jnp.broadcast_to(part, (lat,) + part.shape)
    mine = lax.all_to_all(part, ("lat", "lon"), 0, 0, axis_index_groups=planes)
    other = lax.ppermute(mine, "lat", pairs)
    return mine.reshape(PACKED, LANES), other.reshape(PACKED, LANES)


def bias_sums(table):
    lon = lax.axis_size("lon")
    parts = table.reshape(lon, table.shape[0] // lon, *table.shape[1:])
    got = lax.all_to_all(parts, "lon", 0, 0)
    part = jnp.sum(got.astype(F32), axis=0).astype(BF)
    got = lax.all_to_all(jnp.broadcast_to(part, (lon,) + part.shape), "lon", 0, 0)
    return got.reshape(table.shape)


def on_device(tokens, w_qkv, w_proj, w_up, w_down, earth_bias, cotangent):
    band = lax.axis_index("lat")
    bands = lax.axis_size("lat")
    core = (band % 2).astype(jnp.int32).reshape(1)
    last = (band == bands - 1).astype(jnp.int32).reshape(1)

    windows = rolled_windows(jnp.stack([tokens, cotangent]))
    table = earth_bias.reshape(HEADS, 2, WA, 2, CUT)
    table = jnp.stack([table[:, 0, :, 0], table[:, 1, :, 1]])
    table = jnp.broadcast_to(table[:, :, None], (2, HEADS, 2, WA, CUT)).reshape(-1, CUT)
    order = jnp.asarray(table_order(), BF)
    bias = call(bias_kernel, [shape(2, HEADS * WIN, WIN)], 1, 2)(last, table, order)[0]

    def tokens_of(width, kind=BF):
        return pltpu.VMEM((TOKENS, width), kind)

    outs = [
        shape(TOKENS, C, kind=BF),
        shape(TOKENS, C, kind=BF),
        shape(PACKED, LANES),
        shape(PACKED, LANES, kind=BF),
        shape(16, 16, WIDE, kind=BF),
    ]
    scratch = [tokens_of(C)] * 4 + [pltpu.VMEM((PARTS, HEADS * WIN, WIN), BF), tokens_of(C), tokens_of(C, F32)]
    scratch += [tokens_of(C), tokens_of(HID, F32)] + [tokens_of(HID)] * 3 + [tokens_of(C, F32)]
    scratch += [tokens_of(C)] * 5 + [pltpu.VMEM((2, HEADS * WIN, WIDE), F32)]
    result, grad_tokens, mine, other, grad_table = call(block_kernel, outs, 1, 9, scratch)(
        core, windows[0], windows[1], w_qkv[:, :C], w_qkv[:, C : 2 * C], w_qkv[:, 2 * C :], w_proj, w_up, w_down, bias
    )
    mine, other = weight_sums(mine, other)
    grad_table = bias_sums(grad_table)
    back = rolled_back(jnp.stack([result, grad_tokens]))

    count = w_qkv.size + w_proj.size + w_up.size + w_down.size + earth_bias.size * bands
    outs = [shape(C, 3 * C), shape(C, C), shape(C, HID), shape(HID, C), shape(HEADS, 2 * WA, 2 * CUT)]
    grads = call(functools.partial(final_kernel, count), outs, 1, 4)(
        core, mine, other, grad_table, jnp.asarray(table_back(), BF)
    )
    return (back[0], back[1], *grads[:4], grads[4][None, None])


def solution(mesh):
    placed = (
        P(None, "lat", "lon", None),
        P(),
        P(),
        P(),
        P(),
        P("lat", None, None, None, None),
        P(None, "lat", "lon", None),
    )
    return jax.shard_map(
        on_device,
        mesh=mesh,
        in_specs=placed,
        out_specs=(
            P(None, "lat", "lon", None),
            P(None, "lat", "lon", None),
            P(),
            P(),
            P(),
            P(),
            P("lat", None, None, None, None),
        ),
        check_vma=False,
    )
```

time: 573 us -> 133 us (0.23)
  the two profiles are of different devices: /device:TPU:2 before, /device:TPU:1 now
where the time goes in v1:
time: 133 us; the launch traced here: 131 us
  starting transfers between devices  36.7 us (28%)
  blocking collectives  28.7 us (22%)
  Pallas kernels  26.7 us (20%)
  local copies, waits for them, and re-layouts  17.3 us (13%)
  waiting for transfers between devices  13.8 us (10%)
  other arithmetic  7.21 us (5%)
    pallas_call x1, Pallas kernels, on_device(): call(block_kernel, outs, 1, 9, scratch)  23.4 us
    ppermute x6, starting transfers between devices, from_next(): return lax.ppermute(block, tuple(axes), route)  19.2 us
    all_to_all x1, blocking collectives, weight_sums(): got = lax.all_to_all(mine, ('lat', 'lon'), 0, 0, axis_index_groups=planes)  16.9 us
    all_to_all x1, blocking collectives, weight_sums(): lax.all_to_all(jnp.broadcast_to(part, (depth,) + part.shape), 'lon', 0, 0...  11.7 us
    all_to_all x1, waiting for transfers between devices, bias_sums(): got = lax.all_to_all(parts, 'lon', 0, 0)  7.81 us
    all_to_all x1, starting transfers between devices, bias_sums(): lax.all_to_all(jnp.broadcast_to(part, (lon,) + part.shape), 'lon', 0, 0)  4.97 us
    all_to_all x1, waiting for transfers between devices, bias_sums(): lax.all_to_all(jnp.broadcast_to(part, (lon,) + part.shape), 'lon', 0, 0)  4.5 us
    all_to_all x1, starting transfers between devices, bias_sums(): got = lax.all_to_all(parts, 'lon', 0, 0)  3.74 us
  transfers between devices with their start and end apart: 11, of which 3 were waited for; matrix products, arithmetic and copies ran while one was open for 9% of the time, Pallas kernels for 1%

profile of v1, /device:TPU:1, one launch (start us, length us, event | category | flops | bytes accessed | tf_op | source)
XLA Modules:
  0.0 131.3 jit_solution(5065952340641523373)
XLA Ops:
  0.6 1.6 %fusion.2 = (bf16[2,2,6,6,192]{4,3,2,1,0:T(8,128)(2,1)}, bf16[2,2,6,6,192]{4,3,2,1,0:T(8,128)(2,1)S(1)}) fusion(bf16[1,2,12,24,192]{4,3,2,1,0:T(8,128)(2,1)} %bitcast.37, bf16[1,2,12,24,192]{4,3,2,1,0:T(8,128)(2,1)} %bitcast.39), kind=kLoop, calls=%fused_computation.17 | loop fusion | flops 221184 | bytes 552960 | tf_op jit(solution)/shard_map/stack | solution.py:383
  2.2 7.4 %collective-permute-start = (bf16[2,2,6,6,192]{4,3,2,1,0:T(8,128)(2,1)}, bf16[2,2,6,6,192]{4,3,2,1,0:T(8,128)(2,1)}, u32[]{:S(2)}, u32[]{:S(2)}) collective-permute-start(bf16[2,2,6,6,192]{4,3,2,1,0:T(8,128)(2,1)} %get-tuple-element.65), channel_id=1, source_target_pairs={{1,0},{2,1},{3,2},{4,3},{5,4},{6,5},{7,6},{8,7},{9,8},{10,9},{11,1... | collective-permute-start | bytes 165896 | tf_op jit(solution)/shard_map/ppermute | solution.py:316
  9.7 1.0 collective-permute-start.2
  10.7 2.0 %fusion.1 = (bf16[2,2,6,18,192]{4,3,2,1,0:T(8,128)(2,1)S(1)}, bf16[2,2,6,18,192]{4,3,2,1,0:T(8,128)(2,1)}) fusion(bf16[1,2,12,24,192]{4,3,2,1,0:T(8,128)(2,1)} %bitcast.38, bf16[1,2,12,24,192]{4,3,2,1,0:T(8,128)(2,1)} %bitcast.40), kind=kLoop, calls=%fused_computation.11 | loop fusion | flops 165888 | bytes 774144 | tf_op jit(solution)/shard_map/stack | solution.py:383
  12.7 3.5 %collective-permute-start.1 = (bf16[2,2,6,18,192]{4,3,2,1,0:T(8,128)(2,1)}, bf16[2,2,6,18,192]{4,3,2,1,0:T(8,128)(2,1)}, u32[]{:S(2)}, u32[]{:S(2)}) collective-permute-start(bf16[2,2,6,18,192]{4,3,2,1,0:T(8,128)(2,1)} %get-tuple-element.64), channel_id=1, source_target_pairs={{16,0},{32,16},{48,32},{64,48},{80,64},{96,80},{112,96},{128,112},... | collective-permute-start | bytes 497672 | tf_op jit(solution)/shard_map/ppermute | solution.py:316
  17.4 0.8 copy-done.6
  18.2 1.2 shard_map.144.bias_ref
  19.4 2.0 %maximum_maximum_fusion = bf16[2,2,12,24,192]{4,3,2,1,0:T(8,128)(2,1)} fusion(bf16[2,2,6,6,192]{4,3,2,1,0:T(8,128)(2,1)} %collective-permute-done.2, bf16[2,2,6,18,192]{4,3,2,1,0:T(8,128)(2,1)} %collective-permute-done.1, bf16[2,2,6,6,192]{4,3,2,1,0:T(8,128)(2,1)} %collective-permute-done, bf16[2,2,6,18,192]{4,3,2,1,0:T(8,128)(2,1)S(1)} %get-tuple-element.63), kind=kLoop, calls=%fused_computation.8 | loop fusion | flops 1769472 | bytes 884736 | tf_op jit(solution)/shard_map/concatenate | solution.py:327
  21.5 1.1 rev.4
  23.2 1.1 fusion.5
  24.6 1.8 %copy.44 = bf16[1,2,2,12,12,192]{5,4,3,2,1,0:T(8,128)(2,1)} copy(bf16[1,2,2,12,12,192]{5,2,3,1,4,0:T(2,128)(2,1)} %get-tuple-element.62) | data formatting | bytes 442368 | tf_op jit(solution)/shard_map/slice | solution.py:404
  26.4 1.1 squeeze.12.x_ref
  27.5 23.4 %shard_map.145 = (bf16[576,192]{1,0:T(8,128)(2,1)S(1)}, bf16[576,192]{1,0:T(8,128)(2,1)S(1)}, f32[1792,128]{1,0:T(8,128)S(1)}, bf16[1792,128]{1,0:T(8,128)(2,1)S(1)}, bf16[16,16,384]{2,1,0:T(8,128)(2,1)}) custom-call(s32[1]{0:T(128)} %bitcast.core_ref, bf16[576,192]{1,0:T(8,128)(2,1)S(1)} %squeeze.12.x_ref, bf16[576,192]{1,0:T(8,128)(2,1)S(1)} %squeeze.13.cot_ref, ...), custom_call_target="tpu_custom_call" | custom-call | tf_op jit(solution)/shard_map/pallas_call | solution.py:403
  51.0 3.3 %collective-permute-start.6 = (bf16[1792,128]{1,0:T(8,128)(2,1)S(1)}, bf16[1792,128]{1,0:T(8,128)(2,1)S(1)}, u32[]{:S(2)}, u32[]{:S(2)}) collective-permute-start(bf16[1792,128]{1,0:T(8,128)(2,1)S(1)} %get-tuple-element.20), channel_id=1, source_target_pairs={{0,16},{16,0},{32,48},{48,32},{64,80},{80,64},{96,112},{112,96},{1... | collective-permute-start | bytes 1376264 | tf_op jit(solution)/shard_map/ppermute | solution.py:356
  54.3 1.4 %collective-permute-done.6 = bf16[1792,128]{1,0:T(8,128)(2,1)S(1)} collective-permute-done((bf16[1792,128]{1,0:T(8,128)(2,1)S(1)}, bf16[1792,128]{1,0:T(8,128)(2,1)S(1)}, u32[]{:S(2)}, u32[]{:S(2)}) %collective-permute-start.6) | collective-permute-done | bytes 458784 | tf_op jit(solution)/shard_map/ppermute | solution.py:356
  55.9 16.9 %all_to_all.25 = bf16[16,112,128]{2,1,0:T(8,128)(2,1)S(1)} all-to-all(bf16[16,112,128]{2,1,0:T(8,128)(2,1)S(1)} %bitcast.36), channel_id=1, replica_groups={{0,1,32,33,64,65,96,97,128,129,160,161,192,193,224,225},{2,3,34,35,66,6..., dimensions={0} | all-to-all | bytes 917504 | tf_op jit(solution)/shard_map/all_to_all | solution.py:358
  72.9 11.7 %all_to_all.26 = bf16[8,112,128]{2,1,0:T(8,128)(2,1)S(1)} all-to-all(bf16[8,112,128]{2,1,0:T(8,128)(2,1)S(1)} %broadcast_in_dim.19), channel_id=1, replica_groups={{0,2,4,6,8,10,12,14},{1,3,5,7,9,11,13,15},{16,18,20,22,24,26,28,30},{17..., dimensions={0} | all-to-all | bytes 458752 | tf_op jit(solution)/shard_map/all_to_all | solution.py:360
  84.7 3.7 %all-to-all-start.3 = ((bf16[16,1,16,384]{3,2,1,0:T(8,128)(2,1)}), bf16[16,1,16,384]{3,2,1,0:T(8,128)(2,1)S(1)}, u32[]{:S(2)}, u32[]{:S(2)}) async-start(bf16[16,1,16,384]{3,2,1,0:T(8,128)(2,1)} %bitcast.17), calls=%async_computation.3 | async-start | bytes 393216 | tf_op jit(solution)/shard_map/all_to_all | solution.py:371
  89.4 7.8 %all-to-all-done.3 = bf16[16,1,16,384]{3,2,1,0:T(8,128)(2,1)S(1)} async-done(((bf16[16,1,16,384]{3,2,1,0:T(8,128)(2,1)}), bf16[16,1,16,384]{3,2,1,0:T(8,128)(2,1)S(1)}, u32[]{:S(2)}, u32[]{:S(2)}) %all-to-all-start.3) | async-done | bytes 196640 | tf_op jit(solution)/shard_map/all_to_all | solution.py:371
  97.3 0.8 broadcast_in_dim.20
  98.1 3.6 %all-to-all-start.2 = ((bf16[16,112,128]{2,1,0:T(8,128)(2,1)}), bf16[16,112,128]{2,1,0:T(8,128)(2,1)S(1)}, u32[]{:S(2)}, u32[]{:S(2)}) async-start(bf16[16,112,128]{2,1,0:T(8,128)(2,1)} %broadcast_in_dim.20), calls=%async_computation.2 | async-start | bytes 917504 | tf_op jit(solution)/shard_map/all_to_all | solution.py:363
  102.0 1.5 %slice.79 = bf16[2,2,6,18,192]{4,1,3,2,0:T(2,128)(2,1)S(1)} reverse(bf16[2,2,6,18,192]{4,1,3,2,0:T(2,128)(2,1)S(1)} %get-tuple-element.59), dimensions={1} | reverse | bytes 331776 | tf_op jit(solution)/shard_map/slice | solution.py:337
  103.5 6.1 %collective-permute-start.4 = (bf16[2,2,6,18,192]{4,1,3,2,0:T(2,128)(2,1)S(1)}, bf16[2,2,6,18,192]{4,1,3,2,0:T(2,128)(2,1)S(1)}, u32[]{:S(2)}, u32[]{:S(2)}) collective-permute-start(bf16[2,2,6,18,192]{4,1,3,2,0:T(2,128)(2,1)S(1)} %slice.79), channel_id=1, source_target_pairs={{240,0},{0,16},{16,32},{32,48},{48,64},{64,80},{80,96},{96,112},{1... | collective-permute-start | bytes 497672 | tf_op jit(solution)/shard_map/ppermute | solution.py:316
  110.6 1.3 collective-permute-start.5
  111.8 1.5 %slice.83 = bf16[2,2,6,18,192]{4,1,3,2,0:T(2,128)(2,1)S(1)} reverse(bf16[2,2,6,18,192]{4,1,3,2,0:T(2,128)(2,1)S(1)} %get-tuple-element.60), dimensions={1} | reverse | bytes 331776 | tf_op jit(solution)/shard_map/slice | solution.py:336
  114.1 5.0 %all-to-all-start.4 = ((bf16[16,1,16,384]{3,2,1,0:T(8,128)(2,1)}), bf16[16,1,16,384]{3,2,1,0:T(8,128)(2,1)S(1)}, u32[]{:S(2)}, u32[]{:S(2)}) async-start(bf16[16,1,16,384]{3,2,1,0:T(8,128)(2,1)} %broadcast_in_dim.21), calls=%async_computation.4 | async-start | bytes 393216 | tf_op jit(solution)/shard_map/all_to_all | solution.py:373
  119.1 1.8 %collective-permute-start.7 = (bf16[16,112,128]{2,1,0:T(8,128)(2,1)S(1)}, bf16[16,112,128]{2,1,0:T(8,128)(2,1)S(1)}, u32[]{:S(2)}, u32[]{:S(2)}) collective-permute-start(bf16[16,112,128]{2,1,0:T(8,128)(2,1)S(1)} %all-to-all-done.2), channel_id=1, source_target_pairs={{0,16},{16,0},{32,48},{48,32},{64,80},{80,64},{96,112},{112,96},{1... | collective-permute-start | bytes 1376264 | tf_op jit(solution)/shard_map/ppermute | solution.py:364
  120.9 0.9 maximum_maximum_fusion.1
  122.2 0.7 copy.52
  123.7 4.5 %all-to-all-done.4 = bf16[16,1,16,384]{3,2,1,0:T(8,128)(2,1)S(1)} async-done(((bf16[16,1,16,384]{3,2,1,0:T(8,128)(2,1)}), bf16[16,1,16,384]{3,2,1,0:T(8,128)(2,1)S(1)}, u32[]{:S(2)}, u32[]{:S(2)}) %all-to-all-start.4) | async-done | bytes 196640 | tf_op jit(solution)/shard_map/all_to_all | solution.py:373
  128.2 2.0 %shard_map.146 = (f32[192,576]{1,0:T(8,128)}, f32[192,192]{1,0:T(8,128)}, f32[192,768]{1,0:T(8,128)}, f32[768,192]{1,0:T(8,128)S(1)}, f32[6,24,552]{2,1,0:T(8,128)}) custom-call(s32[1]{0:T(128)} %bitcast.core_ref, bf16[1792,128]{1,0:T(8,128)(2,1)S(1)} %bitcast.30, bf16[1792,128]{1,0:T(8,128)(2,1)S(1)} %bitcast.32, bf16[16,16,384]{2,1,0:T(8,128)(2,1)S(1)} %bitcast.31, ...), custom_call_target="tpu_custom_call" | custom-call | tf_op jit(solution)/shard_map/pallas_call | solution.py:412
  130.3 1.1 copy.53
  (57 shorter events, 6.4 us)
Async XLA Ops:
  0.6 15.6 %copy-start.8 = (f32[1,1,6,24,552]{4,3,2,1,0:T(8,128)S(1)}, f32[1,1,6,24,552]{4,3,2,1,0:T(8,128)}, u32[]{:S(2)}) copy-start(f32[1,1,6,24,552]{4,3,2,1,0:T(8,128)} %param.14) | copy-start | bytes 953860
  2.2 17.1 %collective-permute-start = (bf16[2,2,6,6,192]{4,3,2,1,0:T(8,128)(2,1)}, bf16[2,2,6,6,192]{4,3,2,1,0:T(8,128)(2,1)}, u32[]{:S(2)}, u32[]{:S(2)}) collective-permute-start(bf16[2,2,6,6,192]{4,3,2,1,0:T(8,128)(2,1)} %get-tuple-element.65), channel_id=1, source_target_pairs={{1,0},{2,1},{3,2},{4,3},{5,4},{6,5},{7,6},{8,7},{9,8},{10,9},{11,1... | collective-permute-start | bytes 165896 | tf_op jit(solution)/shard_map/ppermute | solution.py:316
  9.7 7.1 %copy-start.9 = (bf16[192,576]{1,0:T(8,128)(2,1)S(1)}, bf16[192,576]{1,0:T(8,128)(2,1)}, u32[]{:S(2)}) copy-start(bf16[192,576]{1,0:T(8,128)(2,1)} %param.10) | copy-start | bytes 663556
  9.7 9.7 %collective-permute-start.2 = (bf16[2,2,6,6,192]{4,3,2,1,0:T(8,128)(2,1)S(1)}, bf16[2,2,6,6,192]{4,3,2,1,0:T(8,128)(2,1)}, u32[]{:S(2)}, u32[]{:S(2)}) collective-permute-start(bf16[2,2,6,6,192]{4,3,2,1,0:T(8,128)(2,1)S(1)} %get-tuple-element.66), channel_id=1, source_target_pairs={{17,0},{18,1},{19,2},{20,3},{21,4},{22,5},{23,6},{24,7},{25,8},{26... | collective-permute-start | bytes 165896 | tf_op jit(solution)/shard_map/ppermute | solution.py:316
  12.7 4.4 %copy-start.10 = (bf16[768,192]{0,1:T(8,128)(2,1)S(1)}, bf16[768,192]{0,1:T(8,128)(2,1)}, u32[]{:S(2)}) copy-start(bf16[768,192]{0,1:T(8,128)(2,1)} %param.13) | copy-start | bytes 884740
  12.7 6.7 %collective-permute-start.1 = (bf16[2,2,6,18,192]{4,3,2,1,0:T(8,128)(2,1)}, bf16[2,2,6,18,192]{4,3,2,1,0:T(8,128)(2,1)}, u32[]{:S(2)}, u32[]{:S(2)}) collective-permute-start(bf16[2,2,6,18,192]{4,3,2,1,0:T(8,128)(2,1)} %get-tuple-element.64), channel_id=1, source_target_pairs={{16,0},{32,16},{48,32},{64,48},{80,64},{96,80},{112,96},{128,112},... | collective-permute-start | bytes 497672 | tf_op jit(solution)/shard_map/ppermute | solution.py:316
  17.3 0.9 copy-start.6
  24.4 3.1 %copy-start.1 = (bf16[192,768]{1,0:T(8,128)(2,1)S(1)}, bf16[192,768]{1,0:T(8,128)(2,1)}, u32[]{:S(2)}) copy-start(bf16[192,768]{1,0:T(8,128)(2,1)} %up_ref.1) | copy-start | bytes 884740
  24.4 3.1 %copy-start.7 = (bf16[192,192]{1,0:T(8,128)(2,1)S(1)}, bf16[192,192]{1,0:T(8,128)(2,1)}, u32[]{:S(2)}) copy-start(bf16[192,192]{1,0:T(8,128)(2,1)} %proj_ref.1) | copy-start | bytes 221188
  51.0 4.9 %copy-start.2 = (bf16[576,192]{1,0:T(8,128)(2,1)}, bf16[576,192]{1,0:T(8,128)(2,1)S(1)}, u32[]{:S(2)}) copy-start(bf16[576,192]{1,0:T(8,128)(2,1)S(1)} %get-tuple-element.18) | copy-start | bytes 663556
  51.0 4.9 %copy-start.4 = (bf16[576,192]{1,0:T(8,128)(2,1)}, bf16[576,192]{1,0:T(8,128)(2,1)S(1)}, u32[]{:S(2)}) copy-start(bf16[576,192]{1,0:T(8,128)(2,1)S(1)} %get-tuple-element.17) | copy-start | bytes 663556
  51.0 4.8 %collective-permute-start.6 = (bf16[1792,128]{1,0:T(8,128)(2,1)S(1)}, bf16[1792,128]{1,0:T(8,128)(2,1)S(1)}, u32[]{:S(2)}, u32[]{:S(2)}) collective-permute-start(bf16[1792,128]{1,0:T(8,128)(2,1)S(1)} %get-tuple-element.20), channel_id=1, source_target_pairs={{0,16},{16,0},{32,48},{48,32},{64,80},{80,64},{96,112},{112,96},{1... | collective-permute-start | bytes 1376264 | tf_op jit(solution)/shard_map/ppermute | solution.py:356
  72.8 15.6 %copy-start.5 = (bf16[576,192]{1,0:T(8,128)(2,1)S(1)}, bf16[576,192]{1,0:T(8,128)(2,1)}, u32[]{:S(2)}) copy-start(bf16[576,192]{1,0:T(8,128)(2,1)} %copy-done.4) | copy-start | bytes 663556
  72.8 15.7 %copy-start.3 = (bf16[576,192]{1,0:T(8,128)(2,1)S(1)}, bf16[576,192]{1,0:T(8,128)(2,1)}, u32[]{:S(2)}) copy-start(bf16[576,192]{1,0:T(8,128)(2,1)} %copy-done.2) | copy-start | bytes 663556
  84.7 12.6 %all-to-all-start.3 = ((bf16[16,1,16,384]{3,2,1,0:T(8,128)(2,1)}), bf16[16,1,16,384]{3,2,1,0:T(8,128)(2,1)S(1)}, u32[]{:S(2)}, u32[]{:S(2)}) async-start(bf16[16,1,16,384]{3,2,1,0:T(8,128)(2,1)} %bitcast.17), calls=%async_computation.3 | async-start | bytes 393216 | tf_op jit(solution)/shard_map/all_to_all | solution.py:371
  98.1 15.3 %all-to-all-start.2 = ((bf16[16,112,128]{2,1,0:T(8,128)(2,1)}), bf16[16,112,128]{2,1,0:T(8,128)(2,1)S(1)}, u32[]{:S(2)}, u32[]{:S(2)}) async-start(bf16[16,112,128]{2,1,0:T(8,128)(2,1)} %broadcast_in_dim.20), calls=%async_computation.2 | async-start | bytes 917504 | tf_op jit(solution)/shard_map/all_to_all | solution.py:363
  103.5 17.4 %collective-permute-start.4 = (bf16[2,2,6,18,192]{4,1,3,2,0:T(2,128)(2,1)S(1)}, bf16[2,2,6,18,192]{4,1,3,2,0:T(2,128)(2,1)S(1)}, u32[]{:S(2)}, u32[]{:S(2)}) collective-permute-start(bf16[2,2,6,18,192]{4,1,3,2,0:T(2,128)(2,1)S(1)} %slice.79), channel_id=1, source_target_pairs={{240,0},{0,16},{16,32},{32,48},{48,64},{64,80},{80,96},{96,112},{1... | collective-permute-start | bytes 497672 | tf_op jit(solution)/shard_map/ppermute | solution.py:316
  110.6 10.3 %collective-permute-start.5 = (bf16[2,2,6,6,192]{4,1,3,2,0:T(2,128)(2,1)S(1)}, bf16[2,2,6,6,192]{4,1,3,2,0:T(2,128)(2,1)S(1)}, u32[]{:S(2)}, u32[]{:S(2)}) collective-permute-start(bf16[2,2,6,6,192]{4,1,3,2,0:T(2,128)(2,1)S(1)} %slice.81), channel_id=1, source_target_pairs={{15,0},{0,1},{1,2},{2,3},{3,4},{4,5},{5,6},{6,7},{7,8},{8,9},{9,10... | collective-permute-start | bytes 165896 | tf_op jit(solution)/shard_map/ppermute | solution.py:316
  111.8 9.0 %collective-permute-start.3 = (bf16[2,2,6,6,192]{4,1,3,2,0:T(2,128)(2,1)S(1)}, bf16[2,2,6,6,192]{4,1,3,2,0:T(2,128)(2,1)S(1)}, u32[]{:S(2)}, u32[]{:S(2)}) collective-permute-start(bf16[2,2,6,6,192]{4,1,3,2,0:T(2,128)(2,1)S(1)} %slice.77), channel_id=1, source_target_pairs={{255,0},{240,1},{241,2},{242,3},{243,4},{244,5},{245,6},{246,7},{2... | collective-permute-start | bytes 165896 | tf_op jit(solution)/shard_map/ppermute | solution.py:316
  114.1 14.1 %all-to-all-start.4 = ((bf16[16,1,16,384]{3,2,1,0:T(8,128)(2,1)}), bf16[16,1,16,384]{3,2,1,0:T(8,128)(2,1)S(1)}, u32[]{:S(2)}, u32[]{:S(2)}) async-start(bf16[16,1,16,384]{3,2,1,0:T(8,128)(2,1)} %broadcast_in_dim.21), calls=%async_computation.4 | async-start | bytes 393216 | tf_op jit(solution)/shard_map/all_to_all | solution.py:373
  119.1 9.1 %collective-permute-start.7 = (bf16[16,112,128]{2,1,0:T(8,128)(2,1)S(1)}, bf16[16,112,128]{2,1,0:T(8,128)(2,1)S(1)}, u32[]{:S(2)}, u32[]{:S(2)}) collective-permute-start(bf16[16,112,128]{2,1,0:T(8,128)(2,1)S(1)} %all-to-all-done.2), channel_id=1, source_target_pairs={{0,16},{16,0},{32,48},{48,32},{64,80},{80,64},{96,112},{112,96},{1... | collective-permute-start | bytes 1376264 | tf_op jit(solution)/shard_map/ppermute | solution.py:364
  121.8 6.4 %copy-start = (bf16[2,384,552]{2,1,0:T(8,128)(2,1)S(1)}, bf16[2,384,552]{2,1,0:T(8,128)(2,1)}, u32[]{:S(2)}) copy-start(bf16[2,384,552]{2,1,0:T(8,128)(2,1)} %constant.30.clone.back_ref) | copy-start | bytes 2543620

commit v2 on v1

v2 whole, which is shorter than its diff:
```python
import functools
import math

import jax
import jax.numpy as jnp
import numpy as np
from jax import lax
from jax.experimental import pallas as pl
from jax.experimental.pallas import tpu as pltpu
from jax.sharding import PartitionSpec as P

WA = 12
WO = 12
HALF = 6
HEADS = 6
HEAD = 32
WIN = WA * WO
SPAN = 2 * WO - 1
CUT = WA * SPAN
WIDE = 384
LANES = 128
C = 192
HID = 768
TOKENS = 576
PARTS = 4
PACKED = 1792
SOURCES = 768
MAIN = HEADS * WA
BIAS_ROWS = 176
LEFT = CUT - 2 * LANES
EPS = 1e-05
SCALE = HEAD ** (-0.5)
VMEM = 48 * 1024 * 1024
BF = jnp.bfloat16
F32 = jnp.float32


def table_order():
    lane = np.arange(CUT)
    order = np.zeros((CUT, WIDE), np.float32)
    order[(lane % WA) * SPAN + SPAN - 1 - lane // WA, lane] = 1.0
    return order


def table_back():
    back = np.zeros((2, WIDE, 2 * CUT), np.float32)
    for level in range(2):
        back[level, :, level * CUT : (level + 1) * CUT] = table_order().T
    return back


def window_order():
    order = np.zeros((TOKENS, SOURCES), np.float32)
    near, far = 2 * HALF * 2 * WO, 2 * HALF * 8
    for window, level, column, row in np.ndindex(2, 2, WO, WA):
        token = ((window * 2 + level) * WO + column) * WA + row
        place, across = (1 - level) * HALF + row % HALF, window * WO + column + HALF
        inside = across < 2 * WO
        at = place * 2 * WO + across if inside else 2 * near + place * 8 + across - 2 * WO
        if row >= HALF:
            at += near if inside else far
        order[token, at] = 1.0
    return order


def dot(a, b):
    return jnp.dot(a, b, preferred_element_type=F32)


def dot_rt(a, b):
    return lax.dot_general(a, b, (((1,), (1,)), ((), ())), preferred_element_type=F32)


def dot_lt(a, b):
    return lax.dot_general(a, b, (((0,), (0,)), ((), ())), preferred_element_type=F32)


def row_mean(values, exact=False):
    ones = jnp.full((C, C), 1.0, BF)
    high = values.astype(BF)
    total = dot(high, ones)
    if not exact:
        total = total + dot((values - high.astype(F32)).astype(BF), ones)
    return total * (1.0 / C)


def normal(values, mean):
    centred = values - mean
    inverse = lax.rsqrt(row_mean(centred * centred) + EPS)
    return centred * inverse, inverse


def normal_back(unit, inverse, grad):
    first = row_mean(grad, exact=True)
    second = row_mean(grad * unit)
    return inverse * (grad - first - unit * second)


def halo_kernel(tokens_ref, cot_ref, below_ref, beside_ref, corner_ref):
    for array, ref in enumerate((tokens_ref, cot_ref)):
        for level in range(2):
            for row in range(HALF):
                below_ref[array, level, row] = ref[level, row]
                beside_ref[array, level, row] = ref[level, row + HALF].astype(F32)[:8].astype(BF)
                corner_ref[array, level, row] = ref[level, row].astype(F32)[:8].astype(BF)


def bias_kernel(last_ref, table_ref, order_ref, bias_ref):
    order = order_ref[...]
    table = table_ref[...]
    high = table.astype(BF)
    rest = table - high.astype(F32)
    middle = rest.astype(BF)
    low = (rest - middle.astype(F32)).astype(BF)
    wide = dot(high, order) + (dot(middle, order) + dot(low, order))
    row = lax.broadcasted_iota(jnp.int32, (2 * WA, WIDE), 0)
    row_i = lax.broadcasted_iota(jnp.int32, (2 * WA, WIN), 0) % WA
    row_j = lax.broadcasted_iota(jnp.int32, (2 * WA, WIN), 1) % WA
    split = (row_i >= HALF) != (row_j >= HALF)
    split = jnp.logical_and(split, last_ref[0] == 1)
    for level in range(2):
        for head in range(HEADS):
            at = (level * HEADS + head) * 2 * WA
            both = wide[at : at + 2 * WA]
            both = jnp.where(row < WA, pltpu.roll(both, WIDE - WA, 1), both)
            blocks = []
            for pair in range(WO // 2):
                turn = (WO - 2 - 2 * pair) * WA
                block = pltpu.roll(both, (WIDE - turn) % WIDE, 1)[:, :WIN]
                blocks.append(jnp.where(split, -1e30, block))
            block = jnp.transpose(jnp.concatenate(blocks, axis=0))
            bias_ref[level, head * WIN : (head + 1) * WIN, :] = block


def block_kernel(
    core_ref, low_ref, tokens_ref, cots_ref, below_ref, beside_ref, corner_ref, order_ref,
    wq_ref, wk_ref, wv_ref, proj_ref, up_ref, down_ref, bias_ref,
    result_ref, gtok_ref, mine_ref, other_ref, bmine_ref, bother_ref,
    source_ref, x_ref, cot_ref, bsum_ref, normed_ref, q_ref, k_ref, v_ref, prob_ref, att_ref, res_ref, two_ref, upper_ref, gact_ref, act_ref,
    gup_ref, gres_ref, gmix_ref, gatt_ref, dq_ref, dk_ref, dv_ref, ds_ref, pad_ref, turned_ref,
    unit_ref, inverse_ref, unit_two_ref, inverse_two_ref, mean_ref,
):
    lane = lax.broadcasted_iota(jnp.int32, (1, C), 1) // HEAD
    half_masks = [(lane == head).astype(F32).astype(BF) for head in range(HEADS)]

    def rows_of(part):
        return pl.ds(pl.multiple_of(part * WIN, WIN), WIN)

    near, far = 2 * HALF * 2 * WO, 2 * HALF * 8
    for array, (ref, target) in enumerate(((tokens_ref, x_ref), (cots_ref, cot_ref))):
        for level in range(2):
            for row in range(HALF):
                place = level * HALF + row
                at = place * 2 * WO
                source_ref[at : at + 2 * WO, :] = ref[level, row + HALF].astype(F32)
                source_ref[near + at : near + at + 2 * WO, :] = below_ref[array, level, row].astype(F32)
                at = 2 * near + place * 8
                source_ref[at : at + 8, :] = beside_ref[array, level, row].astype(F32)
                source_ref[far + at : far + at + 8, :] = corner_ref[array, level, row].astype(F32)
        target[...] = dot(order_ref[...], source_ref[...].astype(BF)).astype(BF)

    def first_norm(part, carry):
        rows = rows_of(part)
        mean = row_mean(x_ref[rows, :], exact=True)
        unit, inverse = normal(x_ref[rows, :].astype(F32), mean)
        mean_ref[rows, :] = mean
        unit_ref[rows, :] = unit
        inverse_ref[rows, :] = inverse
        normed_ref[rows, :] = unit.astype(BF)
        return carry

    lax.fori_loop(0, PARTS, first_norm, 0, unroll=4)
    normed = normed_ref[...]
    q_ref[...] = dot(normed, wq_ref[...]).astype(BF)
    k_ref[...] = dot(normed, wk_ref[...]).astype(BF)
    v_ref[...] = dot(normed, wv_ref[...]).astype(BF)

    def attend(part, carry):
        rows = rows_of(part)
        query, key, value = q_ref[rows, :], k_ref[rows, :], v_ref[rows, :]
        level = part % 2
        value_t = jnp.transpose(value)
        chunks = [slice(head * WIN, (head + 1) * WIN) for head in range(HEADS)]
        scores = [dot_rt(key * mask, query) for mask in half_masks]
        for head, chunk in enumerate(chunks):
            score = scores[head] * SCALE + bias_ref[level, chunk, :]
            exponent = jnp.exp(score - jnp.max(score, axis=0, keepdims=True))
            prob = exponent * (1.0 / jnp.sum(exponent, axis=0, keepdims=True))
            prob_ref[part, chunk, :] = prob.astype(BF)
        for head, chunk in enumerate(chunks):
            own = slice(head * HEAD, (head + 1) * HEAD)
            turned_ref[own, :] = dot(value_t[own], prob_ref[part, chunk, :])
        att_ref[rows, :] = jnp.transpose(turned_ref[...]).astype(BF)
        return carry

    lax.fori_loop(0, PARTS, attend, 0, unroll=4)
    res_ref[...] = dot(att_ref[...], proj_ref[...])

    def second_norm(part, carry):
        rows = rows_of(part)
        mixed = res_ref[rows, :].astype(BF)
        residual = x_ref[rows, :].astype(F32) + mixed.astype(F32)
        res_ref[rows, :] = residual
        unit, inverse = normal(residual, mean_ref[rows, :] + row_mean(mixed, exact=True))
        unit_two_ref[rows, :] = unit
        inverse_two_ref[rows, :] = inverse
        two_ref[rows, :] = unit.astype(BF)
        return carry

    lax.fori_loop(0, PARTS, second_norm, 0, unroll=4)
    upper_ref[...] = dot(two_ref[...], up_ref[...])
    gact_ref[...] = dot(cot_ref[...], down_ref[...]).astype(BF)
    step = 32

    def gelu(chunk, carry):
        rows = pl.ds(pl.multiple_of(chunk * step, step), step)
        upper = upper_ref[rows, :]
        cdf = 0.5 + 0.5 * lax.erf(upper * math.sqrt(0.5))
        pdf = jnp.exp(upper * upper * -0.5) * (1.0 / math.sqrt(2.0 * math.pi))
        act_ref[rows, :] = (upper * cdf).astype(BF)
        gup_ref[rows, :] = (gact_ref[rows, :].astype(F32) * (cdf + upper * pdf)).astype(BF)
        return carry

    lax.fori_loop(0, TOKENS // step, gelu, 0)
    result_ref[...] = (res_ref[...] + dot_rt(act_ref[...], down_ref[...])).astype(BF)
    gres_ref[...] = dot_rt(gup_ref[...], up_ref[...])

    def second_back(part, carry):
        rows = rows_of(part)
        unit, inverse = unit_two_ref[rows, :], inverse_two_ref[rows, :]
        grad = gres_ref[rows, :].astype(BF).astype(F32)
        grad = cot_ref[rows, :].astype(F32) + normal_back(unit, inverse, grad)
        gres_ref[rows, :] = grad
        gmix_ref[rows, :] = grad.astype(BF)
        return carry

    lax.fori_loop(0, PARTS, second_back, 0, unroll=4)
    gatt_ref[...] = dot_rt(gmix_ref[...], proj_ref[...]).astype(BF)
    ds_ref[...] = jnp.zeros(ds_ref.shape, F32)
    pad_ref[...] = jnp.zeros(pad_ref.shape, F32)

    def attend_back(part, carry):
        rows = rows_of(part)
        query, key, value = q_ref[rows, :], k_ref[rows, :], v_ref[rows, :]
        gatt = gatt_ref[rows, :]
        level = part % 2
        key_t = jnp.transpose(key)
        chunks = [slice(head * WIN, (head + 1) * WIN) for head in range(HEADS)]
        gowns = [gatt * mask for mask in half_masks]
        gprobs = [dot_rt(value, gown) for gown in gowns]
        gscores = []
        for head, chunk in enumerate(chunks):
            weight = prob_ref[part, chunk, :].astype(F32)
            gscore = weight * (gprobs[head] - jnp.sum(weight * gprobs[head], axis=0, keepdims=True))
            ds_ref[level, chunk, :] += gscore
            gscores.append(gscore.astype(BF))
        gkey = jnp.zeros((WIN, C), F32)
        gvalue = jnp.zeros((WIN, C), F32)
        for head, chunk in enumerate(chunks):
            own = slice(head * HEAD, (head + 1) * HEAD)
            turned_ref[own, :] = dot(key_t[own], gscores[head])
            gkey = gkey + dot(gscores[head], query * half_masks[head])
            gvalue = gvalue + dot(prob_ref[part, chunk, :], gowns[head])
        dq_ref[rows, :] = (jnp.transpose(turned_ref[...]) * SCALE).astype(BF)
        dk_ref[rows, :] = (gkey * SCALE).astype(BF)
        dv_ref[rows, :] = gvalue.astype(BF)
        return carry

    lax.fori_loop(0, PARTS, attend_back, 0, unroll=4)
    normed_grad = dot_rt(dq_ref[...], wq_ref[...])
    normed_grad = normed_grad + dot_rt(dk_ref[...], wk_ref[...])
    res_ref[...] = normed_grad + dot_rt(dv_ref[...], wv_ref[...])

    def first_back(part, carry):
        rows = rows_of(part)
        unit, inverse = unit_ref[rows, :], inverse_ref[rows, :]
        grad = res_ref[rows, :].astype(BF).astype(F32)
        gtok_ref[rows, :] = (gres_ref[rows, :] + normal_back(unit, inverse, grad)).astype(BF)
        return carry

    lax.fori_loop(0, PARTS, first_back, 0, unroll=4)
    first = core_ref[0] == 0

    def put(start, zero, one):
        rows = slice(start, start + zero.shape[0])
        mine_ref[rows, :] = jnp.where(first, zero, one)
        other_ref[rows, :] = jnp.where(first, one, zero).astype(BF)

    gup = dot_lt(two_ref[...], gup_ref[...])
    gdown = dot_lt(cot_ref[...], act_ref[...])
    for chunk in range(6):
        columns = slice(chunk * LANES, (chunk + 1) * LANES)
        put(chunk * C, gup[:, columns], gdown[:, columns])
    normed = normed_ref[...]
    gq = dot_lt(normed, dq_ref[...])
    gk = dot_lt(normed, dk_ref[...])
    gv = dot_lt(normed, dv_ref[...])
    gproj = dot_lt(att_ref[...], gmix_ref[...])
    put(6 * C, gq[:, :LANES], gproj[:, :LANES])
    put(7 * C, gk[:, :LANES], jnp.concatenate([gq[:, LANES:], gk[:, LANES:]], axis=1))
    put(8 * C, gv[:, :LANES], jnp.concatenate([gv[:, LANES:], gproj[:, LANES:]], axis=1))
    mine_ref[9 * C :, :] = jnp.zeros((PACKED - 9 * C, LANES), F32)
    other_ref[9 * C :, :] = jnp.zeros((PACKED - 9 * C, LANES), BF)

    row = lax.broadcasted_iota(jnp.int32, (2 * WA, WIDE), 0)

    def table_grad(level, head):
        place = level * HEADS + head
        pad_ref[place, :, :WIN] = jnp.transpose(ds_ref[level, head * WIN : (head + 1) * WIN, :])
        total = jnp.zeros((2 * WA, WIDE), F32)
        for pair in range(WO // 2):
            turn = (WO - 2 - 2 * pair) * WA
            block = pad_ref[place, pair * 2 * WA : (pair + 1) * 2 * WA, :]
            total = total + (pltpu.roll(block, turn, 1) if turn else block)
        total = jnp.where(row < WA, pltpu.roll(total, WA, 1), total)
        return total + pltpu.roll(total, WA, 0)

    for level in range(2):
        left = jnp.zeros((2 * WA, LANES), F32)
        for pair in range(HEADS // 2):
            both = jnp.where(row < WA, table_grad(level, 2 * pair), table_grad(level, 2 * pair + 1))
            start = pair * 2 * WA
            bsum_ref[level, start : start + 2 * WA, :] = both[:, :LANES]
            bsum_ref[level, MAIN + start : MAIN + start + 2 * WA, :] = both[:, LANES : 2 * LANES]
            rest = both[:, 2 * LANES :]
            left = left + (pltpu.roll(rest, pair * LEFT, 1) if pair else rest)
        bsum_ref[level, 2 * MAIN : 2 * MAIN + 2 * WA, :] = left
        bsum_ref[level, 2 * MAIN + 2 * WA :, :] = jnp.zeros((BIAS_ROWS - 2 * MAIN - 2 * WA, LANES), F32)
    lower = low_ref[0] == 0
    zero, one = bsum_ref[0], bsum_ref[1]
    bmine_ref[...] = jnp.where(lower, zero, one)
    bother_ref[...] = jnp.where(lower, one, zero).astype(BF)


def final_kernel(
    count, core_ref, low_ref, mine_ref, other_ref, bmine_ref, bother_ref, back_ref,
    qkv_ref, proj_ref, up_ref, down_ref, bias_ref,
):
    first = core_ref[0] == 0
    mine = mine_ref[...].astype(F32)
    other = other_ref[...].astype(F32)
    total = jnp.sum(mine * mine) + jnp.sum(other * other)
    factor = jnp.minimum(1.0, math.sqrt(count) / (jnp.sqrt(jnp.full((8, LANES), total)) + 1e-06))[:1]
    zero = jnp.where(first, mine, other) * factor
    one = jnp.where(first, other, mine) * factor

    def chunk(half, place):
        return half[place * C : (place + 1) * C]

    for place in range(6):
        up_ref[:, place * LANES : (place + 1) * LANES] = chunk(zero, place)
        down_ref[:, place * LANES : (place + 1) * LANES] = chunk(one, place)
    last = C - LANES
    left, right = chunk(one, 7), chunk(one, 8)
    qkv_ref[:, :C] = jnp.concatenate([chunk(zero, 6), left[:, :last]], axis=1)
    qkv_ref[:, C : 2 * C] = jnp.concatenate([chunk(zero, 7), left[:, last:]], axis=1)
    qkv_ref[:, 2 * C :] = jnp.concatenate([chunk(zero, 8), right[:, :last]], axis=1)
    proj_ref[...] = jnp.concatenate([chunk(one, 6), right[:, last:]], axis=1)

    lower = low_ref[0] == 0
    bmine = bmine_ref[...].astype(F32)
    bother = bother_ref[...].astype(F32)
    tables = []
    for level, packed in enumerate((jnp.where(lower, bmine, bother), jnp.where(lower, bother, bmine))):
        left = packed[2 * MAIN : 2 * MAIN + 2 * WA]
        left = [left] + [pltpu.roll(left, LANES - pair * LEFT, 1) for pair in range(1, HEADS // 2)]
        rows = [packed[:MAIN], packed[MAIN : 2 * MAIN], jnp.concatenate(left, axis=0)]
        rows = jnp.concatenate(rows, axis=1).astype(BF)
        tables.append(dot(rows, back_ref[level]) * factor[:, :1])
    row = lax.broadcasted_iota(jnp.int32, (2 * WA, 2 * CUT), 0)
    for pair in range(HEADS // 2):
        upper, lower = [table[pair * 2 * WA : (pair + 1) * 2 * WA] for table in tables]
        bias_ref[0, 0, 2 * pair] = jnp.where(row < WA, upper, pltpu.roll(lower, WA, 0))
        bias_ref[0, 0, 2 * pair + 1] = jnp.where(row < WA, pltpu.roll(upper, WA, 0), lower)


def call(kernel, outs, scalars, arrays, scratch=()):
    spaces = [pl.BlockSpec(memory_space=pltpu.SMEM)] * scalars
    spaces += [pl.BlockSpec(memory_space=pltpu.VMEM)] * arrays
    return pl.pallas_call(
        kernel,
        out_shape=outs,
        in_specs=spaces,
        out_specs=[pl.BlockSpec(memory_space=pltpu.VMEM)] * len(outs),
        scratch_shapes=scratch,
        compiler_params=pltpu.CompilerParams(vmem_limit_bytes=VMEM),
    )


def shape(*sizes, kind=F32):
    return jax.ShapeDtypeStruct(sizes, kind)


def from_next(block, axes, distance):
    sizes = [lax.axis_size(axis) for axis in axes]
    route = []
    for place in np.ndindex(*sizes):
        source = [(i + distance) % size for i, size in zip(place, sizes)]
        route.append((int(np.ravel_multi_index(source, sizes)), int(np.ravel_multi_index(place, sizes))))
    return lax.ppermute(block, tuple(axes), route)


def rolled_back(pair):
    whole = pair.reshape(2, 2, 2, WO, WA, C).transpose(0, 2, 4, 1, 3, 5)
    whole = whole.reshape(2, 2, WA, 2 * WO, C)[:, ::-1]
    cut = 2 * WO - HALF
    own, beside = whole[:, :, :HALF, :cut], whole[:, :, :HALF, cut:]
    above, corner = whole[:, :, HALF:, :cut], whole[:, :, HALF:, cut:]
    above = from_next(above, ["lat"], -1)
    beside = from_next(beside, ["lon"], -1)
    corner = from_next(corner, ["lat", "lon"], -1)
    upper = jnp.concatenate([corner, above], axis=3)
    lower = jnp.concatenate([beside, own], axis=3)
    return jnp.concatenate([upper, lower], axis=2)


def gradient_sums(mine, other, bmine, bother):
    lat, lon = lax.axis_size("lat"), lax.axis_size("lon")
    half, depth = lat // 2, lon // 2
    pairs = [(i, i ^ 1) for i in range(lat)]
    beside = [(i, i ^ 1) for i in range(lon)]
    planes = [
        [(2 * i + core) * lon + 2 * z + low for i in range(half) for low in range(2)]
        for core in range(2)
        for z in range(depth)
    ]
    columns = [[2 * z + low for z in range(depth)] for low in range(2)]
    mine = mine + lax.ppermute(other, "lat", pairs).astype(F32)
    bmine = (bmine + lax.ppermute(bother, "lon", beside).astype(F32)).astype(BF)
    mine = mine.astype(BF).reshape(lat, PACKED // lat, LANES)
    got = lax.all_to_all(mine, ("lat", "lon"), 0, 0, axis_index_groups=planes)
    part = jnp.sum(got.astype(F32), axis=0).astype(BF)
    share = part.shape[0]
    part = jnp.concatenate([part, bmine])
    got = lax.all_to_all(jnp.broadcast_to(part, (depth,) + part.shape), "lon", 0, 0, axis_index_groups=columns)
    part = jnp.sum(got.astype(F32), axis=0).astype(BF)
    part, bmine = part[:share], part[share:]
    bother = lax.ppermute(bmine, "lon", beside)
    part = jnp.broadcast_to(part, (lat,) + part.shape)
    mine = lax.all_to_all(part, ("lat", "lon"), 0, 0, axis_index_groups=planes)
    other = lax.ppermute(mine, "lat", pairs)
    return mine.reshape(PACKED, LANES), other.reshape(PACKED, LANES), bmine, bother


def on_device(tokens, w_qkv, w_proj, w_up, w_down, earth_bias, cotangent):
    band = lax.axis_index("lat")
    bands = lax.axis_size("lat")
    core = (band % 2).astype(jnp.int32).reshape(1)
    low = (lax.axis_index("lon") % 2).astype(jnp.int32).reshape(1)
    last = (band == bands - 1).astype(jnp.int32).reshape(1)

    wide, narrow = shape(2, 2, HALF, 2 * WO, C, kind=BF), shape(2, 2, HALF, 8, C, kind=BF)
    below, beside, corner = call(halo_kernel, [wide, narrow, narrow], 0, 2)(tokens, cotangent)
    below = from_next(below, ["lat"], 1)
    corner = from_next(corner, ["lat", "lon"], 1)
    beside = from_next(beside, ["lon"], 1)
    table = earth_bias.reshape(HEADS, 2, WA, 2, CUT)
    table = jnp.stack([table[:, 0, :, 0], table[:, 1, :, 1]])
    table = jnp.broadcast_to(table[:, :, None], (2, HEADS, 2, WA, CUT)).reshape(-1, CUT)
    order = jnp.asarray(table_order(), BF)
    bias = call(bias_kernel, [shape(2, HEADS * WIN, WIN)], 1, 2)(last, table, order)[0]

    def tokens_of(width, kind=BF):
        return pltpu.VMEM((TOKENS, width), kind)

    outs = [
        shape(TOKENS, C, kind=BF),
        shape(TOKENS, C, kind=BF),
        shape(PACKED, LANES),
        shape(PACKED, LANES, kind=BF),
        shape(BIAS_ROWS, LANES),
        shape(BIAS_ROWS, LANES, kind=BF),
    ]
    scratch = [pltpu.VMEM((SOURCES, C), F32), tokens_of(C), tokens_of(C), pltpu.VMEM((2, BIAS_ROWS, LANES), F32)]
    scratch += [tokens_of(C)] * 4 + [pltpu.VMEM((PARTS, HEADS * WIN, WIN), BF), tokens_of(C), tokens_of(C, F32)]
    scratch += [tokens_of(C), tokens_of(HID, F32)] + [tokens_of(HID)] * 3 + [tokens_of(C, F32)]
    scratch += [tokens_of(C)] * 5 + [pltpu.VMEM((2, HEADS * WIN, WIN), F32)]
    scratch += [pltpu.VMEM((2 * HEADS, WIN, WIDE), F32), pltpu.VMEM((C, WIN), F32)]
    scratch += [tokens_of(C, F32)] * 5
    result, grad_tokens, *grads = call(block_kernel, outs, 2, 13, scratch)(
        core, low, tokens, cotangent, below, beside, corner, jnp.asarray(window_order(), BF),
        w_qkv[:, :C], w_qkv[:, C : 2 * C], w_qkv[:, 2 * C :], w_proj, w_up, w_down.T, bias,
    )
    sums = gradient_sums(*grads)
    back = rolled_back(jnp.stack([result, grad_tokens]))

    count = w_qkv.size + w_proj.size + w_up.size + w_down.size + earth_bias.size * bands
    outs = [shape(C, 3 * C), shape(C, C), shape(C, HID), shape(C, HID), shape(1, 1, HEADS, 2 * WA, 2 * CUT)]
    grads = call(functools.partial(final_kernel, count), outs, 2, 5)(
        core, low, *sums, jnp.asarray(table_back(), BF)
    )
    return (back[0], back[1], *grads[:3], grads[3].T, grads[4])


def solution(mesh):
    placed = (
        P(None, "lat", "lon", None),
        P(),
        P(),
        P(),
        P(),
        P("lat", None, None, None, None),
        P(None, "lat", "lon", None),
    )
    return jax.shard_map(
        on_device,
        mesh=mesh,
        in_specs=placed,
        out_specs=(
            P(None, "lat", "lon", None),
            P(None, "lat", "lon", None),
            P(),
            P(),
            P(),
            P(),
            P("lat", None, None, None, None),
        ),
        check_vma=False,
    )
```

time: 133 us -> 105 us (0.79)
  blocking collectives: 28.7 us -> 0 us
  waiting for transfers between devices: 13.8 us -> 31.7 us
  Pallas kernels: 26.7 us -> 18.9 us
  other arithmetic: 7.21 us -> 2.37 us
  starting transfers between devices: 36.7 us -> 34.3 us
  local copies, waits for them, and re-layouts: 17.3 us -> 15.7 us
    all_to_all x2 -> x0, blocking collectives: 28.7 us -> none  [the longest x1 16.9 us: weight_sums(): got = lax.all_to_all(mine, ('lat', 'lon'), 0, 0, axis_index_groups=planes)]
    all_to_all x3, waiting for transfers between devices: 12.3 us -> 25.1 us  [the longest x1 17.2 us: gradient_sums(): lax.all_to_all(jnp.broadcast_to(part, (depth,) + part.shape), 'lon', 0, 0...]
    pallas_call x2 -> x3, Pallas kernels: 25.5 us -> 16.5 us  [the longest x1 13.6 us: on_device(): call(block_kernel, outs, 2, 13, scratch)]
    another operation x2 -> x0, other arithmetic: 3.62 us -> none  [on_device(): windows = rolled_windows(jnp.stack([tokens, cotangent]))]
    ppermute x2 -> x4, waiting for transfers between devices: 1.45 us -> 4.94 us  [the longest x1 2.78 us: gradient_sums(): bmine = (bmine + lax.ppermute(bother, 'lon', beside).astype(F32)).astype(BF)]
    ppermute x6, starting transfers between devices: 19.2 us -> 15.9 us  [from_next(): return lax.ppermute(block, tuple(axes), route)]
    slice x3 -> x2, local copies, waits for them, and re-layouts: 3.02 us -> 0.01 us  [gradient_sums(): part, bmine = (part[:share], part[share:])]
    concatenate x1, other arithmetic: 2.05 us -> 0.01 us  [gradient_sums(): part = jnp.concatenate([part, bmine])]
  transfers between devices with their start and end apart: 11 -> 13, of which waited for: 3 -> 7; matrix products, arithmetic and copies ran while one was open for 9% -> 12% of each run, Pallas kernels for 1% -> 2%
where the time goes in v2:
time: 105 us; the launch traced here: 104 us
  starting transfers between devices  34.3 us (33%)
  waiting for transfers between devices  31.7 us (30%)
  Pallas kernels  18.9 us (18%)
  local copies, waits for them, and re-layouts  15.7 us (15%)
  other arithmetic  2.37 us (2%)
    all_to_all x1, waiting for transfers between devices, gradient_sums(): lax.all_to_all(jnp.broadcast_to(part, (depth,) + part.shape), 'lon', 0, 0...  17.2 us
    ppermute x6, starting transfers between devices, from_next(): return lax.ppermute(block, tuple(axes), route)  15.9 us
    pallas_call x1, Pallas kernels, on_device(): call(block_kernel, outs, 2, 13, scratch)  13.6 us
    all_to_all x1, waiting for transfers between devices, gradient_sums(): got = lax.all_to_all(mine, ('lat', 'lon'), 0, 0, axis_index_groups=planes)  6.21 us
    all_to_all x1, starting transfers between devices, gradient_sums(): mine = lax.all_to_all(part, ('lat', 'lon'), 0, 0, axis_index_groups=planes)  5.08 us
    unnamed x26, local copies, waits for them, and re-layouts  4.69 us
    all_to_all x1, starting transfers between devices, gradient_sums(): got = lax.all_to_all(mine, ('lat', 'lon'), 0, 0, axis_index_groups=planes)  3.56 us
    all_to_all x1, starting transfers between devices, gradient_sums(): lax.all_to_all(jnp.broadcast_to(part, (depth,) + part.shape), 'lon', 0, 0...  3.54 us
  transfers between devices with their start and end apart: 13, of which 7 were waited for; matrix products, arithmetic and copies ran while one was open for 12% of the time, Pallas kernels for 2%

profile of v2, /device:TPU:1, one launch (start us, length us, event | category | flops | bytes accessed | tf_op | source)
XLA Modules:
  0.0 103.9 jit_solution(16446928202990446436)
XLA Ops:
  0.6 1.0 copy-done.1
  1.6 1.0 copy-done.3
  3.4 7.4 %collective-permute-start.1 = (bf16[2,2,6,8,192]{4,3,2,1,0:T(8,128)(2,1)}, bf16[2,2,6,8,192]{4,3,2,1,0:T(8,128)(2,1)}, u32[]{:S(2)}, u32[]{:S(2)}) collective-permute-start(bf16[2,2,6,8,192]{4,3,2,1,0:T(8,128)(2,1)} %get-tuple-element.22), channel_id=1, source_target_pairs={{1,0},{2,1},{3,2},{4,3},{5,4},{6,5},{7,6},{8,7},{9,8},{10,9},{11,1... | collective-permute-start | bytes 221192 | tf_op jit(solution)/shard_map/ppermute | solution.py:400
  10.8 1.0 collective-permute-start.2
  11.8 3.5 %collective-permute-start = (bf16[2,2,6,24,192]{4,3,2,1,0:T(8,128)(2,1)}, bf16[2,2,6,24,192]{4,3,2,1,0:T(8,128)(2,1)S(1)}, u32[]{:S(2)}, u32[]{:S(2)}) collective-permute-start(bf16[2,2,6,24,192]{4,3,2,1,0:T(8,128)(2,1)} %get-tuple-element.21), channel_id=1, source_target_pairs={{16,0},{32,16},{48,32},{64,48},{80,64},{96,80},{112,96},{128,112},... | collective-permute-start | bytes 663560 | tf_op jit(solution)/shard_map/ppermute | solution.py:400
  15.3 1.3 %reshape.53 = f32[6,2,12,2,276]{4,3,2,1,0:T(2,128)S(1)} reshape(f32[1,1,6,24,552]{4,3,2,1,0:T(8,128)} %param.15) | data formatting | bytes 635904 | tf_op jit(solution)/shard_map/reshape | solution.py:457
  17.2 0.9 broadcast_in_dim.12
  18.1 1.3 %reshape.54.table_ref = f32[288,276]{1,0:T(8,128)S(1)} reshape(f32[2,6,2,12,276]{4,3,2,1,0:T(8,128)} %broadcast_in_dim.12) | data formatting | bytes 635904 | tf_op jit(solution)/shard_map/reshape | solution.py:459
  19.4 2.4 %shard_map.154.bias_ref = f32[2,864,144]{2,1,0:T(8,128)S(1)} custom-call(s32[1]{0:T(128)} %bitcast.3.last_ref, f32[288,276]{1,0:T(8,128)S(1)} %reshape.54.table_ref, bf16[276,384]{1,0:T(8,128)(2,1)S(1)} %copy-done.9), custom_call_target="tpu_custom_call" | custom-call | tf_op jit(solution)/shard_map/pallas_call | solution.py:461
  21.8 1.2 %copy-done = f32[2,864,144]{2,1,0:T(8,128)} copy-done((f32[2,864,144]{2,1,0:T(8,128)}, f32[2,864,144]{2,1,0:T(8,128)S(1)}, u32[]{:S(2)}) %copy-start) | copy-done | bytes 995352
  23.2 13.6 %shard_map.155 = (bf16[576,192]{1,0:T(8,128)(2,1)S(1)}, bf16[576,192]{1,0:T(8,128)(2,1)S(1)}, f32[1792,128]{1,0:T(8,128)S(1)}, bf16[1792,128]{1,0:T(8,128)(2,1)S...) custom-call(s32[1]{0:T(128)} %bitcast.core_ref, s32[1]{0:T(128)} %bitcast.1.low_ref, ...), custom_call_target="tpu_custom_call" | custom-call | tf_op jit(solution)/shard_map/pallas_call | solution.py:480
  36.8 2.1 %collective-permute-start.6 = (bf16[1792,128]{1,0:T(8,128)(2,1)S(1)}, bf16[1792,128]{1,0:T(8,128)(2,1)S(1)}, u32[]{:S(2)}, u32[]{:S(2)}) collective-permute-start(bf16[1792,128]{1,0:T(8,128)(2,1)S(1)} %get-tuple-element.27), channel_id=1, source_target_pairs={{0,16},{16,0},{32,48},{48,32},{64,80},{80,64},{96,112},{112,96},{1... | collective-permute-start | bytes 1376264 | tf_op jit(solution)/shard_map/ppermute | solution.py:428
  38.9 1.4 %collective-permute-done.6 = bf16[1792,128]{1,0:T(8,128)(2,1)S(1)} collective-permute-done((bf16[1792,128]{1,0:T(8,128)(2,1)S(1)}, bf16[1792,128]{1,0:T(8,128)(2,1)S(1)}, u32[]{:S(2)}, u32[]{:S(2)}) %collective-permute-start.6) | collective-permute-done | bytes 458784 | tf_op jit(solution)/shard_map/ppermute | solution.py:428
  40.3 0.9 add_convert_fusion
  41.2 3.6 %all-to-all-start = ((bf16[16,112,128]{2,1,0:T(8,128)(2,1)}), bf16[16,112,128]{2,1,0:T(8,128)(2,1)S(1)}, u32[]{:S(2)}, u32[]{:S(2)}) async-start(bf16[16,112,128]{2,1,0:T(8,128)(2,1)} %bitcast.10), calls=%async_computation | async-start | bytes 917504 | tf_op jit(solution)/shard_map/all_to_all | solution.py:431
  44.8 1.3 %collective-permute-start.7 = (bf16[176,128]{1,0:T(8,128)(2,1)S(1)}, bf16[176,128]{1,0:T(8,128)(2,1)S(1)}, u32[]{:S(2)}, u32[]{:S(2)}) collective-permute-start(bf16[176,128]{1,0:T(8,128)(2,1)S(1)} %get-tuple-element.29), channel_id=1, source_target_pairs={{0,1},{1,0},{2,3},{3,2},{4,5},{5,4},{6,7},{7,6},{8,9},{9,8},{10,11... | collective-permute-start | bytes 135176 | tf_op jit(solution)/shard_map/ppermute | solution.py:429
  46.1 2.8 %collective-permute-done.7 = bf16[176,128]{1,0:T(8,128)(2,1)S(1)} collective-permute-done((bf16[176,128]{1,0:T(8,128)(2,1)S(1)}, bf16[176,128]{1,0:T(8,128)(2,1)S(1)}, u32[]{:S(2)}, u32[]{:S(2)}) %collective-permute-start.7) | collective-permute-done | bytes 45088 | tf_op jit(solution)/shard_map/ppermute | solution.py:429
  48.9 6.2 %all-to-all-done = bf16[16,112,128]{2,1,0:T(8,128)(2,1)S(1)} async-done(((bf16[16,112,128]{2,1,0:T(8,128)(2,1)}), bf16[16,112,128]{2,1,0:T(8,128)(2,1)S(1)}, u32[]{:S(2)}, u32[]{:S(2)}) %all-to-all-start) | async-done | bytes 458784 | tf_op jit(solution)/shard_map/all_to_all | solution.py:431
  55.2 0.9 broadcast_in_dim.13
  56.1 3.5 %all-to-all-start.1 = ((bf16[8,288,128]{2,1,0:T(8,128)(2,1)}), bf16[8,288,128]{2,1,0:T(8,128)(2,1)S(1)}, u32[]{:S(2)}, u32[]{:S(2)}) async-start(bf16[8,288,128]{2,1,0:T(8,128)(2,1)} %broadcast_in_dim.13), calls=%async_computation.1 | async-start | bytes 1179648 | tf_op jit(solution)/shard_map/all_to_all | solution.py:435
  60.6 17.2 %all-to-all-done.1 = bf16[8,288,128]{2,1,0:T(8,128)(2,1)S(1)} async-done(((bf16[8,288,128]{2,1,0:T(8,128)(2,1)}), bf16[8,288,128]{2,1,0:T(8,128)(2,1)S(1)}, u32[]{:S(2)}, u32[]{:S(2)}) %all-to-all-start.1) | async-done | bytes 589856 | tf_op jit(solution)/shard_map/all_to_all | solution.py:435
  77.8 0.8 broadcast_in_dim.14
  78.7 5.1 %all-to-all-start.2 = ((bf16[16,112,128]{2,1,0:T(8,128)(2,1)}), bf16[16,112,128]{2,1,0:T(8,128)(2,1)S(1)}, u32[]{:S(2)}, u32[]{:S(2)}) async-start(bf16[16,112,128]{2,1,0:T(8,128)(2,1)} %broadcast_in_dim.14), calls=%async_computation.2 | async-start | bytes 917504 | tf_op jit(solution)/shard_map/all_to_all | solution.py:440
  84.1 1.5 %slice.59 = bf16[2,2,6,18,192]{4,1,3,2,0:T(2,128)(2,1)S(1)} reverse(bf16[2,2,6,18,192]{4,1,3,2,0:T(2,128)(2,1)S(1)} %get-tuple-element.53), dimensions={1} | reverse | bytes 331776 | tf_op jit(solution)/shard_map/slice | solution.py:408
  85.6 2.4 %collective-permute-start.4 = (bf16[2,2,6,18,192]{4,1,3,2,0:T(2,128)(2,1)S(1)}, bf16[2,2,6,18,192]{4,1,3,2,0:T(2,128)(2,1)S(1)}, u32[]{:S(2)}, u32[]{:S(2)}) collective-permute-start(bf16[2,2,6,18,192]{4,1,3,2,0:T(2,128)(2,1)S(1)} %slice.59), channel_id=1, source_target_pairs={{240,0},{0,16},{16,32},{32,48},{48,64},{64,80},{80,96},{96,112},{1... | collective-permute-start | bytes 497672 | tf_op jit(solution)/shard_map/ppermute | solution.py:400
  89.0 1.3 %collective-permute-start.5 = (bf16[2,2,6,6,192]{4,1,3,2,0:T(2,128)(2,1)S(1)}, bf16[2,2,6,6,192]{4,1,3,2,0:T(2,128)(2,1)S(1)}, u32[]{:S(2)}, u32[]{:S(2)}) collective-permute-start(bf16[2,2,6,6,192]{4,1,3,2,0:T(2,128)(2,1)S(1)} %slice.61), channel_id=1, source_target_pairs={{15,0},{0,1},{1,2},{2,3},{3,4},{4,5},{5,6},{6,7},{7,8},{8,9},{9,10... | collective-permute-start | bytes 165896 | tf_op jit(solution)/shard_map/ppermute | solution.py:400
  90.5 1.5 %slice.63 = bf16[2,2,6,18,192]{4,1,3,2,0:T(2,128)(2,1)S(1)} reverse(bf16[2,2,6,18,192]{4,1,3,2,0:T(2,128)(2,1)S(1)} %get-tuple-element.54), dimensions={1} | reverse | bytes 331776 | tf_op jit(solution)/shard_map/slice | solution.py:407
  92.1 1.7 %all-to-all-done.2 = bf16[16,112,128]{2,1,0:T(8,128)(2,1)S(1)} async-done(((bf16[16,112,128]{2,1,0:T(8,128)(2,1)}), bf16[16,112,128]{2,1,0:T(8,128)(2,1)S(1)}, u32[]{:S(2)}, u32[]{:S(2)}) %all-to-all-start.2) | async-done | bytes 458784 | tf_op jit(solution)/shard_map/all_to_all | solution.py:440
  93.8 2.5 %collective-permute-start.8 = (bf16[16,112,128]{2,1,0:T(8,128)(2,1)S(1)}, bf16[16,112,128]{2,1,0:T(8,128)(2,1)S(1)}, u32[]{:S(2)}, u32[]{:S(2)}) collective-permute-start(bf16[16,112,128]{2,1,0:T(8,128)(2,1)S(1)} %all-to-all-done.2), channel_id=1, source_target_pairs={{0,16},{16,0},{32,48},{48,32},{64,80},{80,64},{96,112},{112,96},{1... | collective-permute-start | bytes 1376264 | tf_op jit(solution)/shard_map/ppermute | solution.py:441
  96.2 1.6 %collective-permute-done.3 = bf16[2,2,6,6,192]{4,1,3,2,0:T(2,128)(2,1)S(1)} collective-permute-done((bf16[2,2,6,6,192]{4,1,3,2,0:T(2,128)(2,1)S(1)}, bf16[2,2,6,6,192]{4,1,3,2,0:T(2,128)(2,1)S(1)}, u32[]{:S(2)}, u32[]{:S(2)}) %collective-permute-start.3) | collective-permute-done | bytes 55328 | tf_op jit(solution)/shard_map/ppermute | solution.py:400
  97.9 0.9 maximum_maximum_fusion
  101.8 2.1 %shard_map.156 = (f32[192,576]{1,0:T(8,128)}, f32[192,192]{1,0:T(8,128)}, f32[192,768]{1,0:T(8,128)}, f32[192,768]{1,0:T(8,128)}, f32[1,1,6,24,552]{4,3,2,1,0:T(8,128)}) custom-call(s32[1]{0:T(128)} %bitcast.core_ref, s32[1]{0:T(128)} %bitcast.1.low_ref, bf16[1792,128]{1,0:T(8,128)(2,1)S(1)} %bitcast.23, bf16[1792,128]{1,0:T(8,128)(2,1)S(1)} %bitcast.24, ...), custom_call_target="tpu_custom_call" | custom-call | tf_op jit(solution)/shard_map/pallas_call | solution.py:489
  (52 shorter events, 7.1 us)
Async XLA Ops:
  0.6 1.0 copy-start.1
  1.6 1.0 copy-start.3
  2.6 14.2 %copy-start.11 = (bf16[192,576]{1,0:T(8,128)(2,1)S(1)}, bf16[192,576]{1,0:T(8,128)(2,1)}, u32[]{:S(2)}) copy-start(bf16[192,576]{1,0:T(8,128)(2,1)} %param.11) | copy-start | bytes 663556
  3.4 19.7 %collective-permute-start.1 = (bf16[2,2,6,8,192]{4,3,2,1,0:T(8,128)(2,1)}, bf16[2,2,6,8,192]{4,3,2,1,0:T(8,128)(2,1)}, u32[]{:S(2)}, u32[]{:S(2)}) collective-permute-start(bf16[2,2,6,8,192]{4,3,2,1,0:T(8,128)(2,1)} %get-tuple-element.22), channel_id=1, source_target_pairs={{1,0},{2,1},{3,2},{4,3},{5,4},{6,5},{7,6},{8,7},{9,8},{10,9},{11,1... | collective-permute-start | bytes 221192 | tf_op jit(solution)/shard_map/ppermute | solution.py:400
  10.8 12.3 %collective-permute-start.2 = (bf16[2,2,6,8,192]{4,3,2,1,0:T(8,128)(2,1)}, bf16[2,2,6,8,192]{4,3,2,1,0:T(8,128)(2,1)}, u32[]{:S(2)}, u32[]{:S(2)}) collective-permute-start(bf16[2,2,6,8,192]{4,3,2,1,0:T(8,128)(2,1)} %get-tuple-element.23), channel_id=1, source_target_pairs={{17,0},{18,1},{19,2},{20,3},{21,4},{22,5},{23,6},{24,7},{25,8},{26... | collective-permute-start | bytes 221192 | tf_op jit(solution)/shard_map/ppermute | solution.py:400
  11.8 11.3 %collective-permute-start = (bf16[2,2,6,24,192]{4,3,2,1,0:T(8,128)(2,1)}, bf16[2,2,6,24,192]{4,3,2,1,0:T(8,128)(2,1)S(1)}, u32[]{:S(2)}, u32[]{:S(2)}) collective-permute-start(bf16[2,2,6,24,192]{4,3,2,1,0:T(8,128)(2,1)} %get-tuple-element.21), channel_id=1, source_target_pairs={{16,0},{32,16},{48,32},{64,48},{80,64},{96,80},{112,96},{128,112},... | collective-permute-start | bytes 663560 | tf_op jit(solution)/shard_map/ppermute | solution.py:400
  16.8 2.6 %copy-start.9 = (bf16[276,384]{1,0:T(8,128)(2,1)S(1)}, bf16[276,384]{1,0:T(8,128)(2,1)}, u32[]{:S(2)}) copy-start(bf16[276,384]{1,0:T(8,128)(2,1)} %constant.36.clone.order_ref) | copy-start | bytes 635908
  18.1 5.0 %copy-start.2 = (bf16[2,12,24,192]{3,2,1,0:T(8,128)(2,1)S(1)}, bf16[2,12,24,192]{3,2,1,0:T(8,128)(2,1)}, u32[]{:S(2)}) copy-start(bf16[2,12,24,192]{3,2,1,0:T(8,128)(2,1)} %tokens_ref.3) | copy-start | bytes 663556
  18.1 5.0 %copy-start.4 = (bf16[2,12,24,192]{3,2,1,0:T(8,128)(2,1)S(1)}, bf16[2,12,24,192]{3,2,1,0:T(8,128)(2,1)}, u32[]{:S(2)}) copy-start(bf16[2,12,24,192]{3,2,1,0:T(8,128)(2,1)} %cots_ref.1) | copy-start | bytes 663556
  18.1 5.0 %copy-start.6 = (bf16[576,768]{1,0:T(8,128)(2,1)S(1)}, bf16[576,768]{1,0:T(8,128)(2,1)}, u32[]{:S(2)}) copy-start(bf16[576,768]{1,0:T(8,128)(2,1)} %constant.37.clone.order_ref) | copy-start | bytes 2654212
  18.1 5.1 %copy-start.7 = (bf16[192,768]{1,0:T(8,128)(2,1)S(1)}, bf16[192,768]{1,0:T(8,128)(2,1)}, u32[]{:S(2)}) copy-start(bf16[192,768]{1,0:T(8,128)(2,1)} %up_ref.1) | copy-start | bytes 884740
  18.1 5.1 %copy-start.8 = (bf16[768,192]{0,1:T(8,128)(2,1)S(1)}, bf16[768,192]{0,1:T(8,128)(2,1)}, u32[]{:S(2)}) copy-start(bf16[768,192]{0,1:T(8,128)(2,1)} %param.14) | copy-start | bytes 884740
  18.1 5.1 %copy-start.10 = (bf16[192,192]{1,0:T(8,128)(2,1)S(1)}, bf16[192,192]{1,0:T(8,128)(2,1)}, u32[]{:S(2)}) copy-start(bf16[192,192]{1,0:T(8,128)(2,1)} %proj_ref.1) | copy-start | bytes 221188
  21.8 1.2 %copy-start = (f32[2,864,144]{2,1,0:T(8,128)}, f32[2,864,144]{2,1,0:T(8,128)S(1)}, u32[]{:S(2)}) copy-start(f32[2,864,144]{2,1,0:T(8,128)S(1)} %shard_map.154.bias_ref) | copy-start | bytes 2985988
  36.8 3.6 %collective-permute-start.6 = (bf16[1792,128]{1,0:T(8,128)(2,1)S(1)}, bf16[1792,128]{1,0:T(8,128)(2,1)S(1)}, u32[]{:S(2)}, u32[]{:S(2)}) collective-permute-start(bf16[1792,128]{1,0:T(8,128)(2,1)S(1)} %get-tuple-element.27), channel_id=1, source_target_pairs={{0,16},{16,0},{32,48},{48,32},{64,80},{80,64},{96,112},{112,96},{1... | collective-permute-start | bytes 1376264 | tf_op jit(solution)/shard_map/ppermute | solution.py:428
  41.2 13.9 %all-to-all-start = ((bf16[16,112,128]{2,1,0:T(8,128)(2,1)}), bf16[16,112,128]{2,1,0:T(8,128)(2,1)S(1)}, u32[]{:S(2)}, u32[]{:S(2)}) async-start(bf16[16,112,128]{2,1,0:T(8,128)(2,1)} %bitcast.10), calls=%async_computation | async-start | bytes 917504 | tf_op jit(solution)/shard_map/all_to_all | solution.py:431
  44.8 4.1 %collective-permute-start.7 = (bf16[176,128]{1,0:T(8,128)(2,1)S(1)}, bf16[176,128]{1,0:T(8,128)(2,1)S(1)}, u32[]{:S(2)}, u32[]{:S(2)}) collective-permute-start(bf16[176,128]{1,0:T(8,128)(2,1)S(1)} %get-tuple-element.29), channel_id=1, source_target_pairs={{0,1},{1,0},{2,3},{3,2},{4,5},{5,4},{6,7},{7,6},{8,9},{9,8},{10,11... | collective-permute-start | bytes 135176 | tf_op jit(solution)/shard_map/ppermute | solution.py:429
  56.1 21.7 %all-to-all-start.1 = ((bf16[8,288,128]{2,1,0:T(8,128)(2,1)}), bf16[8,288,128]{2,1,0:T(8,128)(2,1)S(1)}, u32[]{:S(2)}, u32[]{:S(2)}) async-start(bf16[8,288,128]{2,1,0:T(8,128)(2,1)} %broadcast_in_dim.13), calls=%async_computation.1 | async-start | bytes 1179648 | tf_op jit(solution)/shard_map/all_to_all | solution.py:435
  78.7 15.1 %all-to-all-start.2 = ((bf16[16,112,128]{2,1,0:T(8,128)(2,1)}), bf16[16,112,128]{2,1,0:T(8,128)(2,1)S(1)}, u32[]{:S(2)}, u32[]{:S(2)}) async-start(bf16[16,112,128]{2,1,0:T(8,128)(2,1)} %broadcast_in_dim.14), calls=%async_computation.2 | async-start | bytes 917504 | tf_op jit(solution)/shard_map/all_to_all | solution.py:440
  85.6 12.3 %collective-permute-start.4 = (bf16[2,2,6,18,192]{4,1,3,2,0:T(2,128)(2,1)S(1)}, bf16[2,2,6,18,192]{4,1,3,2,0:T(2,128)(2,1)S(1)}, u32[]{:S(2)}, u32[]{:S(2)}) collective-permute-start(bf16[2,2,6,18,192]{4,1,3,2,0:T(2,128)(2,1)S(1)} %slice.59), channel_id=1, source_target_pairs={{240,0},{0,16},{16,32},{32,48},{48,64},{64,80},{80,96},{96,112},{1... | collective-permute-start | bytes 497672 | tf_op jit(solution)/shard_map/ppermute | solution.py:400
  89.0 7.3 %collective-permute-start.5 = (bf16[2,2,6,6,192]{4,1,3,2,0:T(2,128)(2,1)S(1)}, bf16[2,2,6,6,192]{4,1,3,2,0:T(2,128)(2,1)S(1)}, u32[]{:S(2)}, u32[]{:S(2)}) collective-permute-start(bf16[2,2,6,6,192]{4,1,3,2,0:T(2,128)(2,1)S(1)} %slice.61), channel_id=1, source_target_pairs={{15,0},{0,1},{1,2},{2,3},{3,4},{4,5},{5,6},{6,7},{7,8},{8,9},{9,10... | collective-permute-start | bytes 165896 | tf_op jit(solution)/shard_map/ppermute | solution.py:400
  90.2 7.6 %collective-permute-start.3 = (bf16[2,2,6,6,192]{4,1,3,2,0:T(2,128)(2,1)S(1)}, bf16[2,2,6,6,192]{4,1,3,2,0:T(2,128)(2,1)S(1)}, u32[]{:S(2)}, u32[]{:S(2)}) collective-permute-start(bf16[2,2,6,6,192]{4,1,3,2,0:T(2,128)(2,1)S(1)} %slice.57), channel_id=1, source_target_pairs={{255,0},{240,1},{241,2},{242,3},{243,4},{244,5},{245,6},{246,7},{2... | collective-permute-start | bytes 165896 | tf_op jit(solution)/shard_map/ppermute | solution.py:400
  92.1 9.7 %copy-start.5 = (bf16[2,384,552]{2,1,0:T(8,128)(2,1)S(1)}, bf16[2,384,552]{2,1,0:T(8,128)(2,1)}, u32[]{:S(2)}) copy-start(bf16[2,384,552]{2,1,0:T(8,128)(2,1)} %constant.38.clone.back_ref) | copy-start | bytes 2543620
  93.8 8.0 %collective-permute-start.8 = (bf16[16,112,128]{2,1,0:T(8,128)(2,1)S(1)}, bf16[16,112,128]{2,1,0:T(8,128)(2,1)S(1)}, u32[]{:S(2)}, u32[]{:S(2)}) collective-permute-start(bf16[16,112,128]{2,1,0:T(8,128)(2,1)S(1)} %all-to-all-done.2), channel_id=1, source_target_pairs={{0,16},{16,0},{32,48},{48,32},{64,80},{80,64},{96,112},{112,96},{1... | collective-permute-start | bytes 1376264 | tf_op jit(solution)/shard_map/ppermute | solution.py:441
  98.8 3.0 %collective-permute-start.9 = (bf16[176,128]{1,0:T(8,128)(2,1)S(1)}, bf16[176,128]{1,0:T(8,128)(2,1)S(1)}, u32[]{:S(2)}, u32[]{:S(2)}) collective-permute-start(bf16[176,128]{1,0:T(8,128)(2,1)S(1)} %slice.77.bmine_ref), channel_id=1, source_target_pairs={{0,1},{1,0},{2,3},{3,2},{4,5},{5,4},{6,7},{7,6},{8,9},{9,8},{10,11... | collective-permute-start | bytes 135176 | tf_op jit(solution)/shard_map/ppermute | solution.py:438

commit v3 on v2

--- a/solution.py
+++ b/solution.py
@@ -30,7 +30,8 @@
 LEFT = CUT - 2 * LANES
 EPS = 1e-05
 SCALE = HEAD ** (-0.5)
-VMEM = 48 * 1024 * 1024
+LARGE = 28 * 1024 * 1024
+SMALL = 12 * 1024 * 1024
 BF = jnp.bfloat16
 F32 = jnp.float32
 
@@ -106,23 +107,24 @@
 
 
 def bias_kernel(last_ref, table_ref, order_ref, bias_ref):
-    order = order_ref[...]
-    table = table_ref[...]
+    table = table_ref[0, 0].reshape(HEADS * 2 * WA, 2 * CUT)
     high = table.astype(BF)
     rest = table - high.astype(F32)
     middle = rest.astype(BF)
     low = (rest - middle.astype(F32)).astype(BF)
-    wide = dot(high, order) + (dot(middle, order) + dot(low, order))
     row = lax.broadcasted_iota(jnp.int32, (2 * WA, WIDE), 0)
     row_i = lax.broadcasted_iota(jnp.int32, (2 * WA, WIN), 0) % WA
     row_j = lax.broadcasted_iota(jnp.int32, (2 * WA, WIN), 1) % WA
     split = (row_i >= HALF) != (row_j >= HALF)
     split = jnp.logical_and(split, last_ref[0] == 1)
     for level in range(2):
+        order = order_ref[level]
+        wide = dot(high, order) + (dot(middle, order) + dot(low, order))
         for head in range(HEADS):
-            at = (level * HEADS + head) * 2 * WA
-            both = wide[at : at + 2 * WA]
-            both = jnp.where(row < WA, pltpu.roll(both, WIDE - WA, 1), both)
+            both = wide[head * 2 * WA : (head + 1) * 2 * WA]
+            other = pltpu.roll(both, WA, 0)
+            upper, lower = (other, both) if level else (both, other)
+            both = jnp.where(row < WA, pltpu.roll(upper, WIDE - WA, 1), lower)
             blocks = []
             for pair in range(WO // 2):
                 turn = (WO - 2 - 2 * pair) * WA
@@ -133,9 +135,9 @@
 
 
 def block_kernel(
-    core_ref, low_ref, tokens_ref, cots_ref, below_ref, beside_ref, corner_ref, order_ref,
+    core_ref, tokens_ref, cots_ref, below_ref, beside_ref, corner_ref, order_ref,
     wq_ref, wk_ref, wv_ref, proj_ref, up_ref, down_ref, bias_ref,
-    result_ref, gtok_ref, mine_ref, other_ref, bmine_ref, bother_ref,
+    result_ref, gtok_ref, mine_ref, other_ref, gbias_ref,
     source_ref, x_ref, cot_ref, bsum_ref, normed_ref, q_ref, k_ref, v_ref, prob_ref, att_ref, res_ref, two_ref, upper_ref, gact_ref, act_ref,
     gup_ref, gres_ref, gmix_ref, gatt_ref, dq_ref, dk_ref, dv_ref, ds_ref, pad_ref, turned_ref,
     unit_ref, inverse_ref, unit_two_ref, inverse_two_ref, mean_ref,
@@ -326,19 +328,52 @@
             left = left + (pltpu.roll(rest, pair * LEFT, 1) if pair else rest)
         bsum_ref[level, 2 * MAIN : 2 * MAIN + 2 * WA, :] = left
         bsum_ref[level, 2 * MAIN + 2 * WA :, :] = jnp.zeros((BIAS_ROWS - 2 * MAIN - 2 * WA, LANES), F32)
-    lower = low_ref[0] == 0
-    zero, one = bsum_ref[0], bsum_ref[1]
-    bmine_ref[...] = jnp.where(lower, zero, one)
-    bother_ref[...] = jnp.where(lower, one, zero).astype(BF)
+    gbias_ref[...] = bsum_ref[...].reshape(2 * BIAS_ROWS, LANES).astype(BF)
+
+
+def added(one, two):
+    return (one.astype(F32) + two.astype(F32)).astype(BF)
+
+
+def middle_kernel(got_ref, own_ref, came_ref, wait_ref, wide_ref, bias_ref):
+    total = jnp.sum(got_ref[...].astype(F32), axis=0).astype(BF)
+    for block in range(wide_ref.shape[0]):
+        wide_ref[block] = total
+    bias_ref[...] = added(own_ref[...], came_ref[...])
+
+
+def split_kernel(result_ref, gtok_ref, order_ref, own_ref, above_ref, beside_ref, corner_ref):
+    near, far = 2 * HALF * 2 * WO, 2 * HALF * 8
+    for array, ref in enumerate((result_ref, gtok_ref)):
+        rows = dot(order_ref[...], ref[...])
+        for level in range(2):
+            for row in range(HALF):
+                place = level * HALF + row
+                at = place * 2 * WO
+                own_ref[array, level, row] = rows[at : at + 2 * WO].astype(BF)
+                above_ref[array, level, row] = rows[near + at : near + at + 2 * WO].astype(BF)
+                at = 2 * near + place * 8
+                beside_ref[array, level, row] = rows[at : at + 8].astype(BF)
+                corner_ref[array, level, row] = rows[far + at : far + at + 8].astype(BF)
+
+
+def join_kernel(own_ref, above_ref, beside_ref, corner_ref, result_ref, gtok_ref):
+    for array, ref in enumerate((result_ref, gtok_ref)):
+        for level in range(2):
+            for row in range(HALF):
+                for start, long_ref, short_ref in ((0, above_ref, corner_ref), (HALF, own_ref, beside_ref)):
+                    rows = long_ref[array, level, row].astype(F32)
+                    first = rows[:8] + short_ref[array, level, row].astype(F32)
+                    ref[level, start + row] = jnp.concatenate([first, rows[8:]], axis=0).astype(BF)
 
 
 def final_kernel(
-    count, core_ref, low_ref, mine_ref, other_ref, bmine_ref, bother_ref, back_ref,
+    count, core_ref, mine_ref, other_ref, gbias_ref, back_ref,
     qkv_ref, proj_ref, up_ref, down_ref, bias_ref,
 ):
     first = core_ref[0] == 0
-    mine = mine_ref[...].astype(F32)
-    other = other_ref[...].astype(F32)
+    mine = mine_ref[...].astype(F32)[: 9 * C]
+    other = other_ref[...].astype(F32)[: 9 * C]
     total = jnp.sum(mine * mine) + jnp.sum(other * other)
     factor = jnp.minimum(1.0, math.sqrt(count) / (jnp.sqrt(jnp.full((8, LANES), total)) + 1e-06))[:1]
     zero = jnp.where(first, mine, other) * factor
@@ -357,11 +392,10 @@
     qkv_ref[:, 2 * C :] = jnp.concatenate([chunk(zero, 8), right[:, :last]], axis=1)
     proj_ref[...] = jnp.concatenate([chunk(one, 6), right[:, last:]], axis=1)
 
-    lower = low_ref[0] == 0
-    bmine = bmine_ref[...].astype(F32)
-    bother = bother_ref[...].astype(F32)
+    sums = gbias_ref[...].astype(F32)
     tables = []
-    for level, packed in enumerate((jnp.where(lower, bmine, bother), jnp.where(lower, bother, bmine))):
+    for level in range(2):
+        packed = sums[level * BIAS_ROWS : (level + 1) * BIAS_ROWS]
         left = packed[2 * MAIN : 2 * MAIN + 2 * WA]
         left = [left] + [pltpu.roll(left, LANES - pair * LEFT, 1) for pair in range(1, HEADS // 2)]
         rows = [packed[:MAIN], packed[MAIN : 2 * MAIN], jnp.concatenate(left, axis=0)]
@@ -374,7 +408,7 @@
         bias_ref[0, 0, 2 * pair + 1] = jnp.where(row < WA, pltpu.roll(upper, WA, 0), lower)
 
 
-def call(kernel, outs, scalars, arrays, scratch=()):
+def call(kernel, outs, scalars, arrays, scratch=(), limit=SMALL):
     spaces = [pl.BlockSpec(memory_space=pltpu.SMEM)] * scalars
     spaces += [pl.BlockSpec(memory_space=pltpu.VMEM)] * arrays
     return pl.pallas_call(
@@ -383,7 +417,7 @@
         in_specs=spaces,
         out_specs=[pl.BlockSpec(memory_space=pltpu.VMEM)] * len(outs),
         scratch_shapes=scratch,
-        compiler_params=pltpu.CompilerParams(vmem_limit_bytes=VMEM),
+        compiler_params=pltpu.CompilerParams(vmem_limit_bytes=limit),
     )
 
 
@@ -400,53 +434,60 @@
     return lax.ppermute(block, tuple(axes), route)
 
 
-def rolled_back(pair):
-    whole = pair.reshape(2, 2, 2, WO, WA, C).transpose(0, 2, 4, 1, 3, 5)
-    whole = whole.reshape(2, 2, WA, 2 * WO, C)[:, ::-1]
-    cut = 2 * WO - HALF
-    own, beside = whole[:, :, :HALF, :cut], whole[:, :, :HALF, cut:]
-    above, corner = whole[:, :, HALF:, :cut], whole[:, :, HALF:, cut:]
+def roll_back_start(result, grad_tokens):
+    wide, narrow = shape(2, 2, HALF, 2 * WO, C, kind=BF), shape(2, 2, HALF, 8, C, kind=BF)
+    order = jnp.asarray(window_order().T, BF)
+    pieces = call(split_kernel, [wide, wide, narrow, narrow], 0, 3)(result, grad_tokens, order)
+    own, above, beside, corner = pieces
     above = from_next(above, ["lat"], -1)
+    corner = from_next(corner, ["lat", "lon"], -1)
     beside = from_next(beside, ["lon"], -1)
-    corner = from_next(corner, ["lat", "lon"], -1)
-    upper = jnp.concatenate([corner, above], axis=3)
-    lower = jnp.concatenate([beside, own], axis=3)
-    return jnp.concatenate([upper, lower], axis=2)
-
-
-def gradient_sums(mine, other, bmine, bother):
+    return own, above, beside, corner
+
+
+def roll_back_end(pieces):
+    whole = shape(2, WA, 2 * WO, C, kind=BF)
+    return call(join_kernel, [whole, whole], 0, 4)(*pieces)
+
+
+def gradient_sums(mine, other, bias, pieces):
     lat, lon = lax.axis_size("lat"), lax.axis_size("lon")
     half, depth = lat // 2, lon // 2
     pairs = [(i, i ^ 1) for i in range(lat)]
-    beside = [(i, i ^ 1) for i in range(lon)]
     planes = [
         [(2 * i + core) * lon + 2 * z + low for i in range(half) for low in range(2)]
         for core in range(2)
         for z in range(depth)
     ]
     columns = [[2 * z + low for z in range(depth)] for low in range(2)]
+    share = PACKED // lat
+
+    def partner(block, distance):
+        return lax.ppermute(block, "lon", [(i, i ^ distance) for i in range(lon)])
+
+    def middle(got, own, came, blocks, wait):
+        outs = [shape(blocks, share, LANES, kind=BF), shape(2 * BIAS_ROWS, LANES, kind=BF)]
+        return call(middle_kernel, outs, 0, 4)(got, own, came, wait)
+
     mine = mine + lax.ppermute(other, "lat", pairs).astype(F32)
-    bmine = (bmine + lax.ppermute(bother, "lon", beside).astype(F32)).astype(BF)
-    mine = mine.astype(BF).reshape(lat, PACKED // lat, LANES)
+    mine = mine.astype(BF).reshape(lat, share, LANES)
     got = lax.all_to_all(mine, ("lat", "lon"), 0, 0, axis_index_groups=planes)
-    part = jnp.sum(got.astype(F32), axis=0).astype(BF)
-    share = part.shape[0]
-    part = jnp.concatenate([part, bmine])
-    got = lax.all_to_all(jnp.broadcast_to(part, (depth,) + part.shape), "lon", 0, 0, axis_index_groups=columns)
-    part = jnp.sum(got.astype(F32), axis=0).astype(BF)
-    part, bmine = part[:share], part[share:]
-    bother = lax.ppermute(bmine, "lon", beside)
-    part = jnp.broadcast_to(part, (lat,) + part.shape)
-    mine = lax.all_to_all(part, ("lat", "lon"), 0, 0, axis_index_groups=planes)
+    bias = added(bias, partner(bias, 1))
+    wide, bias = middle(got, bias, partner(bias, 2), depth, bias[:8])
+    got = lax.all_to_all(wide, "lon", 0, 0, axis_index_groups=columns)
+    wait = functools.reduce(added, [piece[0, 0, 0, :8] for piece in pieces[1:]])
+    wide, bias = middle(got, bias, partner(bias, 4), lat, wait)
+    bias = added(bias, partner(bias, 8))
+    mine = lax.all_to_all(wide, ("lat", "lon"), 0, 0, axis_index_groups=planes)
+    mine = lax.dynamic_update_slice(mine, bias[None, :16], (lat - 1, share - 16, 0))
     other = lax.ppermute(mine, "lat", pairs)
-    return mine.reshape(PACKED, LANES), other.reshape(PACKED, LANES), bmine, bother
+    return mine.reshape(PACKED, LANES), other.reshape(PACKED, LANES), bias
 
 
 def on_device(tokens, w_qkv, w_proj, w_up, w_down, earth_bias, cotangent):
     band = lax.axis_index("lat")
     bands = lax.axis_size("lat")
     core = (band % 2).astype(jnp.int32).reshape(1)
-    low = (lax.axis_index("lon") % 2).astype(jnp.int32).reshape(1)
     last = (band == bands - 1).astype(jnp.int32).reshape(1)
 
     wide, narrow = shape(2, 2, HALF, 2 * WO, C, kind=BF), shape(2, 2, HALF, 8, C, kind=BF)
@@ -454,11 +495,9 @@
     below = from_next(below, ["lat"], 1)
     corner = from_next(corner, ["lat", "lon"], 1)
     beside = from_next(beside, ["lon"], 1)
-    table = earth_bias.reshape(HEADS, 2, WA, 2, CUT)
-    table = jnp.stack([table[:, 0, :, 0], table[:, 1, :, 1]])
-    table = jnp.broadcast_to(table[:, :, None], (2, HEADS, 2, WA, CUT)).reshape(-1, CUT)
-    order = jnp.asarray(table_order(), BF)
-    bias = call(bias_kernel, [shape(2, HEADS * WIN, WIN)], 1, 2)(last, table, order)[0]
+    back = table_back()
+    order = jnp.asarray(back.transpose(0, 2, 1), BF)
+    bias = call(bias_kernel, [shape(2, HEADS * WIN, WIN)], 1, 2)(last, earth_bias, order)[0]
 
     def tokens_of(width, kind=BF):
         return pltpu.VMEM((TOKENS, width), kind)
@@ -468,8 +507,7 @@
         shape(TOKENS, C, kind=BF),
         shape(PACKED, LANES),
         shape(PACKED, LANES, kind=BF),
-        shape(BIAS_ROWS, LANES),
-        shape(BIAS_ROWS, LANES, kind=BF),
+        shape(2 * BIAS_ROWS, LANES, kind=BF),
     ]
     scratch = [pltpu.VMEM((SOURCES, C), F32), tokens_of(C), tokens_of(C), pltpu.VMEM((2, BIAS_ROWS, LANES), F32)]
     scratch += [tokens_of(C)] * 4 + [pltpu.VMEM((PARTS, HEADS * WIN, WIN), BF), tokens_of(C), tokens_of(C, F32)]
@@ -477,19 +515,18 @@
     scratch += [tokens_of(C)] * 5 + [pltpu.VMEM((2, HEADS * WIN, WIN), F32)]
     scratch += [pltpu.VMEM((2 * HEADS, WIN, WIDE), F32), pltpu.VMEM((C, WIN), F32)]
     scratch += [tokens_of(C, F32)] * 5
-    result, grad_tokens, *grads = call(block_kernel, outs, 2, 13, scratch)(
-        core, low, tokens, cotangent, below, beside, corner, jnp.asarray(window_order(), BF),
+    result, grad_tokens, *grads = call(block_kernel, outs, 1, 13, scratch, limit=LARGE)(
+        core, tokens, cotangent, below, beside, corner, jnp.asarray(window_order(), BF),
         w_qkv[:, :C], w_qkv[:, C : 2 * C], w_qkv[:, 2 * C :], w_proj, w_up, w_down.T, bias,
     )
-    sums = gradient_sums(*grads)
-    back = rolled_back(jnp.stack([result, grad_tokens]))
+    pieces = roll_back_start(result, grad_tokens)
+    sums = gradient_sums(*grads, pieces)
+    result, grad_tokens = roll_back_end(pieces)
 
     count = w_qkv.size + w_proj.size + w_up.size + w_down.size + earth_bias.size * bands
     outs = [shape(C, 3 * C), shape(C, C), shape(C, HID), shape(C, HID), shape(1, 1, HEADS, 2 * WA, 2 * CUT)]
-    grads = call(functools.partial(final_kernel, count), outs, 2, 5)(
-        core, low, *sums, jnp.asarray(table_back(), BF)
-    )
-    return (back[0], back[1], *grads[:3], grads[3].T, grads[4])
+    grads = call(functools.partial(final_kernel, count), outs, 1, 4)(core, *sums, jnp.asarray(back, BF))
+    return (result, grad_tokens, *grads[:3], grads[3].T, grads[4])
 
 
 def solution(mesh):

time: 105 us -> 95.6 us (0.910)
  starting transfers between devices: 34.3 us -> 50.5 us
  waiting for transfers between devices: 31.7 us -> 18.9 us
  local copies, waits for them, and re-layouts: 15.7 us -> 4.05 us
  other arithmetic: 2.37 us -> 0.95 us
    all_to_all x2, waiting for transfers between devices: 18.9 us -> 2.62 us  [the longest x1 2.62 us: gradient_sums(): mine = lax.all_to_all(wide, ('lat', 'lon'), 0, 0, axis_index_groups=planes)]
    ppermute x6, starting transfers between devices: 15.9 us -> 22.6 us  [from_next(): return lax.ppermute(block, tuple(axes), route)]
    all_to_all x1, waiting for transfers between devices: 6.21 us -> 0.01 us  [gradient_sums(): got = lax.all_to_all(mine, ('lat', 'lon'), 0, 0, axis_index_groups=planes)]
    ppermute x2 -> x4, waiting for transfers between devices: 3.5 us -> 9.22 us  [partner(): return lax.ppermute(block, 'lon', [(i, i ^ distance) for i in range(lon)])]
    ppermute x2 -> x4, starting transfers between devices: 1.66 us -> 6.77 us  [partner(): return lax.ppermute(block, 'lon', [(i, i ^ distance) for i in range(lon)])]
    slice x8 -> x1, local copies, waits for them, and re-layouts: 4.33 us -> 0.01 us  [gradient_sums(): wide, bias = middle(got, bias, partner(bias, 2), depth, bias[:8])]
    ppermute x6, waiting for transfers between devices: 1.66 us -> 4.98 us  [from_next(): return lax.ppermute(block, tuple(axes), route)]
    all_to_all x1, starting transfers between devices: 3.56 us -> 6.82 us  [gradient_sums(): got = lax.all_to_all(mine, ('lat', 'lon'), 0, 0, axis_index_groups=planes)]
  transfers between devices with their start and end apart: 13 -> 15, of which waited for: 7 -> 8; matrix products, arithmetic and copies ran while one was open for 12% -> 1% of each run, Pallas kernels for 2% -> 5%
where the time goes in v3:
time: 95.6 us; the launch traced here: 95.1 us
  starting transfers between devices  50.5 us (53%)
  Pallas kernels  19.9 us (21%)
  waiting for transfers between devices  18.9 us (20%)
  local copies, waits for them, and re-layouts  4.05 us (4%)
    ppermute x6, starting transfers between devices, from_next(): return lax.ppermute(block, tuple(axes), route)  22.6 us
    pallas_call x1, Pallas kernels, on_device(): call(block_kernel, outs, 1, 13, scratch, limit=LARGE)  11.8 us
    ppermute x4, waiting for transfers between devices, partner(): return lax.ppermute(block, 'lon', [(i, i ^ distance) for i in range(lon)])  9.22 us
    all_to_all x1, starting transfers between devices, gradient_sums(): got = lax.all_to_all(mine, ('lat', 'lon'), 0, 0, axis_index_groups=planes)  6.82 us
    ppermute x4, starting transfers between devices, partner(): return lax.ppermute(block, 'lon', [(i, i ^ distance) for i in range(lon)])  6.77 us
    all_to_all x1, starting transfers between devices, gradient_sums(): mine = lax.all_to_all(wide, ('lat', 'lon'), 0, 0, axis_index_groups=planes)  6.26 us
    ppermute x6, waiting for transfers between devices, from_next(): return lax.ppermute(block, tuple(axes), route)  4.98 us
    all_to_all x1, starting transfers between devices, gradient_sums(): got = lax.all_to_all(wide, 'lon', 0, 0, axis_index_groups=columns)  4.33 us
  transfers between devices with their start and end apart: 15, of which 8 were waited for; matrix products, arithmetic and copies ran while one was open for 1% of the time, Pallas kernels for 5%

profile of v3, /device:TPU:1, one launch (start us, length us, event | category | flops | bytes accessed | tf_op | source)
XLA Modules:
  0.0 95.1 jit_solution(11889763508947998869)
XLA Ops:
  0.6 1.0 %copy-done = bf16[2,12,24,192]{3,2,1,0:T(8,128)(2,1)S(1)} copy-done((bf16[2,12,24,192]{3,2,1,0:T(8,128)(2,1)S(1)}, bf16[2,12,24,192]{3,2,1,0:T(8,128)(2,1)}, u32[]{:S(2)}) %copy-start) | copy-done | bytes 221208
  1.6 1.0 %copy-done.2 = bf16[2,12,24,192]{3,2,1,0:T(8,128)(2,1)S(1)} copy-done((bf16[2,12,24,192]{3,2,1,0:T(8,128)(2,1)S(1)}, bf16[2,12,24,192]{3,2,1,0:T(8,128)(2,1)}, u32[]{:S(2)}) %copy-start.2) | copy-done | bytes 221208
  2.6 0.7 shard_map.162
  3.2 7.4 %collective-permute-start.1 = (bf16[2,2,6,8,192]{4,3,2,1,0:T(8,128)(2,1)}, bf16[2,2,6,8,192]{4,3,2,1,0:T(8,128)(2,1)S(1)}, u32[]{:S(2)}, u32[]{:S(2)}) collective-permute-start(bf16[2,2,6,8,192]{4,3,2,1,0:T(8,128)(2,1)} %get-tuple-element.31), channel_id=1, source_target_pairs={{1,0},{2,1},{3,2},{4,3},{5,4},{6,5},{7,6},{8,7},{9,8},{10,9},{11,1... | collective-permute-start | bytes 221192 | tf_op jit(solution)/shard_map/ppermute | solution.py:434
  10.7 1.0 %collective-permute-start.2 = (bf16[2,2,6,8,192]{4,3,2,1,0:T(8,128)(2,1)S(1)}, bf16[2,2,6,8,192]{4,3,2,1,0:T(8,128)(2,1)S(1)}, u32[]{:S(2)}, u32[]{:S(2)}) collective-permute-start(bf16[2,2,6,8,192]{4,3,2,1,0:T(8,128)(2,1)S(1)} %get-tuple-element.32), channel_id=1, source_target_pairs={{17,0},{18,1},{19,2},{20,3},{21,4},{22,5},{23,6},{24,7},{25,8},{26... | collective-permute-start | bytes 221192 | tf_op jit(solution)/shard_map/ppermute | solution.py:434
  11.7 3.5 %collective-permute-start = (bf16[2,2,6,24,192]{4,3,2,1,0:T(8,128)(2,1)S(1)}, bf16[2,2,6,24,192]{4,3,2,1,0:T(8,128)(2,1)S(1)}, u32[]{:S(2)}, u32[]{:S(2)}) collective-permute-start(bf16[2,2,6,24,192]{4,3,2,1,0:T(8,128)(2,1)S(1)} %get-tuple-element.30), channel_id=1, source_target_pairs={{16,0},{32,16},{48,32},{64,48},{80,64},{96,80},{112,96},{128,112},... | collective-permute-start | bytes 663560 | tf_op jit(solution)/shard_map/ppermute | solution.py:434
  15.2 1.1 %fusion.2 = (bf16[192,192]{1,0:T(8,128)(2,1)S(1)}, bf16[192,192]{1,0:T(8,128)(2,1)S(1)}, bf16[192,192]{1,0:T(8,128)(2,1)S(1)}) fusion(bf16[192,576]{1,0:T(8,128)(2,1)} %param.12), kind=kLoop, calls=%fused_computation.8 | loop fusion | bytes 442368 | tf_op jit(solution)/shard_map/slice | solution.py:520
  16.3 1.0 %copy-done.8 = f32[1,1,6,24,552]{4,3,2,1,0:T(8,128)S(1)} copy-done((f32[1,1,6,24,552]{4,3,2,1,0:T(8,128)S(1)}, f32[1,1,6,24,552]{4,3,2,1,0:T(8,128)}, u32[]{:S(2)}) %copy-start.8) | copy-done | bytes 317976
  17.3 2.1 %shard_map.163.bias_ref = f32[2,864,144]{2,1,0:T(8,128)S(1)} custom-call(s32[1]{0:T(128)} %bitcast.2.last_ref, f32[1,1,6,24,552]{4,3,2,1,0:T(8,128)S(1)} %copy-done.8, bf16[2,552,384]{2,1,0:T(8,128)(2,1)S(1)} %copy-done.7), custom_call_target="tpu_custom_call" | custom-call | tf_op jit(solution)/shard_map/pallas_call | solution.py:500
  19.5 11.8 %shard_map.164 = (bf16[576,192]{1,0:T(8,128)(2,1)S(1)}, bf16[576,192]{1,0:T(8,128)(2,1)S(1)}, f32[1792,128]{1,0:T(8,128)S(1)}, bf16[1792,128]{1,0:T(8,128)(2,1)S(1)}, bf16[352,128]{1,0:T(8,128)(2,1)S(1)}) custom-call(s32[1]{0:T(128)} %bitcast.core_ref, bf16[2,12,24,192]{3,2,1,0:T(8,128)(2,1)S(1)} %copy-done.1, bf16[2,12,24,192]{3,2,1,0:T(8,128)(2,1)S(1)} %copy-done.3, ...), custom_call_target="tpu_custom_call" | custom-call | tf_op jit(solution)/shard_map/pallas_call | solution.py:518
  31.3 2.1 %collective-permute-start.6 = (bf16[1792,128]{1,0:T(8,128)(2,1)S(1)}, bf16[1792,128]{1,0:T(8,128)(2,1)S(1)}, u32[]{:S(2)}, u32[]{:S(2)}) collective-permute-start(bf16[1792,128]{1,0:T(8,128)(2,1)S(1)} %get-tuple-element.42), channel_id=1, source_target_pairs={{0,16},{16,0},{32,48},{48,32},{64,80},{80,64},{96,112},{112,96},{1... | collective-permute-start | bytes 1376264 | tf_op jit(solution)/shard_map/ppermute | solution.py:472
  33.5 1.4 %collective-permute-done.6 = bf16[1792,128]{1,0:T(8,128)(2,1)S(1)} collective-permute-done((bf16[1792,128]{1,0:T(8,128)(2,1)S(1)}, bf16[1792,128]{1,0:T(8,128)(2,1)S(1)}, u32[]{:S(2)}, u32[]{:S(2)}) %collective-permute-start.6) | collective-permute-done | bytes 458784 | tf_op jit(solution)/shard_map/ppermute | solution.py:472
  34.9 0.9 add_convert_fusion
  35.8 6.8 %all-to-all-start = ((bf16[16,112,128]{2,1,0:T(8,128)(2,1)}), bf16[16,112,128]{2,1,0:T(8,128)(2,1)S(1)}, u32[]{:S(2)}, u32[]{:S(2)}) async-start(bf16[16,112,128]{2,1,0:T(8,128)(2,1)} %bitcast.3), calls=%async_computation | async-start | bytes 917504 | tf_op jit(solution)/shard_map/all_to_all | solution.py:474
  42.6 1.4 %collective-permute-start.7 = (bf16[352,128]{1,0:T(8,128)(2,1)S(1)}, bf16[352,128]{1,0:T(8,128)(2,1)S(1)}, u32[]{:S(2)}, u32[]{:S(2)}) collective-permute-start(bf16[352,128]{1,0:T(8,128)(2,1)S(1)} %get-tuple-element.43), channel_id=1, source_target_pairs={{0,1},{1,0},{2,3},{3,2},{4,5},{5,4},{6,7},{7,6},{8,9},{9,8},{10,11... | collective-permute-start | bytes 270344 | tf_op jit(solution)/shard_map/ppermute | solution.py:466
  44.0 4.7 %collective-permute-done.7 = bf16[352,128]{1,0:T(8,128)(2,1)S(1)} collective-permute-done((bf16[352,128]{1,0:T(8,128)(2,1)S(1)}, bf16[352,128]{1,0:T(8,128)(2,1)S(1)}, u32[]{:S(2)}, u32[]{:S(2)}) %collective-permute-start.7) | collective-permute-done | bytes 90144 | tf_op jit(solution)/shard_map/ppermute | solution.py:466
  48.8 0.8 shard_map.165
  49.6 5.2 %collective-permute-start.3 = (bf16[2,2,6,24,192]{4,3,2,1,0:T(8,128)(2,1)S(1)}, bf16[2,2,6,24,192]{4,3,2,1,0:T(8,128)(2,1)S(1)}, u32[]{:S(2)}, u32[]{:S(2)}) collective-permute-start(bf16[2,2,6,24,192]{4,3,2,1,0:T(8,128)(2,1)S(1)} %get-tuple-element.36), channel_id=1, source_target_pairs={{240,0},{0,16},{16,32},{32,48},{48,64},{64,80},{80,96},{96,112},{1... | collective-permute-start | bytes 663560 | tf_op jit(solution)/shard_map/ppermute | solution.py:434
  54.8 0.8 shard_map.167
  55.5 4.3 %all-to-all-start.1 = ((bf16[8,112,128]{2,1,0:T(8,128)(2,1)}), bf16[8,112,128]{2,1,0:T(8,128)(2,1)S(1)}, u32[]{:S(2)}, u32[]{:S(2)}) async-start(bf16[8,112,128]{2,1,0:T(8,128)(2,1)} %get-tuple-element.44), calls=%async_computation.1 | async-start | bytes 458752 | tf_op jit(solution)/shard_map/all_to_all | solution.py:477
  60.1 5.2 %collective-permute-start.5 = (bf16[2,2,6,8,192]{4,3,2,1,0:T(8,128)(2,1)S(1)}, bf16[2,2,6,8,192]{4,3,2,1,0:T(8,128)(2,1)S(1)}, u32[]{:S(2)}, u32[]{:S(2)}) collective-permute-start(bf16[2,2,6,8,192]{4,3,2,1,0:T(8,128)(2,1)S(1)} %get-tuple-element.38), channel_id=1, source_target_pairs={{255,0},{240,1},{241,2},{242,3},{243,4},{244,5},{245,6},{246,7},{2... | collective-permute-start | bytes 221192 | tf_op jit(solution)/shard_map/ppermute | solution.py:434
  65.4 2.1 %collective-permute-start.9 = (bf16[352,128]{1,0:T(8,128)(2,1)S(1)}, bf16[352,128]{1,0:T(8,128)(2,1)S(1)}, u32[]{:S(2)}, u32[]{:S(2)}) collective-permute-start(bf16[352,128]{1,0:T(8,128)(2,1)S(1)} %get-tuple-element.45.own_ref), channel_id=1, source_target_pairs={{0,4},{1,5},{2,6},{3,7},{4,0},{5,1},{6,2},{7,3},{8,12},{9,13},{10,... | collective-permute-start | bytes 270344 | tf_op jit(solution)/shard_map/ppermute | solution.py:466
  67.5 3.2 %collective-permute-done.4.beside_ref = bf16[2,2,6,8,192]{4,3,2,1,0:T(8,128)(2,1)S(1)} collective-permute-done((bf16[2,2,6,8,192]{4,3,2,1,0:T(8,128)(2,1)S(1)}, bf16[2,2,6,8,192]{4,3,2,1,0:T(8,128)(2,1)S(1)}, u32[]{:S(2)}, u32[]{:S(2)}) %collective-permute-start.4) | collective-permute-done | bytes 73760 | tf_op jit(solution)/shard_map/ppermute | solution.py:434
  70.7 1.7 %collective-permute-done.5.corner_ref = bf16[2,2,6,8,192]{4,3,2,1,0:T(8,128)(2,1)S(1)} collective-permute-done((bf16[2,2,6,8,192]{4,3,2,1,0:T(8,128)(2,1)S(1)}, bf16[2,2,6,8,192]{4,3,2,1,0:T(8,128)(2,1)S(1)}, u32[]{:S(2)}, u32[]{:S(2)}) %collective-permute-start.5) | collective-permute-done | bytes 73760 | tf_op jit(solution)/shard_map/ppermute | solution.py:434
  72.8 0.8 shard_map.168
  73.6 6.3 %all-to-all-start.2 = ((bf16[16,112,128]{2,1,0:T(8,128)(2,1)}), bf16[16,112,128]{2,1,0:T(8,128)(2,1)S(1)}, u32[]{:S(2)}, u32[]{:S(2)}) async-start(bf16[16,112,128]{2,1,0:T(8,128)(2,1)} %get-tuple-element.46), calls=%async_computation.2 | async-start | bytes 917504 | tf_op jit(solution)/shard_map/all_to_all | solution.py:481
  79.9 3.2 %collective-permute-start.10 = (bf16[352,128]{1,0:T(8,128)(2,1)S(1)}, bf16[352,128]{1,0:T(8,128)(2,1)S(1)}, u32[]{:S(2)}, u32[]{:S(2)}) collective-permute-start(bf16[352,128]{1,0:T(8,128)(2,1)S(1)} %get-tuple-element.47), channel_id=1, source_target_pairs={{0,8},{1,9},{2,10},{3,11},{4,12},{5,13},{6,14},{7,15},{8,0},{9,1},... | collective-permute-start | bytes 270344 | tf_op jit(solution)/shard_map/ppermute | solution.py:466
  83.1 4.2 %collective-permute-done.10 = bf16[352,128]{1,0:T(8,128)(2,1)S(1)} collective-permute-done((bf16[352,128]{1,0:T(8,128)(2,1)S(1)}, bf16[352,128]{1,0:T(8,128)(2,1)S(1)}, u32[]{:S(2)}, u32[]{:S(2)}) %collective-permute-start.10) | collective-permute-done | bytes 90144 | tf_op jit(solution)/shard_map/ppermute | solution.py:466
  87.4 2.6 %all-to-all-done.2 = bf16[16,112,128]{2,1,0:T(8,128)(2,1)S(1)} async-done(((bf16[16,112,128]{2,1,0:T(8,128)(2,1)}), bf16[16,112,128]{2,1,0:T(8,128)(2,1)S(1)}, u32[]{:S(2)}, u32[]{:S(2)}) %all-to-all-start.2) | async-done | bytes 458784 | tf_op jit(solution)/shard_map/all_to_all | solution.py:481
  90.0 1.6 %collective-permute-start.11 = (bf16[16,112,128]{2,1,0:T(8,128)(2,1)S(1)}, bf16[16,112,128]{2,1,0:T(8,128)(2,1)S(1)}, u32[]{:S(2)}, u32[]{:S(2)}) collective-permute-start(bf16[16,112,128]{2,1,0:T(8,128)(2,1)S(1)} %fusion.1), channel_id=1, source_target_pairs={{0,16},{16,0},{32,48},{48,32},{64,80},{80,64},{96,112},{112,96},{1... | collective-permute-start | bytes 1376264 | tf_op jit(solution)/shard_map/ppermute | solution.py:483
  91.6 0.9 shard_map.166
  93.1 2.1 %shard_map.169 = (f32[192,576]{1,0:T(8,128)}, f32[192,192]{1,0:T(8,128)}, f32[192,768]{1,0:T(8,128)}, f32[192,768]{1,0:T(8,128)}, f32[1,1,6,24,552]{4,3,2,1,0:T(8,128)}) custom-call(s32[1]{0:T(128)} %bitcast.core_ref, bf16[1792,128]{1,0:T(8,128)(2,1)S(1)} %bitcast.13, bf16[1792,128]{1,0:T(8,128)(2,1)S(1)} %bitcast.14, ...), custom_call_target="tpu_custom_call" | custom-call | tf_op jit(solution)/shard_map/pallas_call | solution.py:528
  (37 shorter events, 1.4 us)
Async XLA Ops:
  0.6 1.0 %copy-start = (bf16[2,12,24,192]{3,2,1,0:T(8,128)(2,1)S(1)}, bf16[2,12,24,192]{3,2,1,0:T(8,128)(2,1)}, u32[]{:S(2)}) copy-start(bf16[2,12,24,192]{3,2,1,0:T(8,128)(2,1)} %tokens_ref.3) | copy-start | bytes 663556
  1.6 1.0 %copy-start.2 = (bf16[2,12,24,192]{3,2,1,0:T(8,128)(2,1)S(1)}, bf16[2,12,24,192]{3,2,1,0:T(8,128)(2,1)}, u32[]{:S(2)}) copy-start(bf16[2,12,24,192]{3,2,1,0:T(8,128)(2,1)} %cots_ref.1) | copy-start | bytes 663556
  2.6 13.7 %copy-start.7 = (bf16[2,552,384]{2,1,0:T(8,128)(2,1)S(1)}, bf16[2,552,384]{2,1,0:T(8,128)(2,1)}, u32[]{:S(2)}) copy-start(bf16[2,552,384]{2,1,0:T(8,128)(2,1)} %constant.31.clone.order_ref) | copy-start | bytes 2543620
  3.2 16.2 %collective-permute-start.1 = (bf16[2,2,6,8,192]{4,3,2,1,0:T(8,128)(2,1)}, bf16[2,2,6,8,192]{4,3,2,1,0:T(8,128)(2,1)S(1)}, u32[]{:S(2)}, u32[]{:S(2)}) collective-permute-start(bf16[2,2,6,8,192]{4,3,2,1,0:T(8,128)(2,1)} %get-tuple-element.31), channel_id=1, source_target_pairs={{1,0},{2,1},{3,2},{4,3},{5,4},{6,5},{7,6},{8,7},{9,8},{10,9},{11,1... | collective-permute-start | bytes 221192 | tf_op jit(solution)/shard_map/ppermute | solution.py:434
  10.7 8.8 %collective-permute-start.2 = (bf16[2,2,6,8,192]{4,3,2,1,0:T(8,128)(2,1)S(1)}, bf16[2,2,6,8,192]{4,3,2,1,0:T(8,128)(2,1)S(1)}, u32[]{:S(2)}, u32[]{:S(2)}) collective-permute-start(bf16[2,2,6,8,192]{4,3,2,1,0:T(8,128)(2,1)S(1)} %get-tuple-element.32), channel_id=1, source_target_pairs={{17,0},{18,1},{19,2},{20,3},{21,4},{22,5},{23,6},{24,7},{25,8},{26... | collective-permute-start | bytes 221192 | tf_op jit(solution)/shard_map/ppermute | solution.py:434
  11.7 7.8 %copy-start.1 = (bf16[2,12,24,192]{3,2,1,0:T(8,128)(2,1)S(1)}, bf16[2,12,24,192]{3,2,1,0:T(8,128)(2,1)}, u32[]{:S(2)}) copy-start(bf16[2,12,24,192]{3,2,1,0:T(8,128)(2,1)} %tokens_ref.3) | copy-start | bytes 663556
  11.7 7.8 %copy-start.3 = (bf16[2,12,24,192]{3,2,1,0:T(8,128)(2,1)S(1)}, bf16[2,12,24,192]{3,2,1,0:T(8,128)(2,1)}, u32[]{:S(2)}) copy-start(bf16[2,12,24,192]{3,2,1,0:T(8,128)(2,1)} %cots_ref.1) | copy-start | bytes 663556
  11.7 7.8 %copy-start.6 = (bf16[576,768]{1,0:T(8,128)(2,1)S(1)}, bf16[576,768]{1,0:T(8,128)(2,1)}, u32[]{:S(2)}) copy-start(bf16[576,768]{1,0:T(8,128)(2,1)} %constant.32.clone.order_ref) | copy-start | bytes 2654212
  11.7 7.8 %collective-permute-start = (bf16[2,2,6,24,192]{4,3,2,1,0:T(8,128)(2,1)S(1)}, bf16[2,2,6,24,192]{4,3,2,1,0:T(8,128)(2,1)S(1)}, u32[]{:S(2)}, u32[]{:S(2)}) collective-permute-start(bf16[2,2,6,24,192]{4,3,2,1,0:T(8,128)(2,1)S(1)} %get-tuple-element.30), channel_id=1, source_target_pairs={{16,0},{32,16},{48,32},{64,48},{80,64},{96,80},{112,96},{128,112},... | collective-permute-start | bytes 663560 | tf_op jit(solution)/shard_map/ppermute | solution.py:434
  16.3 1.0 %copy-start.8 = (f32[1,1,6,24,552]{4,3,2,1,0:T(8,128)S(1)}, f32[1,1,6,24,552]{4,3,2,1,0:T(8,128)}, u32[]{:S(2)}) copy-start(f32[1,1,6,24,552]{4,3,2,1,0:T(8,128)} %table_ref.1) | copy-start | bytes 953860
  17.3 2.2 %copy-start.9 = (bf16[192,768]{1,0:T(8,128)(2,1)S(1)}, bf16[192,768]{1,0:T(8,128)(2,1)}, u32[]{:S(2)}) copy-start(bf16[192,768]{1,0:T(8,128)(2,1)} %up_ref.1) | copy-start | bytes 884740
  17.3 2.2 %copy-start.10 = (bf16[768,192]{0,1:T(8,128)(2,1)S(1)}, bf16[768,192]{0,1:T(8,128)(2,1)}, u32[]{:S(2)}) copy-start(bf16[768,192]{0,1:T(8,128)(2,1)} %param.15) | copy-start | bytes 884740
  17.3 2.2 %copy-start.11 = (bf16[192,192]{1,0:T(8,128)(2,1)S(1)}, bf16[192,192]{1,0:T(8,128)(2,1)}, u32[]{:S(2)}) copy-start(bf16[192,192]{1,0:T(8,128)(2,1)} %proj_ref.1) | copy-start | bytes 221188
  31.3 17.4 %copy-start.5 = (bf16[768,576]{1,0:T(8,128)(2,1)S(1)}, bf16[768,576]{1,0:T(8,128)(2,1)}, u32[]{:S(2)}) copy-start(bf16[768,576]{1,0:T(8,128)(2,1)} %constant.33.clone.order_ref) | copy-start | bytes 2654212
  31.3 3.6 %collective-permute-start.6 = (bf16[1792,128]{1,0:T(8,128)(2,1)S(1)}, bf16[1792,128]{1,0:T(8,128)(2,1)S(1)}, u32[]{:S(2)}, u32[]{:S(2)}) collective-permute-start(bf16[1792,128]{1,0:T(8,128)(2,1)S(1)} %get-tuple-element.42), channel_id=1, source_target_pairs={{0,16},{16,0},{32,48},{48,32},{64,80},{80,64},{96,112},{112,96},{1... | collective-permute-start | bytes 1376264 | tf_op jit(solution)/shard_map/ppermute | solution.py:472
  35.8 19.0 %all-to-all-start = ((bf16[16,112,128]{2,1,0:T(8,128)(2,1)}), bf16[16,112,128]{2,1,0:T(8,128)(2,1)S(1)}, u32[]{:S(2)}, u32[]{:S(2)}) async-start(bf16[16,112,128]{2,1,0:T(8,128)(2,1)} %bitcast.3), calls=%async_computation | async-start | bytes 917504 | tf_op jit(solution)/shard_map/all_to_all | solution.py:474
  42.6 6.0 %collective-permute-start.7 = (bf16[352,128]{1,0:T(8,128)(2,1)S(1)}, bf16[352,128]{1,0:T(8,128)(2,1)S(1)}, u32[]{:S(2)}, u32[]{:S(2)}) collective-permute-start(bf16[352,128]{1,0:T(8,128)(2,1)S(1)} %get-tuple-element.43), channel_id=1, source_target_pairs={{0,1},{1,0},{2,3},{3,2},{4,5},{5,4},{6,7},{7,6},{8,9},{9,8},{10,11... | collective-permute-start | bytes 270344 | tf_op jit(solution)/shard_map/ppermute | solution.py:466
  48.7 6.1 %collective-permute-start.8 = (bf16[352,128]{1,0:T(8,128)(2,1)S(1)}, bf16[352,128]{1,0:T(8,128)(2,1)S(1)}, u32[]{:S(2)}, u32[]{:S(2)}) collective-permute-start(bf16[352,128]{1,0:T(8,128)(2,1)S(1)} %add_convert_fusion.2.own_ref), channel_id=1, source_target_pairs={{0,2},{1,3},{2,0},{3,1},{4,6},{5,7},{6,4},{7,5},{8,10},{9,11},{10,... | collective-permute-start | bytes 270344 | tf_op jit(solution)/shard_map/ppermute | solution.py:466
  49.6 43.5 %copy-start.4 = (bf16[2,384,552]{2,1,0:T(8,128)(2,1)S(1)}, bf16[2,384,552]{2,1,0:T(8,128)(2,1)}, u32[]{:S(2)}) copy-start(bf16[2,384,552]{2,1,0:T(8,128)(2,1)} %constant.34.clone.back_ref) | copy-start | bytes 2543620
  49.6 22.9 %collective-permute-start.3 = (bf16[2,2,6,24,192]{4,3,2,1,0:T(8,128)(2,1)S(1)}, bf16[2,2,6,24,192]{4,3,2,1,0:T(8,128)(2,1)S(1)}, u32[]{:S(2)}, u32[]{:S(2)}) collective-permute-start(bf16[2,2,6,24,192]{4,3,2,1,0:T(8,128)(2,1)S(1)} %get-tuple-element.36), channel_id=1, source_target_pairs={{240,0},{0,16},{16,32},{32,48},{48,64},{64,80},{80,96},{96,112},{1... | collective-permute-start | bytes 663560 | tf_op jit(solution)/shard_map/ppermute | solution.py:434
  55.5 17.2 %all-to-all-start.1 = ((bf16[8,112,128]{2,1,0:T(8,128)(2,1)}), bf16[8,112,128]{2,1,0:T(8,128)(2,1)S(1)}, u32[]{:S(2)}, u32[]{:S(2)}) async-start(bf16[8,112,128]{2,1,0:T(8,128)(2,1)} %get-tuple-element.44), calls=%async_computation.1 | async-start | bytes 458752 | tf_op jit(solution)/shard_map/all_to_all | solution.py:477
  59.9 10.8 %collective-permute-start.4 = (bf16[2,2,6,8,192]{4,3,2,1,0:T(8,128)(2,1)S(1)}, bf16[2,2,6,8,192]{4,3,2,1,0:T(8,128)(2,1)S(1)}, u32[]{:S(2)}, u32[]{:S(2)}) collective-permute-start(bf16[2,2,6,8,192]{4,3,2,1,0:T(8,128)(2,1)S(1)} %get-tuple-element.37), channel_id=1, source_target_pairs={{15,0},{0,1},{1,2},{2,3},{3,4},{4,5},{5,6},{6,7},{7,8},{8,9},{9,10... | collective-permute-start | bytes 221192 | tf_op jit(solution)/shard_map/ppermute | solution.py:434
  60.1 12.3 %collective-permute-start.5 = (bf16[2,2,6,8,192]{4,3,2,1,0:T(8,128)(2,1)S(1)}, bf16[2,2,6,8,192]{4,3,2,1,0:T(8,128)(2,1)S(1)}, u32[]{:S(2)}, u32[]{:S(2)}) collective-permute-start(bf16[2,2,6,8,192]{4,3,2,1,0:T(8,128)(2,1)S(1)} %get-tuple-element.38), channel_id=1, source_target_pairs={{255,0},{240,1},{241,2},{242,3},{243,4},{244,5},{245,6},{246,7},{2... | collective-permute-start | bytes 221192 | tf_op jit(solution)/shard_map/ppermute | solution.py:434
  65.4 7.4 %collective-permute-start.9 = (bf16[352,128]{1,0:T(8,128)(2,1)S(1)}, bf16[352,128]{1,0:T(8,128)(2,1)S(1)}, u32[]{:S(2)}, u32[]{:S(2)}) collective-permute-start(bf16[352,128]{1,0:T(8,128)(2,1)S(1)} %get-tuple-element.45.own_ref), channel_id=1, source_target_pairs={{0,4},{1,5},{2,6},{3,7},{4,0},{5,1},{6,2},{7,3},{8,12},{9,13},{10,... | collective-permute-start | bytes 270344 | tf_op jit(solution)/shard_map/ppermute | solution.py:466
  73.6 16.4 %all-to-all-start.2 = ((bf16[16,112,128]{2,1,0:T(8,128)(2,1)}), bf16[16,112,128]{2,1,0:T(8,128)(2,1)S(1)}, u32[]{:S(2)}, u32[]{:S(2)}) async-start(bf16[16,112,128]{2,1,0:T(8,128)(2,1)} %get-tuple-element.46), calls=%async_computation.2 | async-start | bytes 917504 | tf_op jit(solution)/shard_map/all_to_all | solution.py:481
  79.9 7.5 %collective-permute-start.10 = (bf16[352,128]{1,0:T(8,128)(2,1)S(1)}, bf16[352,128]{1,0:T(8,128)(2,1)S(1)}, u32[]{:S(2)}, u32[]{:S(2)}) collective-permute-start(bf16[352,128]{1,0:T(8,128)(2,1)S(1)} %get-tuple-element.47), channel_id=1, source_target_pairs={{0,8},{1,9},{2,10},{3,11},{4,12},{5,13},{6,14},{7,15},{8,0},{9,1},... | collective-permute-start | bytes 270344 | tf_op jit(solution)/shard_map/ppermute | solution.py:466
  90.0 3.1 %collective-permute-start.11 = (bf16[16,112,128]{2,1,0:T(8,128)(2,1)S(1)}, bf16[16,112,128]{2,1,0:T(8,128)(2,1)S(1)}, u32[]{:S(2)}, u32[]{:S(2)}) collective-permute-start(bf16[16,112,128]{2,1,0:T(8,128)(2,1)S(1)} %fusion.1), channel_id=1, source_target_pairs={{0,16},{16,0},{32,48},{48,32},{64,80},{80,64},{96,112},{112,96},{1... | collective-permute-start | bytes 1376264 | tf_op jit(solution)/shard_map/ppermute | solution.py:483

commit v4 on v3

--- a/solution.py
+++ b/solution.py
@@ -118,8 +118,8 @@
     split = (row_i >= HALF) != (row_j >= HALF)
     split = jnp.logical_and(split, last_ref[0] == 1)
     for level in range(2):
-        order = order_ref[level]
-        wide = dot(high, order) + (dot(middle, order) + dot(low, order))
+        own = slice(level * CUT, (level + 1) * CUT)
+        wide = sum(dot(term[:, own], order_ref[...]) for term in (low, middle, high))
         for head in range(HEADS):
             both = wide[head * 2 * WA : (head + 1) * 2 * WA]
             other = pltpu.roll(both, WA, 0)
@@ -136,7 +136,7 @@
 
 def block_kernel(
     core_ref, tokens_ref, cots_ref, below_ref, beside_ref, corner_ref, order_ref,
-    wq_ref, wk_ref, wv_ref, proj_ref, up_ref, down_ref, bias_ref,
+    qkv_ref, proj_ref, up_ref, down_ref, bias_ref,
     result_ref, gtok_ref, mine_ref, other_ref, gbias_ref,
     source_ref, x_ref, cot_ref, bsum_ref, normed_ref, q_ref, k_ref, v_ref, prob_ref, att_ref, res_ref, two_ref, upper_ref, gact_ref, act_ref,
     gup_ref, gres_ref, gmix_ref, gatt_ref, dq_ref, dk_ref, dv_ref, ds_ref, pad_ref, turned_ref,
@@ -173,9 +173,9 @@
 
     lax.fori_loop(0, PARTS, first_norm, 0, unroll=4)
     normed = normed_ref[...]
-    q_ref[...] = dot(normed, wq_ref[...]).astype(BF)
-    k_ref[...] = dot(normed, wk_ref[...]).astype(BF)
-    v_ref[...] = dot(normed, wv_ref[...]).astype(BF)
+    weights = [qkv_ref[:, part * C : (part + 1) * C] for part in range(3)]
+    for target, weight in zip((q_ref, k_ref, v_ref), weights):
+        target[...] = dot(normed, weight).astype(BF)
 
     def attend(part, carry):
         rows = rows_of(part)
@@ -269,9 +269,7 @@
         return carry
 
     lax.fori_loop(0, PARTS, attend_back, 0, unroll=4)
-    normed_grad = dot_rt(dq_ref[...], wq_ref[...])
-    normed_grad = normed_grad + dot_rt(dk_ref[...], wk_ref[...])
-    res_ref[...] = normed_grad + dot_rt(dv_ref[...], wv_ref[...])
+    res_ref[...] = sum(dot_rt(ref[...], weight) for ref, weight in zip((dq_ref, dk_ref, dv_ref), weights))
 
     def first_back(part, carry):
         rows = rows_of(part)
@@ -335,6 +333,11 @@
     return (one.astype(F32) + two.astype(F32)).astype(BF)
 
 
+def first_kernel(mine_ref, got_ref, own_ref, came_ref, sum_ref, bias_ref):
+    sum_ref[...] = (mine_ref[...] + got_ref[...].astype(F32)).astype(BF)
+    bias_ref[...] = added(own_ref[...], came_ref[...])
+
+
 def middle_kernel(got_ref, own_ref, came_ref, wait_ref, wide_ref, bias_ref):
     total = jnp.sum(got_ref[...].astype(F32), axis=0).astype(BF)
     for block in range(wide_ref.shape[0]):
@@ -469,17 +472,17 @@
         outs = [shape(blocks, share, LANES, kind=BF), shape(2 * BIAS_ROWS, LANES, kind=BF)]
         return call(middle_kernel, outs, 0, 4)(got, own, came, wait)
 
-    mine = mine + lax.ppermute(other, "lat", pairs).astype(F32)
-    mine = mine.astype(BF).reshape(lat, share, LANES)
-    got = lax.all_to_all(mine, ("lat", "lon"), 0, 0, axis_index_groups=planes)
-    bias = added(bias, partner(bias, 1))
-    wide, bias = middle(got, bias, partner(bias, 2), depth, bias[:8])
+    own, above, beside, corner = pieces
+    outs = [shape(PACKED, LANES, kind=BF), shape(2 * BIAS_ROWS, LANES, kind=BF)]
+    mine, bias = call(first_kernel, outs, 0, 4)(mine, lax.ppermute(other, "lat", pairs), bias, partner(bias, 1))
+    got = lax.all_to_all(mine.reshape(lat, share, LANES), ("lat", "lon"), 0, 0, axis_index_groups=planes)
+    wide, bias = middle(got, bias, partner(bias, 2), depth, beside[0, 0, 0])
     got = lax.all_to_all(wide, "lon", 0, 0, axis_index_groups=columns)
-    wait = functools.reduce(added, [piece[0, 0, 0, :8] for piece in pieces[1:]])
-    wide, bias = middle(got, bias, partner(bias, 4), lat, wait)
+    wide, bias = middle(got, bias, partner(bias, 4), lat, above[0, 0, 0, :8])
     bias = added(bias, partner(bias, 8))
     mine = lax.all_to_all(wide, ("lat", "lon"), 0, 0, axis_index_groups=planes)
-    mine = lax.dynamic_update_slice(mine, bias[None, :16], (lat - 1, share - 16, 0))
+    wait = added(bias[:8], corner[0, 0, 0, :, :LANES])
+    mine = lax.dynamic_update_slice(mine, wait[None], (lat - 1, share - 8, 0))
     other = lax.ppermute(mine, "lat", pairs)
     return mine.reshape(PACKED, LANES), other.reshape(PACKED, LANES), bias
 
@@ -496,7 +499,7 @@
     corner = from_next(corner, ["lat", "lon"], 1)
     beside = from_next(beside, ["lon"], 1)
     back = table_back()
-    order = jnp.asarray(back.transpose(0, 2, 1), BF)
+    order = jnp.asarray(table_order(), BF)
     bias = call(bias_kernel, [shape(2, HEADS * WIN, WIN)], 1, 2)(last, earth_bias, order)[0]
 
     def tokens_of(width, kind=BF):
@@ -515,9 +518,9 @@
     scratch += [tokens_of(C)] * 5 + [pltpu.VMEM((2, HEADS * WIN, WIN), F32)]
     scratch += [pltpu.VMEM((2 * HEADS, WIN, WIDE), F32), pltpu.VMEM((C, WIN), F32)]
     scratch += [tokens_of(C, F32)] * 5
-    result, grad_tokens, *grads = call(block_kernel, outs, 1, 13, scratch, limit=LARGE)(
+    result, grad_tokens, *grads = call(block_kernel, outs, 1, 11, scratch, limit=LARGE)(
         core, tokens, cotangent, below, beside, corner, jnp.asarray(window_order(), BF),
-        w_qkv[:, :C], w_qkv[:, C : 2 * C], w_qkv[:, 2 * C :], w_proj, w_up, w_down.T, bias,
+        w_qkv, w_proj, w_up, w_down.T, bias,
     )
     pieces = roll_back_start(result, grad_tokens)
     sums = gradient_sums(*grads, pieces)

time: 95.6 us -> 95.9 us (level)
  starting transfers between devices: 50.5 us -> 51.8 us
    ppermute x1, starting transfers between devices: 1.63 us -> 6.2 us  [gradient_sums(): other = lax.ppermute(mine, 'lat', pairs)]
    all_to_all x1, starting transfers between devices: 6.82 us -> 3.56 us  [gradient_sums(): lax.all_to_all(mine.reshape(lat, share, LANES), ('lat', 'lon'), 0, 0, axi...]
    all_to_all x1, waiting for transfers between devices: 2.62 us -> 0.01 us  [gradient_sums(): mine = lax.all_to_all(wide, ('lat', 'lon'), 0, 0, axis_index_groups=planes)]
    ppermute x1, starting transfers between devices: 2.11 us -> 0.09 us  [gradient_sums(): lax.ppermute(other, 'lat', pairs)]
    all_to_all x1, waiting for transfers between devices: 0.01 us -> 1.86 us  [gradient_sums(): got = lax.all_to_all(wide, 'lon', 0, 0, axis_index_groups=columns)]
    ppermute x4, starting transfers between devices: 6.77 us -> 8.5 us  [partner(): return lax.ppermute(block, 'lon', [(i, i ^ distance) for i in range(lon)])]
    ppermute x6, starting transfers between devices: 22.6 us -> 21.2 us  [from_next(): return lax.ppermute(block, tuple(axes), route)]
    ppermute x1, waiting for transfers between devices: 1.44 us -> 0.01 us  [gradient_sums(): lax.ppermute(other, 'lat', pairs)]
  transfers between devices with their start and end apart: 15 -> 15, of which waited for: 8 -> 8; matrix products, arithmetic and copies ran while one was open for 1% -> 0% of each run, Pallas kernels for 5% -> 5%
where the time goes in v4:
time: 95.9 us; the launch traced here: 95.4 us
  starting transfers between devices  51.8 us (54%)
  Pallas kernels  20.8 us (22%)
  waiting for transfers between devices  18.1 us (19%)
  local copies, waits for them, and re-layouts  3.88 us (4%)
    ppermute x6, starting transfers between devices, from_next(): return lax.ppermute(block, tuple(axes), route)  21.2 us
    pallas_call x1, Pallas kernels, on_device(): call(block_kernel, outs, 1, 11, scratch, limit=LARGE)  11.8 us
    ppermute x4, waiting for transfers between devices, partner(): return lax.ppermute(block, 'lon', [(i, i ^ distance) for i in range(lon)])  8.91 us
    ppermute x4, starting transfers between devices, partner(): return lax.ppermute(block, 'lon', [(i, i ^ distance) for i in range(lon)])  8.5 us
    all_to_all x1, starting transfers between devices, gradient_sums(): mine = lax.all_to_all(wide, ('lat', 'lon'), 0, 0, axis_index_groups=planes)  6.78 us
    ppermute x6, waiting for transfers between devices, from_next(): return lax.ppermute(block, tuple(axes), route)  6.24 us
    ppermute x1, starting transfers between devices, gradient_sums(): other = lax.ppermute(mine, 'lat', pairs)  6.2 us
    all_to_all x1, starting transfers between devices, gradient_sums(): got = lax.all_to_all(wide, 'lon', 0, 0, axis_index_groups=columns)  5.5 us
  transfers between devices with their start and end apart: 15, of which 8 were waited for; matrix products, arithmetic and copies ran while one was open for 0% of the time, Pallas kernels for 5%

profile of v4, /device:TPU:1, one launch (start us, length us, event | category | flops | bytes accessed | tf_op | source)
XLA Modules:
  0.0 95.4 jit_solution(6483290592894020765)
XLA Ops:
  0.6 1.0 copy-done
  1.6 1.0 %copy-done.2 = bf16[2,12,24,192]{3,2,1,0:T(8,128)(2,1)S(1)} copy-done((bf16[2,12,24,192]{3,2,1,0:T(8,128)(2,1)S(1)}, bf16[2,12,24,192]{3,2,1,0:T(8,128)(2,1)}, u32[]{:S(2)}) %copy-start.2) | copy-done | bytes 221208
  2.6 3.3 %collective-permute-start = (bf16[2,2,6,24,192]{4,3,2,1,0:T(8,128)(2,1)S(1)}, bf16[2,2,6,24,192]{4,3,2,1,0:T(8,128)(2,1)S(1)}, u32[]{:S(2)}, u32[]{:S(2)}) collective-permute-start(bf16[2,2,6,24,192]{4,3,2,1,0:T(8,128)(2,1)S(1)} %get-tuple-element.32), channel_id=1, source_target_pairs={{16,0},{32,16},{48,32},{64,48},{80,64},{96,80},{112,96},{128,112},... | collective-permute-start | bytes 663560 | tf_op jit(solution)/shard_map/ppermute | solution.py:437
  5.9 4.9 %collective-permute-start.1 = (bf16[2,2,6,8,192]{4,3,2,1,0:T(8,128)(2,1)S(1)}, bf16[2,2,6,8,192]{4,3,2,1,0:T(8,128)(2,1)S(1)}, u32[]{:S(2)}, u32[]{:S(2)}) collective-permute-start(bf16[2,2,6,8,192]{4,3,2,1,0:T(8,128)(2,1)S(1)} %get-tuple-element.33), channel_id=1, source_target_pairs={{1,0},{2,1},{3,2},{4,3},{5,4},{6,5},{7,6},{8,7},{9,8},{10,9},{11,1... | collective-permute-start | bytes 221192 | tf_op jit(solution)/shard_map/ppermute | solution.py:437
  10.8 5.2 %collective-permute-start.2 = (bf16[2,2,6,8,192]{4,3,2,1,0:T(8,128)(2,1)S(1)}, bf16[2,2,6,8,192]{4,3,2,1,0:T(8,128)(2,1)S(1)}, u32[]{:S(2)}, u32[]{:S(2)}) collective-permute-start(bf16[2,2,6,8,192]{4,3,2,1,0:T(8,128)(2,1)S(1)} %get-tuple-element.34), channel_id=1, source_target_pairs={{17,0},{18,1},{19,2},{20,3},{21,4},{22,5},{23,6},{24,7},{25,8},{26... | collective-permute-start | bytes 221192 | tf_op jit(solution)/shard_map/ppermute | solution.py:437
  15.9 1.0 %copy-done.7 = f32[1,1,6,24,552]{4,3,2,1,0:T(8,128)S(1)} copy-done((f32[1,1,6,24,552]{4,3,2,1,0:T(8,128)S(1)}, f32[1,1,6,24,552]{4,3,2,1,0:T(8,128)}, u32[]{:S(2)}) %copy-start.7) | copy-done | bytes 317976
  16.9 0.9 copy-done.11
  17.9 2.8 %shard_map.163.bias_ref = f32[2,864,144]{2,1,0:T(8,128)S(1)} custom-call(s32[1]{0:T(128)} %bitcast.2.last_ref, f32[1,1,6,24,552]{4,3,2,1,0:T(8,128)S(1)} %copy-done.7, bf16[276,384]{1,0:T(8,128)(2,1)S(1)} %copy-done.11), custom_call_target="tpu_custom_call" | custom-call | tf_op jit(solution)/shard_map/pallas_call | solution.py:503
  20.8 11.8 %shard_map.164 = (bf16[576,192]{1,0:T(8,128)(2,1)S(1)}, bf16[576,192]{1,0:T(8,128)(2,1)S(1)}, f32[1792,128]{1,0:T(8,128)S(1)}, bf16[1792,128]{1,0:T(8,128)(2,1)S(1)}, bf16[352,128]{1,0:T(8,128)(2,1)S(1)}) custom-call(s32[1]{0:T(128)} %bitcast.core_ref, bf16[2,12,24,192]{3,2,1,0:T(8,128)(2,1)S(1)} %copy-done.1, bf16[2,12,24,192]{3,2,1,0:T(8,128)(2,1)S(1)} %copy-done.3, ...), custom_call_target="tpu_custom_call" | custom-call | tf_op jit(solution)/shard_map/pallas_call | solution.py:521
  32.7 0.7 collective-permute-start.7
  33.4 3.6 %collective-permute-done.7.came_ref = bf16[352,128]{1,0:T(8,128)(2,1)S(1)} collective-permute-done((bf16[352,128]{1,0:T(8,128)(2,1)S(1)}, bf16[352,128]{1,0:T(8,128)(2,1)S(1)}, u32[]{:S(2)}, u32[]{:S(2)}) %collective-permute-start.7) | collective-permute-done | bytes 90144 | tf_op jit(solution)/shard_map/ppermute | solution.py:469
  37.1 0.9 shard_map.167
  37.9 3.6 %all-to-all-start = ((bf16[16,112,128]{2,1,0:T(8,128)(2,1)}), bf16[16,112,128]{2,1,0:T(8,128)(2,1)S(1)}, u32[]{:S(2)}, u32[]{:S(2)}) async-start(bf16[16,112,128]{2,1,0:T(8,128)(2,1)} %bitcast.3), calls=%async_computation | async-start | bytes 917504 | tf_op jit(solution)/shard_map/all_to_all | solution.py:478
  41.5 0.8 shard_map.165
  42.3 1.3 %collective-permute-start.4 = (bf16[2,2,6,8,192]{4,3,2,1,0:T(8,128)(2,1)S(1)}, bf16[2,2,6,8,192]{4,3,2,1,0:T(8,128)(2,1)S(1)}, u32[]{:S(2)}, u32[]{:S(2)}) collective-permute-start(bf16[2,2,6,8,192]{4,3,2,1,0:T(8,128)(2,1)S(1)} %get-tuple-element.39), channel_id=1, source_target_pairs={{15,0},{0,1},{1,2},{2,3},{3,4},{4,5},{5,6},{6,7},{7,8},{8,9},{9,10... | collective-permute-start | bytes 221192 | tf_op jit(solution)/shard_map/ppermute | solution.py:437
  43.6 2.6 %collective-permute-start.3 = (bf16[2,2,6,24,192]{4,3,2,1,0:T(8,128)(2,1)S(1)}, bf16[2,2,6,24,192]{4,3,2,1,0:T(8,128)(2,1)S(1)}, u32[]{:S(2)}, u32[]{:S(2)}) collective-permute-start(bf16[2,2,6,24,192]{4,3,2,1,0:T(8,128)(2,1)S(1)} %get-tuple-element.38), channel_id=1, source_target_pairs={{240,0},{0,16},{16,32},{32,48},{48,64},{64,80},{80,96},{96,112},{1... | collective-permute-start | bytes 663560 | tf_op jit(solution)/shard_map/ppermute | solution.py:437
  46.3 3.7 %collective-permute-done.4.beside_ref = bf16[2,2,6,8,192]{4,3,2,1,0:T(8,128)(2,1)S(1)} collective-permute-done((bf16[2,2,6,8,192]{4,3,2,1,0:T(8,128)(2,1)S(1)}, bf16[2,2,6,8,192]{4,3,2,1,0:T(8,128)(2,1)S(1)}, u32[]{:S(2)}, u32[]{:S(2)}) %collective-permute-start.4) | collective-permute-done | bytes 73760 | tf_op jit(solution)/shard_map/ppermute | solution.py:437
  50.3 0.5 all-to-all-done.got_ref
  50.8 0.8 shard_map.168
  51.5 5.5 %all-to-all-start.1 = ((bf16[8,112,128]{2,1,0:T(8,128)(2,1)}), bf16[8,112,128]{2,1,0:T(8,128)(2,1)S(1)}, u32[]{:S(2)}, u32[]{:S(2)}) async-start(bf16[8,112,128]{2,1,0:T(8,128)(2,1)} %get-tuple-element.48), calls=%async_computation.1 | async-start | bytes 458752 | tf_op jit(solution)/shard_map/all_to_all | solution.py:480
  57.0 2.4 %collective-permute-start.9 = (bf16[352,128]{1,0:T(8,128)(2,1)S(1)}, bf16[352,128]{1,0:T(8,128)(2,1)S(1)}, u32[]{:S(2)}, u32[]{:S(2)}) collective-permute-start(bf16[352,128]{1,0:T(8,128)(2,1)S(1)} %get-tuple-element.49.own_ref), channel_id=1, source_target_pairs={{0,4},{1,5},{2,6},{3,7},{4,0},{5,1},{6,2},{7,3},{8,12},{9,13},{10,... | collective-permute-start | bytes 270344 | tf_op jit(solution)/shard_map/ppermute | solution.py:469
  59.4 4.9 %collective-permute-done.9.came_ref = bf16[352,128]{1,0:T(8,128)(2,1)S(1)} collective-permute-done((bf16[352,128]{1,0:T(8,128)(2,1)S(1)}, bf16[352,128]{1,0:T(8,128)(2,1)S(1)}, u32[]{:S(2)}, u32[]{:S(2)}) %collective-permute-start.9) | collective-permute-done | bytes 90144 | tf_op jit(solution)/shard_map/ppermute | solution.py:469
  64.3 1.9 %all-to-all-done.1.got_ref = bf16[8,112,128]{2,1,0:T(8,128)(2,1)S(1)} async-done(((bf16[8,112,128]{2,1,0:T(8,128)(2,1)}), bf16[8,112,128]{2,1,0:T(8,128)(2,1)S(1)}, u32[]{:S(2)}, u32[]{:S(2)}) %all-to-all-start.1) | async-done | bytes 229408 | tf_op jit(solution)/shard_map/all_to_all | solution.py:480
  66.2 0.8 shard_map.169
  67.0 6.8 %all-to-all-start.2 = ((bf16[16,112,128]{2,1,0:T(8,128)(2,1)}), bf16[16,112,128]{2,1,0:T(8,128)(2,1)S(1)}, u32[]{:S(2)}, u32[]{:S(2)}) async-start(bf16[16,112,128]{2,1,0:T(8,128)(2,1)} %get-tuple-element.50), calls=%async_computation.2 | async-start | bytes 917504 | tf_op jit(solution)/shard_map/all_to_all | solution.py:483
  73.8 5.4 %collective-permute-start.10 = (bf16[352,128]{1,0:T(8,128)(2,1)S(1)}, bf16[352,128]{1,0:T(8,128)(2,1)S(1)}, u32[]{:S(2)}, u32[]{:S(2)}) collective-permute-start(bf16[352,128]{1,0:T(8,128)(2,1)S(1)} %get-tuple-element.51), channel_id=1, source_target_pairs={{0,8},{1,9},{2,10},{3,11},{4,12},{5,13},{6,14},{7,15},{8,0},{9,1},... | collective-permute-start | bytes 270344 | tf_op jit(solution)/shard_map/ppermute | solution.py:469
  79.2 3.9 %collective-permute-start.5 = (bf16[2,2,6,8,192]{4,3,2,1,0:T(8,128)(2,1)S(1)}, bf16[2,2,6,8,192]{4,3,2,1,0:T(8,128)(2,1)S(1)}, u32[]{:S(2)}, u32[]{:S(2)}) collective-permute-start(bf16[2,2,6,8,192]{4,3,2,1,0:T(8,128)(2,1)S(1)} %get-tuple-element.40), channel_id=1, source_target_pairs={{255,0},{240,1},{241,2},{242,3},{243,4},{244,5},{245,6},{246,7},{2... | collective-permute-start | bytes 221192 | tf_op jit(solution)/shard_map/ppermute | solution.py:437
  83.1 2.6 %collective-permute-done.5.corner_ref = bf16[2,2,6,8,192]{4,3,2,1,0:T(8,128)(2,1)S(1)} collective-permute-done((bf16[2,2,6,8,192]{4,3,2,1,0:T(8,128)(2,1)S(1)}, bf16[2,2,6,8,192]{4,3,2,1,0:T(8,128)(2,1)S(1)}, u32[]{:S(2)}, u32[]{:S(2)}) %collective-permute-start.5) | collective-permute-done | bytes 73760 | tf_op jit(solution)/shard_map/ppermute | solution.py:437
  85.7 6.2 %collective-permute-start.11 = (bf16[16,112,128]{2,1,0:T(8,128)(2,1)S(1)}, bf16[16,112,128]{2,1,0:T(8,128)(2,1)S(1)}, u32[]{:S(2)}, u32[]{:S(2)}) collective-permute-start(bf16[16,112,128]{2,1,0:T(8,128)(2,1)S(1)} %fusion.2), channel_id=1, source_target_pairs={{0,16},{16,0},{32,48},{48,32},{64,80},{80,64},{96,112},{112,96},{1... | collective-permute-start | bytes 1376264 | tf_op jit(solution)/shard_map/ppermute | solution.py:486
  91.9 0.9 shard_map.166
  92.7 0.6 collective-permute-done.11
  93.3 2.1 %shard_map.170 = (f32[192,576]{1,0:T(8,128)}, f32[192,192]{1,0:T(8,128)}, f32[192,768]{1,0:T(8,128)}, f32[192,768]{1,0:T(8,128)}, f32[1,1,6,24,552]{4,3,2,1,0:T(8,128)}) custom-call(s32[1]{0:T(128)} %bitcast.core_ref, bf16[1792,128]{1,0:T(8,128)(2,1)S(1)} %bitcast.20, bf16[1792,128]{1,0:T(8,128)(2,1)S(1)} %bitcast.21, ...), custom_call_target="tpu_custom_call" | custom-call | tf_op jit(solution)/shard_map/pallas_call | solution.py:531
  (37 shorter events, 0.6 us)
Async XLA Ops:
  0.6 1.0 %copy-start = (bf16[2,12,24,192]{3,2,1,0:T(8,128)(2,1)S(1)}, bf16[2,12,24,192]{3,2,1,0:T(8,128)(2,1)}, u32[]{:S(2)}) copy-start(bf16[2,12,24,192]{3,2,1,0:T(8,128)(2,1)} %tokens_ref.3) | copy-start | bytes 663556
  1.6 1.0 %copy-start.2 = (bf16[2,12,24,192]{3,2,1,0:T(8,128)(2,1)S(1)}, bf16[2,12,24,192]{3,2,1,0:T(8,128)(2,1)}, u32[]{:S(2)}) copy-start(bf16[2,12,24,192]{3,2,1,0:T(8,128)(2,1)} %cots_ref.1) | copy-start | bytes 663556
  2.6 18.2 %copy-start.1 = (bf16[2,12,24,192]{3,2,1,0:T(8,128)(2,1)S(1)}, bf16[2,12,24,192]{3,2,1,0:T(8,128)(2,1)}, u32[]{:S(2)}) copy-start(bf16[2,12,24,192]{3,2,1,0:T(8,128)(2,1)} %tokens_ref.3) | copy-start | bytes 663556
  2.6 18.2 %copy-start.3 = (bf16[2,12,24,192]{3,2,1,0:T(8,128)(2,1)S(1)}, bf16[2,12,24,192]{3,2,1,0:T(8,128)(2,1)}, u32[]{:S(2)}) copy-start(bf16[2,12,24,192]{3,2,1,0:T(8,128)(2,1)} %cots_ref.1) | copy-start | bytes 663556
  2.6 18.2 %copy-start.6 = (bf16[576,768]{1,0:T(8,128)(2,1)S(1)}, bf16[576,768]{1,0:T(8,128)(2,1)}, u32[]{:S(2)}) copy-start(bf16[576,768]{1,0:T(8,128)(2,1)} %constant.32.clone.order_ref) | copy-start | bytes 2654212
  2.6 18.1 %collective-permute-start = (bf16[2,2,6,24,192]{4,3,2,1,0:T(8,128)(2,1)S(1)}, bf16[2,2,6,24,192]{4,3,2,1,0:T(8,128)(2,1)S(1)}, u32[]{:S(2)}, u32[]{:S(2)}) collective-permute-start(bf16[2,2,6,24,192]{4,3,2,1,0:T(8,128)(2,1)S(1)} %get-tuple-element.32), channel_id=1, source_target_pairs={{16,0},{32,16},{48,32},{64,48},{80,64},{96,80},{112,96},{128,112},... | collective-permute-start | bytes 663560 | tf_op jit(solution)/shard_map/ppermute | solution.py:437
  5.9 14.8 %collective-permute-start.1 = (bf16[2,2,6,8,192]{4,3,2,1,0:T(8,128)(2,1)S(1)}, bf16[2,2,6,8,192]{4,3,2,1,0:T(8,128)(2,1)S(1)}, u32[]{:S(2)}, u32[]{:S(2)}) collective-permute-start(bf16[2,2,6,8,192]{4,3,2,1,0:T(8,128)(2,1)S(1)} %get-tuple-element.33), channel_id=1, source_target_pairs={{1,0},{2,1},{3,2},{4,3},{5,4},{6,5},{7,6},{8,7},{9,8},{10,9},{11,1... | collective-permute-start | bytes 221192 | tf_op jit(solution)/shard_map/ppermute | solution.py:437
  10.8 9.9 %collective-permute-start.2 = (bf16[2,2,6,8,192]{4,3,2,1,0:T(8,128)(2,1)S(1)}, bf16[2,2,6,8,192]{4,3,2,1,0:T(8,128)(2,1)S(1)}, u32[]{:S(2)}, u32[]{:S(2)}) collective-permute-start(bf16[2,2,6,8,192]{4,3,2,1,0:T(8,128)(2,1)S(1)} %get-tuple-element.34), channel_id=1, source_target_pairs={{17,0},{18,1},{19,2},{20,3},{21,4},{22,5},{23,6},{24,7},{25,8},{26... | collective-permute-start | bytes 221192 | tf_op jit(solution)/shard_map/ppermute | solution.py:437
  15.9 1.0 %copy-start.7 = (f32[1,1,6,24,552]{4,3,2,1,0:T(8,128)S(1)}, f32[1,1,6,24,552]{4,3,2,1,0:T(8,128)}, u32[]{:S(2)}) copy-start(f32[1,1,6,24,552]{4,3,2,1,0:T(8,128)} %table_ref.1) | copy-start | bytes 953860
  16.9 0.9 copy-start.11
  17.9 2.9 %copy-start.8 = (bf16[192,768]{1,0:T(8,128)(2,1)S(1)}, bf16[192,768]{1,0:T(8,128)(2,1)}, u32[]{:S(2)}) copy-start(bf16[192,768]{1,0:T(8,128)(2,1)} %up_ref.1) | copy-start | bytes 884740
  17.9 2.9 %copy-start.9 = (bf16[768,192]{0,1:T(8,128)(2,1)S(1)}, bf16[768,192]{0,1:T(8,128)(2,1)}, u32[]{:S(2)}) copy-start(bf16[768,192]{0,1:T(8,128)(2,1)} %param.15) | copy-start | bytes 884740
  17.9 2.9 %copy-start.10 = (bf16[192,576]{1,0:T(8,128)(2,1)S(1)}, bf16[192,576]{1,0:T(8,128)(2,1)}, u32[]{:S(2)}) copy-start(bf16[192,576]{1,0:T(8,128)(2,1)} %qkv_ref.1) | copy-start | bytes 663556
  17.9 2.9 %copy-start.12 = (bf16[192,192]{1,0:T(8,128)(2,1)S(1)}, bf16[192,192]{1,0:T(8,128)(2,1)}, u32[]{:S(2)}) copy-start(bf16[192,192]{1,0:T(8,128)(2,1)} %proj_ref.1) | copy-start | bytes 221188
  32.6 8.9 %copy-start.5 = (bf16[768,576]{1,0:T(8,128)(2,1)S(1)}, bf16[768,576]{1,0:T(8,128)(2,1)}, u32[]{:S(2)}) copy-start(bf16[768,576]{1,0:T(8,128)(2,1)} %constant.33.clone.order_ref) | copy-start | bytes 2654212
  32.6 4.4 %collective-permute-start.6 = (bf16[1792,128]{1,0:T(8,128)(2,1)S(1)}, bf16[1792,128]{1,0:T(8,128)(2,1)S(1)}, u32[]{:S(2)}, u32[]{:S(2)}) collective-permute-start(bf16[1792,128]{1,0:T(8,128)(2,1)S(1)} %get-tuple-element.44), channel_id=1, source_target_pairs={{0,16},{16,0},{32,48},{48,32},{64,80},{80,64},{96,112},{112,96},{1... | collective-permute-start | bytes 1376264 | tf_op jit(solution)/shard_map/ppermute | solution.py:477
  32.7 4.3 %collective-permute-start.7 = (bf16[352,128]{1,0:T(8,128)(2,1)S(1)}, bf16[352,128]{1,0:T(8,128)(2,1)S(1)}, u32[]{:S(2)}, u32[]{:S(2)}) collective-permute-start(bf16[352,128]{1,0:T(8,128)(2,1)S(1)} %get-tuple-element.45.own_ref), channel_id=1, source_target_pairs={{0,1},{1,0},{2,3},{3,2},{4,5},{5,4},{6,7},{7,6},{8,9},{9,8},{10,11... | collective-permute-start | bytes 270344 | tf_op jit(solution)/shard_map/ppermute | solution.py:469
  37.9 12.8 %all-to-all-start = ((bf16[16,112,128]{2,1,0:T(8,128)(2,1)}), bf16[16,112,128]{2,1,0:T(8,128)(2,1)S(1)}, u32[]{:S(2)}, u32[]{:S(2)}) async-start(bf16[16,112,128]{2,1,0:T(8,128)(2,1)} %bitcast.3), calls=%async_computation | async-start | bytes 917504 | tf_op jit(solution)/shard_map/all_to_all | solution.py:478
  42.3 51.0 %copy-start.4 = (bf16[2,384,552]{2,1,0:T(8,128)(2,1)S(1)}, bf16[2,384,552]{2,1,0:T(8,128)(2,1)}, u32[]{:S(2)}) copy-start(bf16[2,384,552]{2,1,0:T(8,128)(2,1)} %constant.34.clone.back_ref) | copy-start | bytes 2543620
  42.3 7.6 %collective-permute-start.4 = (bf16[2,2,6,8,192]{4,3,2,1,0:T(8,128)(2,1)S(1)}, bf16[2,2,6,8,192]{4,3,2,1,0:T(8,128)(2,1)S(1)}, u32[]{:S(2)}, u32[]{:S(2)}) collective-permute-start(bf16[2,2,6,8,192]{4,3,2,1,0:T(8,128)(2,1)S(1)} %get-tuple-element.39), channel_id=1, source_target_pairs={{15,0},{0,1},{1,2},{2,3},{3,4},{4,5},{5,6},{6,7},{7,8},{8,9},{9,10... | collective-permute-start | bytes 221192 | tf_op jit(solution)/shard_map/ppermute | solution.py:437
  43.6 15.8 %collective-permute-start.3 = (bf16[2,2,6,24,192]{4,3,2,1,0:T(8,128)(2,1)S(1)}, bf16[2,2,6,24,192]{4,3,2,1,0:T(8,128)(2,1)S(1)}, u32[]{:S(2)}, u32[]{:S(2)}) collective-permute-start(bf16[2,2,6,24,192]{4,3,2,1,0:T(8,128)(2,1)S(1)} %get-tuple-element.38), channel_id=1, source_target_pairs={{240,0},{0,16},{16,32},{32,48},{48,64},{64,80},{80,96},{96,112},{1... | collective-permute-start | bytes 663560 | tf_op jit(solution)/shard_map/ppermute | solution.py:437
  46.3 4.0 %collective-permute-start.8 = (bf16[352,128]{1,0:T(8,128)(2,1)S(1)}, bf16[352,128]{1,0:T(8,128)(2,1)S(1)}, u32[]{:S(2)}, u32[]{:S(2)}) collective-permute-start(bf16[352,128]{1,0:T(8,128)(2,1)S(1)} %get-tuple-element.47.own_ref), channel_id=1, source_target_pairs={{0,2},{1,3},{2,0},{3,1},{4,6},{5,7},{6,4},{7,5},{8,10},{9,11},{10,... | collective-permute-start | bytes 270344 | tf_op jit(solution)/shard_map/ppermute | solution.py:469
  51.5 14.7 %all-to-all-start.1 = ((bf16[8,112,128]{2,1,0:T(8,128)(2,1)}), bf16[8,112,128]{2,1,0:T(8,128)(2,1)S(1)}, u32[]{:S(2)}, u32[]{:S(2)}) async-start(bf16[8,112,128]{2,1,0:T(8,128)(2,1)} %get-tuple-element.48), calls=%async_computation.1 | async-start | bytes 458752 | tf_op jit(solution)/shard_map/all_to_all | solution.py:480
  57.0 7.3 %collective-permute-start.9 = (bf16[352,128]{1,0:T(8,128)(2,1)S(1)}, bf16[352,128]{1,0:T(8,128)(2,1)S(1)}, u32[]{:S(2)}, u32[]{:S(2)}) collective-permute-start(bf16[352,128]{1,0:T(8,128)(2,1)S(1)} %get-tuple-element.49.own_ref), channel_id=1, source_target_pairs={{0,4},{1,5},{2,6},{3,7},{4,0},{5,1},{6,2},{7,3},{8,12},{9,13},{10,... | collective-permute-start | bytes 270344 | tf_op jit(solution)/shard_map/ppermute | solution.py:469
  67.0 18.7 %all-to-all-start.2 = ((bf16[16,112,128]{2,1,0:T(8,128)(2,1)}), bf16[16,112,128]{2,1,0:T(8,128)(2,1)S(1)}, u32[]{:S(2)}, u32[]{:S(2)}) async-start(bf16[16,112,128]{2,1,0:T(8,128)(2,1)} %get-tuple-element.50), calls=%async_computation.2 | async-start | bytes 917504 | tf_op jit(solution)/shard_map/all_to_all | solution.py:483
  73.8 9.3 %collective-permute-start.10 = (bf16[352,128]{1,0:T(8,128)(2,1)S(1)}, bf16[352,128]{1,0:T(8,128)(2,1)S(1)}, u32[]{:S(2)}, u32[]{:S(2)}) collective-permute-start(bf16[352,128]{1,0:T(8,128)(2,1)S(1)} %get-tuple-element.51), channel_id=1, source_target_pairs={{0,8},{1,9},{2,10},{3,11},{4,12},{5,13},{6,14},{7,15},{8,0},{9,1},... | collective-permute-start | bytes 270344 | tf_op jit(solution)/shard_map/ppermute | solution.py:469
  79.2 6.5 %collective-permute-start.5 = (bf16[2,2,6,8,192]{4,3,2,1,0:T(8,128)(2,1)S(1)}, bf16[2,2,6,8,192]{4,3,2,1,0:T(8,128)(2,1)S(1)}, u32[]{:S(2)}, u32[]{:S(2)}) collective-permute-start(bf16[2,2,6,8,192]{4,3,2,1,0:T(8,128)(2,1)S(1)} %get-tuple-element.40), channel_id=1, source_target_pairs={{255,0},{240,1},{241,2},{242,3},{243,4},{244,5},{245,6},{246,7},{2... | collective-permute-start | bytes 221192 | tf_op jit(solution)/shard_map/ppermute | solution.py:437
  85.7 7.6 %collective-permute-start.11 = (bf16[16,112,128]{2,1,0:T(8,128)(2,1)S(1)}, bf16[16,112,128]{2,1,0:T(8,128)(2,1)S(1)}, u32[]{:S(2)}, u32[]{:S(2)}) collective-permute-start(bf16[16,112,128]{2,1,0:T(8,128)(2,1)S(1)} %fusion.2), channel_id=1, source_target_pairs={{0,16},{16,0},{32,48},{48,32},{64,80},{80,64},{96,112},{112,96},{1... | collective-permute-start | bytes 1376264 | tf_op jit(solution)/shard_map/ppermute | solution.py:486

commit v5 on v4

--- a/solution.py
+++ b/solution.py
@@ -25,6 +25,9 @@
 PARTS = 4
 PACKED = 1792
 SOURCES = 768
+INNER = 2 * WO - HALF
+LONG = 2 * HALF * INNER
+SHORT = 2 * HALF * HALF
 MAIN = HEADS * WA
 BIAS_ROWS = 176
 LEFT = CUT - 2 * LANES
@@ -64,6 +67,28 @@
     return order
 
 
+def piece_row(level, row, column):
+    place, inside = level * HALF + row % HALF, column >= HALF
+    at = place * INNER + column - HALF if inside else 2 * LONG + place * HALF + column
+    return at + (0 if row >= HALF else LONG if inside else SHORT)
+
+
+def split_order():
+    order = np.zeros((TOKENS, TOKENS), np.float32)
+    for window, level, column, row in np.ndindex(2, 2, WO, WA):
+        token = ((window * 2 + level) * WO + column) * WA + row
+        across = (window * WO + column + HALF) % (2 * WO)
+        order[piece_row(1 - level, (row + HALF) % WA, across), token] = 1.0
+    return order
+
+
+def join_order():
+    order = np.zeros((TOKENS, TOKENS), np.float32)
+    for level, row, column in np.ndindex(2, WA, 2 * WO):
+        order[(level * WA + row) * 2 * WO + column, piece_row(level, row, column)] = 1.0
+    return order
+
+
 def dot(a, b):
     return jnp.dot(a, b, preferred_element_type=F32)
 
@@ -106,20 +131,23 @@
                 corner_ref[array, level, row] = ref[level, row].astype(F32)[:8].astype(BF)
 
 
-def bias_kernel(last_ref, table_ref, order_ref, bias_ref):
+def bias_kernel(last_ref, table_ref, bias_ref):
     table = table_ref[0, 0].reshape(HEADS * 2 * WA, 2 * CUT)
     high = table.astype(BF)
     rest = table - high.astype(F32)
     middle = rest.astype(BF)
     low = (rest - middle.astype(F32)).astype(BF)
+    lane = lax.broadcasted_iota(jnp.int32, (1, WIDE), 1)
+    source = jnp.where(lane < CUT, lane % WA * SPAN + SPAN - 1 - lane // WA, -2 * CUT)
+    place = lax.broadcasted_iota(jnp.int32, (2 * CUT, WIDE), 0)
     row = lax.broadcasted_iota(jnp.int32, (2 * WA, WIDE), 0)
     row_i = lax.broadcasted_iota(jnp.int32, (2 * WA, WIN), 0) % WA
     row_j = lax.broadcasted_iota(jnp.int32, (2 * WA, WIN), 1) % WA
     split = (row_i >= HALF) != (row_j >= HALF)
     split = jnp.logical_and(split, last_ref[0] == 1)
     for level in range(2):
-        own = slice(level * CUT, (level + 1) * CUT)
-        wide = sum(dot(term[:, own], order_ref[...]) for term in (low, middle, high))
+        order = (place == source + level * CUT).astype(F32).astype(BF)
+        wide = sum(dot(term, order) for term in (low, middle, high))
         for head in range(HEADS):
             both = wide[head * 2 * WA : (head + 1) * 2 * WA]
             other = pltpu.roll(both, WA, 0)
@@ -137,10 +165,9 @@
 def block_kernel(
     core_ref, tokens_ref, cots_ref, below_ref, beside_ref, corner_ref, order_ref,
     qkv_ref, proj_ref, up_ref, down_ref, bias_ref,
-    result_ref, gtok_ref, mine_ref, other_ref, gbias_ref,
-    source_ref, x_ref, cot_ref, bsum_ref, normed_ref, q_ref, k_ref, v_ref, prob_ref, att_ref, res_ref, two_ref, upper_ref, gact_ref, act_ref,
-    gup_ref, gres_ref, gmix_ref, gatt_ref, dq_ref, dk_ref, dv_ref, ds_ref, pad_ref, turned_ref,
-    unit_ref, inverse_ref, unit_two_ref, inverse_two_ref, mean_ref,
+    mine_ref, other_ref, ds_ref, act_ref, res_ref, gres_ref, dq_ref, dk_ref, dv_ref, unit_ref, inverse_ref,
+    source_ref, x_ref, cot_ref, normed_ref, q_ref, k_ref, v_ref, prob_ref, att_ref, two_ref, upper_ref, gact_ref,
+    gup_ref, gmix_ref, gatt_ref, turned_ref, unit_two_ref, inverse_two_ref, mean_ref,
 ):
     lane = lax.broadcasted_iota(jnp.int32, (1, C), 1) // HEAD
     half_masks = [(lane == head).astype(F32).astype(BF) for head in range(HEADS)]
@@ -224,7 +251,6 @@
         return carry
 
     lax.fori_loop(0, TOKENS // step, gelu, 0)
-    result_ref[...] = (res_ref[...] + dot_rt(act_ref[...], down_ref[...])).astype(BF)
     gres_ref[...] = dot_rt(gup_ref[...], up_ref[...])
 
     def second_back(part, carry):
@@ -239,7 +265,6 @@
     lax.fori_loop(0, PARTS, second_back, 0, unroll=4)
     gatt_ref[...] = dot_rt(gmix_ref[...], proj_ref[...]).astype(BF)
     ds_ref[...] = jnp.zeros(ds_ref.shape, F32)
-    pad_ref[...] = jnp.zeros(pad_ref.shape, F32)
 
     def attend_back(part, carry):
         rows = rows_of(part)
@@ -269,16 +294,6 @@
         return carry
 
     lax.fori_loop(0, PARTS, attend_back, 0, unroll=4)
-    res_ref[...] = sum(dot_rt(ref[...], weight) for ref, weight in zip((dq_ref, dk_ref, dv_ref), weights))
-
-    def first_back(part, carry):
-        rows = rows_of(part)
-        unit, inverse = unit_ref[rows, :], inverse_ref[rows, :]
-        grad = res_ref[rows, :].astype(BF).astype(F32)
-        gtok_ref[rows, :] = (gres_ref[rows, :] + normal_back(unit, inverse, grad)).astype(BF)
-        return carry
-
-    lax.fori_loop(0, PARTS, first_back, 0, unroll=4)
     first = core_ref[0] == 0
 
     def put(start, zero, one):
@@ -302,15 +317,17 @@
     mine_ref[9 * C :, :] = jnp.zeros((PACKED - 9 * C, LANES), F32)
     other_ref[9 * C :, :] = jnp.zeros((PACKED - 9 * C, LANES), BF)
 
+
+def table_kernel(ds_ref, gbias_ref, bsum_ref):
     row = lax.broadcasted_iota(jnp.int32, (2 * WA, WIDE), 0)
 
     def table_grad(level, head):
-        place = level * HEADS + head
-        pad_ref[place, :, :WIN] = jnp.transpose(ds_ref[level, head * WIN : (head + 1) * WIN, :])
+        scores = jnp.transpose(ds_ref[level, head * WIN : (head + 1) * WIN, :])
         total = jnp.zeros((2 * WA, WIDE), F32)
         for pair in range(WO // 2):
             turn = (WO - 2 - 2 * pair) * WA
-            block = pad_ref[place, pair * 2 * WA : (pair + 1) * 2 * WA, :]
+            block = scores[pair * 2 * WA : (pair + 1) * 2 * WA]
+            block = jnp.concatenate([block, jnp.zeros((2 * WA, WIDE - WIN), F32)], axis=1)
             total = total + (pltpu.roll(block, turn, 1) if turn else block)
         total = jnp.where(row < WA, pltpu.roll(total, WA, 1), total)
         return total + pltpu.roll(total, WA, 0)
@@ -333,7 +350,7 @@
     return (one.astype(F32) + two.astype(F32)).astype(BF)
 
 
-def first_kernel(mine_ref, got_ref, own_ref, came_ref, sum_ref, bias_ref):
+def first_kernel(mine_ref, got_ref, own_ref, came_ref, wait_ref, sum_ref, bias_ref):
     sum_ref[...] = (mine_ref[...] + got_ref[...].astype(F32)).astype(BF)
     bias_ref[...] = added(own_ref[...], came_ref[...])
 
@@ -345,29 +362,38 @@
     bias_ref[...] = added(own_ref[...], came_ref[...])
 
 
-def split_kernel(result_ref, gtok_ref, order_ref, own_ref, above_ref, beside_ref, corner_ref):
-    near, far = 2 * HALF * 2 * WO, 2 * HALF * 8
+def late_kernel(
+    act_ref, res_ref, gres_ref, dq_ref, dk_ref, dv_ref, unit_ref, inverse_ref, qkv_ref, down_ref, order_ref,
+    own_ref, above_ref, beside_ref, corner_ref, grad_ref,
+):
+    result = (res_ref[...] + dot_rt(act_ref[...], down_ref[...])).astype(BF)
+    grads = (dq_ref, dk_ref, dv_ref)
+    grad_ref[...] = sum(dot_rt(ref[...], qkv_ref[:, i * C : (i + 1) * C]) for i, ref in enumerate(grads))
+
+    def first_back(part, carry):
+        rows = pl.ds(pl.multiple_of(part * WIN, WIN), WIN)
+        grad = grad_ref[rows, :].astype(BF).astype(F32)
+        grad_ref[rows, :] = gres_ref[rows, :] + normal_back(unit_ref[rows, :], inverse_ref[rows, :], grad)
+        return carry
+
+    lax.fori_loop(0, PARTS, first_back, 0, unroll=4)
+    order = order_ref[...]
+    rows = jnp.concatenate([dot(order, result), dot(order, grad_ref[...].astype(BF))], axis=1)
+    start = 0
+    for ref in (own_ref, above_ref, beside_ref, corner_ref):
+        ref[...] = rows[start : start + ref.shape[0]].astype(BF)
+        start += ref.shape[0]
+
+
+def join_kernel(own_ref, above_ref, beside_ref, corner_ref, order_ref, result_ref, gtok_ref):
+    pieces = [ref[...].astype(F32) for ref in (own_ref, above_ref, beside_ref, corner_ref)]
+    rows = dot(order_ref[...], jnp.concatenate(pieces, axis=0).astype(BF))
     for array, ref in enumerate((result_ref, gtok_ref)):
-        rows = dot(order_ref[...], ref[...])
+        part = rows[:, array * C : (array + 1) * C]
         for level in range(2):
-            for row in range(HALF):
-                place = level * HALF + row
-                at = place * 2 * WO
-                own_ref[array, level, row] = rows[at : at + 2 * WO].astype(BF)
-                above_ref[array, level, row] = rows[near + at : near + at + 2 * WO].astype(BF)
-                at = 2 * near + place * 8
-                beside_ref[array, level, row] = rows[at : at + 8].astype(BF)
-                corner_ref[array, level, row] = rows[far + at : far + at + 8].astype(BF)
-
-
-def join_kernel(own_ref, above_ref, beside_ref, corner_ref, result_ref, gtok_ref):
-    for array, ref in enumerate((result_ref, gtok_ref)):
-        for level in range(2):
-            for row in range(HALF):
-                for start, long_ref, short_ref in ((0, above_ref, corner_ref), (HALF, own_ref, beside_ref)):
-                    rows = long_ref[array, level, row].astype(F32)
-                    first = rows[:8] + short_ref[array, level, row].astype(F32)
-                    ref[level, start + row] = jnp.concatenate([first, rows[8:]], axis=0).astype(BF)
+            for row in range(WA):
+                at = (level * WA + row) * 2 * WO
+                ref[level, row] = part[at : at + 2 * WO].astype(BF)
 
 
 def final_kernel(
@@ -375,25 +401,28 @@
     qkv_ref, proj_ref, up_ref, down_ref, bias_ref,
 ):
     first = core_ref[0] == 0
-    mine = mine_ref[...].astype(F32)[: 9 * C]
-    other = other_ref[...].astype(F32)[: 9 * C]
-    total = jnp.sum(mine * mine) + jnp.sum(other * other)
+    squares = jnp.zeros((C, LANES), F32)
+    for place in range(9):
+        for ref in (mine_ref, other_ref):
+            part = ref[place * C : (place + 1) * C, :].astype(F32)
+            squares = squares + part * part
+    total = jnp.sum(squares)
     factor = jnp.minimum(1.0, math.sqrt(count) / (jnp.sqrt(jnp.full((8, LANES), total)) + 1e-06))[:1]
-    zero = jnp.where(first, mine, other) * factor
-    one = jnp.where(first, other, mine) * factor
 
     def chunk(half, place):
-        return half[place * C : (place + 1) * C]
+        rows = slice(place * C, (place + 1) * C)
+        mine, other = mine_ref[rows, :].astype(F32), other_ref[rows, :].astype(F32)
+        return (jnp.where(first, other, mine) if half else jnp.where(first, mine, other)) * factor
 
     for place in range(6):
-        up_ref[:, place * LANES : (place + 1) * LANES] = chunk(zero, place)
-        down_ref[:, place * LANES : (place + 1) * LANES] = chunk(one, place)
+        up_ref[:, place * LANES : (place + 1) * LANES] = chunk(0, place)
+        down_ref[:, place * LANES : (place + 1) * LANES] = chunk(1, place)
     last = C - LANES
-    left, right = chunk(one, 7), chunk(one, 8)
-    qkv_ref[:, :C] = jnp.concatenate([chunk(zero, 6), left[:, :last]], axis=1)
-    qkv_ref[:, C : 2 * C] = jnp.concatenate([chunk(zero, 7), left[:, last:]], axis=1)
-    qkv_ref[:, 2 * C :] = jnp.concatenate([chunk(zero, 8), right[:, :last]], axis=1)
-    proj_ref[...] = jnp.concatenate([chunk(one, 6), right[:, last:]], axis=1)
+    left, right = chunk(1, 7), chunk(1, 8)
+    qkv_ref[:, :C] = jnp.concatenate([chunk(0, 6), left[:, :last]], axis=1)
+    qkv_ref[:, C : 2 * C] = jnp.concatenate([chunk(0, 7), left[:, last:]], axis=1)
+    qkv_ref[:, 2 * C :] = jnp.concatenate([chunk(0, 8), right[:, :last]], axis=1)
+    proj_ref[...] = jnp.concatenate([chunk(1, 6), right[:, last:]], axis=1)
 
     sums = gbias_ref[...].astype(F32)
     tables = []
@@ -437,10 +466,10 @@
     return lax.ppermute(block, tuple(axes), route)
 
 
-def roll_back_start(result, grad_tokens):
-    wide, narrow = shape(2, 2, HALF, 2 * WO, C, kind=BF), shape(2, 2, HALF, 8, C, kind=BF)
-    order = jnp.asarray(window_order().T, BF)
-    pieces = call(split_kernel, [wide, wide, narrow, narrow], 0, 3)(result, grad_tokens, order)
+def roll_back_start(*arrays):
+    outs = [shape(rows, 2 * C, kind=BF) for rows in (LONG, LONG, SHORT, SHORT)]
+    order = jnp.asarray(split_order(), BF)
+    pieces = call(late_kernel, outs, 0, 11, [pltpu.VMEM((TOKENS, C), F32)])(*arrays, order)
     own, above, beside, corner = pieces
     above = from_next(above, ["lat"], -1)
     corner = from_next(corner, ["lat", "lon"], -1)
@@ -450,7 +479,7 @@
 
 def roll_back_end(pieces):
     whole = shape(2, WA, 2 * WO, C, kind=BF)
-    return call(join_kernel, [whole, whole], 0, 4)(*pieces)
+    return call(join_kernel, [whole, whole], 0, 5)(*pieces, jnp.asarray(join_order(), BF))
 
 
 def gradient_sums(mine, other, bias, pieces):
@@ -474,14 +503,15 @@
 
     own, above, beside, corner = pieces
     outs = [shape(PACKED, LANES, kind=BF), shape(2 * BIAS_ROWS, LANES, kind=BF)]
-    mine, bias = call(first_kernel, outs, 0, 4)(mine, lax.ppermute(other, "lat", pairs), bias, partner(bias, 1))
+    got = lax.ppermute(other, "lat", pairs)
+    mine, bias = call(first_kernel, outs, 0, 5)(mine, got, bias, partner(bias, 2), own[:8, :LANES])
     got = lax.all_to_all(mine.reshape(lat, share, LANES), ("lat", "lon"), 0, 0, axis_index_groups=planes)
-    wide, bias = middle(got, bias, partner(bias, 2), depth, beside[0, 0, 0])
+    wide, bias = middle(got, bias, partner(bias, 4), depth, corner[:8, :LANES])
     got = lax.all_to_all(wide, "lon", 0, 0, axis_index_groups=columns)
-    wide, bias = middle(got, bias, partner(bias, 4), lat, above[0, 0, 0, :8])
+    wide, bias = middle(got, bias, partner(bias, 1), lat, above[:8, :LANES])
     bias = added(bias, partner(bias, 8))
     mine = lax.all_to_all(wide, ("lat", "lon"), 0, 0, axis_index_groups=planes)
-    wait = added(bias[:8], corner[0, 0, 0, :, :LANES])
+    wait = added(bias[:8], beside[:8, :LANES])
     mine = lax.dynamic_update_slice(mine, wait[None], (lat - 1, share - 8, 0))
     other = lax.ppermute(mine, "lat", pairs)
     return mine.reshape(PACKED, LANES), other.reshape(PACKED, LANES), bias
@@ -499,31 +529,25 @@
     corner = from_next(corner, ["lat", "lon"], 1)
     beside = from_next(beside, ["lon"], 1)
     back = table_back()
-    order = jnp.asarray(table_order(), BF)
-    bias = call(bias_kernel, [shape(2, HEADS * WIN, WIN)], 1, 2)(last, earth_bias, order)[0]
+    bias = call(bias_kernel, [shape(2, HEADS * WIN, WIN)], 1, 1)(last, earth_bias)[0]
 
     def tokens_of(width, kind=BF):
         return pltpu.VMEM((TOKENS, width), kind)
 
-    outs = [
-        shape(TOKENS, C, kind=BF),
-        shape(TOKENS, C, kind=BF),
-        shape(PACKED, LANES),
-        shape(PACKED, LANES, kind=BF),
-        shape(2 * BIAS_ROWS, LANES, kind=BF),
-    ]
-    scratch = [pltpu.VMEM((SOURCES, C), F32), tokens_of(C), tokens_of(C), pltpu.VMEM((2, BIAS_ROWS, LANES), F32)]
-    scratch += [tokens_of(C)] * 4 + [pltpu.VMEM((PARTS, HEADS * WIN, WIN), BF), tokens_of(C), tokens_of(C, F32)]
-    scratch += [tokens_of(C), tokens_of(HID, F32)] + [tokens_of(HID)] * 3 + [tokens_of(C, F32)]
-    scratch += [tokens_of(C)] * 5 + [pltpu.VMEM((2, HEADS * WIN, WIN), F32)]
-    scratch += [pltpu.VMEM((2 * HEADS, WIN, WIDE), F32), pltpu.VMEM((C, WIN), F32)]
-    scratch += [tokens_of(C, F32)] * 5
-    result, grad_tokens, *grads = call(block_kernel, outs, 1, 11, scratch, limit=LARGE)(
+    outs = [shape(PACKED, LANES), shape(PACKED, LANES, kind=BF), shape(2, HEADS * WIN, WIN)]
+    outs += [shape(TOKENS, HID, kind=BF), shape(TOKENS, C), shape(TOKENS, C)]
+    outs += [shape(TOKENS, C, kind=BF)] * 3 + [shape(TOKENS, C)] * 2
+    scratch = [pltpu.VMEM((SOURCES, C), F32)] + [tokens_of(C)] * 6
+    scratch += [pltpu.VMEM((PARTS, HEADS * WIN, WIN), BF), tokens_of(C), tokens_of(C), tokens_of(HID, F32)]
+    scratch += [tokens_of(HID)] * 2 + [tokens_of(C)] * 2 + [pltpu.VMEM((C, WIN), F32)] + [tokens_of(C, F32)] * 3
+    mine, other, scores, *late = call(block_kernel, outs, 1, 11, scratch, limit=LARGE)(
         core, tokens, cotangent, below, beside, corner, jnp.asarray(window_order(), BF),
         w_qkv, w_proj, w_up, w_down.T, bias,
     )
-    pieces = roll_back_start(result, grad_tokens)
-    sums = gradient_sums(*grads, pieces)
+    scratch = [pltpu.VMEM((2, BIAS_ROWS, LANES), F32)]
+    grad_table = call(table_kernel, [shape(2 * BIAS_ROWS, LANES, kind=BF)], 0, 1, scratch)(scores)[0]
+    pieces = roll_back_start(*late, w_qkv, w_down.T)
+    sums = gradient_sums(mine, other, grad_table, pieces)
     result, grad_tokens = roll_back_end(pieces)
 
     count = w_qkv.size + w_proj.size + w_up.size + w_down.size + earth_bias.size * bands

time: 95.9 us -> 90.8 us (0.947)
  starting transfers between devices: 51.8 us -> 47.7 us
  waiting for transfers between devices: 18.1 us -> 16.8 us
  Pallas kernels: 20.8 us -> 21.9 us
    ppermute x4, waiting for transfers between devices: 8.91 us -> 5.25 us  [partner(): return lax.ppermute(block, 'lon', [(i, i ^ distance) for i in range(lon)])]
    pallas_call x4 -> x5, Pallas kernels: 5.3 us -> 8.35 us  [the longest x1 2.28 us: on_device(): call(table_kernel, [shape(2 * BIAS_ROWS, LANES, kind=BF)], 0, 1, scratch)]
    all_to_all x1, waiting for transfers between devices: 1.86 us -> 3.69 us  [gradient_sums(): got = lax.all_to_all(wide, 'lon', 0, 0, axis_index_groups=columns)]
    ppermute x1, starting transfers between devices: 6.2 us -> 4.41 us  [gradient_sums(): other = lax.ppermute(mine, 'lat', pairs)]
    pallas_call x1, Pallas kernels: 11.8 us -> 10 us  [on_device(): call(block_kernel, outs, 1, 11, scratch, limit=LARGE)]
    ppermute x6, waiting for transfers between devices: 6.24 us -> 7.82 us  [from_next(): return lax.ppermute(block, tuple(axes), route)]
    ppermute x4, starting transfers between devices: 8.5 us -> 7.1 us  [partner(): return lax.ppermute(block, 'lon', [(i, i ^ distance) for i in range(lon)])]
    all_to_all x1, starting transfers between devices: 6.78 us -> 5.48 us  [gradient_sums(): mine = lax.all_to_all(wide, ('lat', 'lon'), 0, 0, axis_index_groups=planes)]
  transfers between devices with their start and end apart: 15 -> 15, of which waited for: 8 -> 8; matrix products, arithmetic and copies ran while one was open for 0% -> 0% of each run, Pallas kernels for 5% -> 8%
where the time goes in v5:
time: 90.8 us; the launch traced here: 90.3 us
  starting transfers between devices  47.7 us (53%)
  Pallas kernels  21.9 us (24%)
  waiting for transfers between devices  16.8 us (19%)
  local copies, waits for them, and re-layouts  2.95 us (3%)
    ppermute x6, starting transfers between devices, from_next(): return lax.ppermute(block, tuple(axes), route)  20.5 us
    pallas_call x1, Pallas kernels, on_device(): call(block_kernel, outs, 1, 11, scratch, limit=LARGE)  10 us
    ppermute x6, waiting for transfers between devices, from_next(): return lax.ppermute(block, tuple(axes), route)  7.82 us
    ppermute x4, starting transfers between devices, partner(): return lax.ppermute(block, 'lon', [(i, i ^ distance) for i in range(lon)])  7.1 us
    all_to_all x1, starting transfers between devices, gradient_sums(): got = lax.all_to_all(wide, 'lon', 0, 0, axis_index_groups=columns)  6.12 us
    all_to_all x1, starting transfers between devices, gradient_sums(): mine = lax.all_to_all(wide, ('lat', 'lon'), 0, 0, axis_index_groups=planes)  5.48 us
    ppermute x4, waiting for transfers between devices, partner(): return lax.ppermute(block, 'lon', [(i, i ^ distance) for i in range(lon)])  5.25 us
    ppermute x1, starting transfers between devices, gradient_sums(): other = lax.ppermute(mine, 'lat', pairs)  4.41 us
  transfers between devices with their start and end apart: 15, of which 8 were waited for; matrix products, arithmetic and copies ran while one was open for 0% of the time, Pallas kernels for 8%

profile of v5, /device:TPU:1, one launch (start us, length us, event | category | flops | bytes accessed | tf_op | source)
XLA Modules:
  0.0 90.3 jit_solution(13280838507987045766)
XLA Ops:
  0.6 1.0 %copy-done = bf16[2,12,24,192]{3,2,1,0:T(8,128)(2,1)S(1)} copy-done((bf16[2,12,24,192]{3,2,1,0:T(8,128)(2,1)S(1)}, bf16[2,12,24,192]{3,2,1,0:T(8,128)(2,1)}, u32[]{:S(2)}) %copy-start) | copy-done | bytes 221208
  1.6 1.0 %copy-done.2 = bf16[2,12,24,192]{3,2,1,0:T(8,128)(2,1)S(1)} copy-done((bf16[2,12,24,192]{3,2,1,0:T(8,128)(2,1)S(1)}, bf16[2,12,24,192]{3,2,1,0:T(8,128)(2,1)}, u32[]{:S(2)}) %copy-start.2) | copy-done | bytes 221208
  2.6 3.3 %collective-permute-start = (bf16[2,2,6,24,192]{4,3,2,1,0:T(8,128)(2,1)S(1)}, bf16[2,2,6,24,192]{4,3,2,1,0:T(8,128)(2,1)S(1)}, u32[]{:S(2)}, u32[]{:S(2)}) collective-permute-start(bf16[2,2,6,24,192]{4,3,2,1,0:T(8,128)(2,1)S(1)} %get-tuple-element.38), channel_id=1, source_target_pairs={{16,0},{32,16},{48,32},{64,48},{80,64},{96,80},{112,96},{128,112},... | collective-permute-start | bytes 663560 | tf_op jit(solution)/shard_map/ppermute | solution.py:466
  5.9 4.9 %collective-permute-start.1 = (bf16[2,2,6,8,192]{4,3,2,1,0:T(8,128)(2,1)S(1)}, bf16[2,2,6,8,192]{4,3,2,1,0:T(8,128)(2,1)S(1)}, u32[]{:S(2)}, u32[]{:S(2)}) collective-permute-start(bf16[2,2,6,8,192]{4,3,2,1,0:T(8,128)(2,1)S(1)} %get-tuple-element.39), channel_id=1, source_target_pairs={{1,0},{2,1},{3,2},{4,3},{5,4},{6,5},{7,6},{8,7},{9,8},{10,9},{11,1... | collective-permute-start | bytes 221192 | tf_op jit(solution)/shard_map/ppermute | solution.py:466
  10.8 5.2 %collective-permute-start.2 = (bf16[2,2,6,8,192]{4,3,2,1,0:T(8,128)(2,1)S(1)}, bf16[2,2,6,8,192]{4,3,2,1,0:T(8,128)(2,1)S(1)}, u32[]{:S(2)}, u32[]{:S(2)}) collective-permute-start(bf16[2,2,6,8,192]{4,3,2,1,0:T(8,128)(2,1)S(1)} %get-tuple-element.40), channel_id=1, source_target_pairs={{17,0},{18,1},{19,2},{20,3},{21,4},{22,5},{23,6},{24,7},{25,8},{26... | collective-permute-start | bytes 221192 | tf_op jit(solution)/shard_map/ppermute | solution.py:466
  16.0 1.0 %copy-done.10 = f32[1,1,6,24,552]{4,3,2,1,0:T(8,128)S(1)} copy-done((f32[1,1,6,24,552]{4,3,2,1,0:T(8,128)S(1)}, f32[1,1,6,24,552]{4,3,2,1,0:T(8,128)}, u32[]{:S(2)}) %copy-start.10) | copy-done | bytes 317976
  17.0 2.2 %shard_map.163.bias_ref = f32[2,864,144]{2,1,0:T(8,128)S(1)} custom-call(s32[1]{0:T(128)} %bitcast.2.last_ref, f32[1,1,6,24,552]{4,3,2,1,0:T(8,128)S(1)} %copy-done.10), custom_call_target="tpu_custom_call" | custom-call | tf_op jit(solution)/shard_map/pallas_call | solution.py:532
  19.2 10.0 %shard_map.164 = (f32[1792,128]{1,0:T(8,128)S(1)}, bf16[1792,128]{1,0:T(8,128)(2,1)S(1)}, f32[2,864,144]{2,1,0:T(8,128)S(1)}, bf16[576,768]{1,0:T(8,128)(2,1)S(1...) custom-call(s32[1]{0:T(128)} %bitcast.core_ref, ...), custom_call_target="tpu_custom_call" | custom-call | tf_op jit(solution)/shard_map/pallas_call | solution.py:543
  29.4 2.3 %shard_map.167.own_ref = bf16[352,128]{1,0:T(8,128)(2,1)S(1)} custom-call(f32[2,864,144]{2,1,0:T(8,128)S(1)} %get-tuple-element.57.ds_ref), custom_call_target="tpu_custom_call" | custom-call | tf_op jit(solution)/shard_map/pallas_call | solution.py:548
  31.7 0.3 collective-permute-start.7
  32.0 1.6 %shard_map.165 = (bf16[216,384]{1,0:T(8,128)(2,1)S(1)}, bf16[216,384]{1,0:T(8,128)(2,1)S(1)}, bf16[72,384]{1,0:T(8,128)(2,1)S(1)}, bf16[72,384]{1,0:T(8,128)(2,1)S(1)}) custom-call(bf16[576,768]{1,0:T(8,128)(2,1)S(1)} %get-tuple-element.41.act_ref, f32[576,192]{1,0:T(8,128)S(1)} %get-tuple-element.42.res_ref, f32[576,192]{1,0:T(8,128)S(1)} %get-tuple-element.43.gres_ref, ...), custom_call_target="tpu_custom_call" | custom-call | tf_op jit(solution)/shard_map/pallas_call | solution.py:472
  33.7 2.1 %collective-permute-done.7.came_ref = bf16[352,128]{1,0:T(8,128)(2,1)S(1)} collective-permute-done((bf16[352,128]{1,0:T(8,128)(2,1)S(1)}, bf16[352,128]{1,0:T(8,128)(2,1)S(1)}, u32[]{:S(2)}, u32[]{:S(2)}) %collective-permute-start.7) | collective-permute-done | bytes 90144 | tf_op jit(solution)/shard_map/ppermute | solution.py:498
  35.8 0.9 shard_map.168
  36.6 4.0 %all-to-all-start = ((bf16[16,112,128]{2,1,0:T(8,128)(2,1)}), bf16[16,112,128]{2,1,0:T(8,128)(2,1)S(1)}, u32[]{:S(2)}, u32[]{:S(2)}) async-start(bf16[16,112,128]{2,1,0:T(8,128)(2,1)} %bitcast.3), calls=%async_computation | async-start | bytes 917504 | tf_op jit(solution)/shard_map/all_to_all | solution.py:508
  40.6 2.7 %collective-permute-start.8 = (bf16[352,128]{1,0:T(8,128)(2,1)S(1)}, bf16[352,128]{1,0:T(8,128)(2,1)S(1)}, u32[]{:S(2)}, u32[]{:S(2)}) collective-permute-start(bf16[352,128]{1,0:T(8,128)(2,1)S(1)} %get-tuple-element.59.own_ref), channel_id=1, source_target_pairs={{0,4},{1,5},{2,6},{3,7},{4,0},{5,1},{6,2},{7,3},{8,12},{9,13},{10,... | collective-permute-start | bytes 270344 | tf_op jit(solution)/shard_map/ppermute | solution.py:498
  43.3 3.9 %collective-permute-start.5 = (bf16[72,384]{1,0:T(8,128)(2,1)S(1)}, bf16[72,384]{1,0:T(8,128)(2,1)S(1)}, u32[]{:S(2)}, u32[]{:S(2)}) collective-permute-start(bf16[72,384]{1,0:T(8,128)(2,1)S(1)} %get-tuple-element.52), channel_id=1, source_target_pairs={{255,0},{240,1},{241,2},{242,3},{243,4},{244,5},{245,6},{246,7},{2... | collective-permute-start | bytes 165896 | tf_op jit(solution)/shard_map/ppermute | solution.py:466
  47.3 3.5 %collective-permute-done.5.corner_ref = bf16[72,384]{1,0:T(8,128)(2,1)S(1)} collective-permute-done((bf16[72,384]{1,0:T(8,128)(2,1)S(1)}, bf16[72,384]{1,0:T(8,128)(2,1)S(1)}, u32[]{:S(2)}, u32[]{:S(2)}) %collective-permute-start.5) | collective-permute-done | bytes 55328 | tf_op jit(solution)/shard_map/ppermute | solution.py:466
  50.8 0.8 shard_map.169
  51.6 6.1 %all-to-all-start.1 = ((bf16[8,112,128]{2,1,0:T(8,128)(2,1)}), bf16[8,112,128]{2,1,0:T(8,128)(2,1)S(1)}, u32[]{:S(2)}, u32[]{:S(2)}) async-start(bf16[8,112,128]{2,1,0:T(8,128)(2,1)} %get-tuple-element.60), calls=%async_computation.1 | async-start | bytes 458752 | tf_op jit(solution)/shard_map/all_to_all | solution.py:510
  57.7 1.9 %collective-permute-start.3 = (bf16[216,384]{1,0:T(8,128)(2,1)S(1)}, bf16[216,384]{1,0:T(8,128)(2,1)S(1)}, u32[]{:S(2)}, u32[]{:S(2)}) collective-permute-start(bf16[216,384]{1,0:T(8,128)(2,1)S(1)} %get-tuple-element.50), channel_id=1, source_target_pairs={{240,0},{0,16},{16,32},{32,48},{48,64},{64,80},{80,96},{96,112},{1... | collective-permute-start | bytes 497672 | tf_op jit(solution)/shard_map/ppermute | solution.py:466
  59.6 2.3 %collective-permute-done.3.above_ref = bf16[216,384]{1,0:T(8,128)(2,1)S(1)} collective-permute-done((bf16[216,384]{1,0:T(8,128)(2,1)S(1)}, bf16[216,384]{1,0:T(8,128)(2,1)S(1)}, u32[]{:S(2)}, u32[]{:S(2)}) %collective-permute-start.3) | collective-permute-done | bytes 165920 | tf_op jit(solution)/shard_map/ppermute | solution.py:466
  61.9 1.1 %collective-permute-done.9.came_ref = bf16[352,128]{1,0:T(8,128)(2,1)S(1)} collective-permute-done((bf16[352,128]{1,0:T(8,128)(2,1)S(1)}, bf16[352,128]{1,0:T(8,128)(2,1)S(1)}, u32[]{:S(2)}, u32[]{:S(2)}) %collective-permute-start.9) | collective-permute-done | bytes 90144 | tf_op jit(solution)/shard_map/ppermute | solution.py:498
  63.0 3.7 %all-to-all-done.1.got_ref = bf16[8,112,128]{2,1,0:T(8,128)(2,1)S(1)} async-done(((bf16[8,112,128]{2,1,0:T(8,128)(2,1)}), bf16[8,112,128]{2,1,0:T(8,128)(2,1)S(1)}, u32[]{:S(2)}, u32[]{:S(2)}) %all-to-all-start.1) | async-done | bytes 229408 | tf_op jit(solution)/shard_map/all_to_all | solution.py:510
  66.7 0.8 shard_map.170
  67.5 5.5 %all-to-all-start.2 = ((bf16[16,112,128]{2,1,0:T(8,128)(2,1)}), bf16[16,112,128]{2,1,0:T(8,128)(2,1)S(1)}, u32[]{:S(2)}, u32[]{:S(2)}) async-start(bf16[16,112,128]{2,1,0:T(8,128)(2,1)} %get-tuple-element.62), calls=%async_computation.2 | async-start | bytes 917504 | tf_op jit(solution)/shard_map/all_to_all | solution.py:513
  73.0 4.1 %collective-permute-start.10 = (bf16[352,128]{1,0:T(8,128)(2,1)S(1)}, bf16[352,128]{1,0:T(8,128)(2,1)S(1)}, u32[]{:S(2)}, u32[]{:S(2)}) collective-permute-start(bf16[352,128]{1,0:T(8,128)(2,1)S(1)} %get-tuple-element.63), channel_id=1, source_target_pairs={{0,8},{1,9},{2,10},{3,11},{4,12},{5,13},{6,14},{7,15},{8,0},{9,1},... | collective-permute-start | bytes 270344 | tf_op jit(solution)/shard_map/ppermute | solution.py:498
  77.1 1.3 %collective-permute-start.4 = (bf16[72,384]{1,0:T(8,128)(2,1)S(1)}, bf16[72,384]{1,0:T(8,128)(2,1)S(1)}, u32[]{:S(2)}, u32[]{:S(2)}) collective-permute-start(bf16[72,384]{1,0:T(8,128)(2,1)S(1)} %get-tuple-element.51), channel_id=1, source_target_pairs={{15,0},{0,1},{1,2},{2,3},{3,4},{4,5},{5,6},{6,7},{7,8},{8,9},{9,10... | collective-permute-start | bytes 165896 | tf_op jit(solution)/shard_map/ppermute | solution.py:466
  78.4 2.1 %collective-permute-done.10 = bf16[352,128]{1,0:T(8,128)(2,1)S(1)} collective-permute-done((bf16[352,128]{1,0:T(8,128)(2,1)S(1)}, bf16[352,128]{1,0:T(8,128)(2,1)S(1)}, u32[]{:S(2)}, u32[]{:S(2)}) %collective-permute-start.10) | collective-permute-done | bytes 90144 | tf_op jit(solution)/shard_map/ppermute | solution.py:498
  80.5 2.0 %collective-permute-done.4.beside_ref = bf16[72,384]{1,0:T(8,128)(2,1)S(1)} collective-permute-done((bf16[72,384]{1,0:T(8,128)(2,1)S(1)}, bf16[72,384]{1,0:T(8,128)(2,1)S(1)}, u32[]{:S(2)}, u32[]{:S(2)}) %collective-permute-start.4) | collective-permute-done | bytes 55328 | tf_op jit(solution)/shard_map/ppermute | solution.py:466
  82.5 4.4 %collective-permute-start.11 = (bf16[16,112,128]{2,1,0:T(8,128)(2,1)S(1)}, bf16[16,112,128]{2,1,0:T(8,128)(2,1)S(1)}, u32[]{:S(2)}, u32[]{:S(2)}) collective-permute-start(bf16[16,112,128]{2,1,0:T(8,128)(2,1)S(1)} %fusion.1), channel_id=1, source_target_pairs={{0,16},{16,0},{32,48},{48,32},{64,80},{80,64},{96,112},{112,96},{1... | collective-permute-start | bytes 1376264 | tf_op jit(solution)/shard_map/ppermute | solution.py:516
  86.9 1.4 %shard_map.166 = (bf16[2,12,24,192]{3,2,1,0:T(8,128)(2,1)}, bf16[2,12,24,192]{3,2,1,0:T(8,128)(2,1)}) custom-call(bf16[216,384]{1,0:T(8,128)(2,1)S(1)} %get-tuple-element.49.own_ref, bf16[216,384]{1,0:T(8,128)(2,1)S(1)} %collective-permute-done.3.above_ref, bf16[72,384]{1,0:T(8,128)(2,1)S(1)} %collective-permute-done.4.beside_ref, ...), custom_call_target="tpu_custom_call" | custom-call | tf_op jit(solution)/shard_map/pallas_call | solution.py:482
  88.4 1.9 %shard_map.171 = (f32[192,576]{1,0:T(8,128)}, f32[192,192]{1,0:T(8,128)}, f32[192,768]{1,0:T(8,128)}, f32[192,768]{1,0:T(8,128)}, f32[1,1,6,24,552]{4,3,2,1,0:T(8,128)}) custom-call(s32[1]{0:T(128)} %bitcast.core_ref, bf16[1792,128]{1,0:T(8,128)(2,1)S(1)} %bitcast.11, bf16[1792,128]{1,0:T(8,128)(2,1)S(1)} %bitcast.14, ...), custom_call_target="tpu_custom_call" | custom-call | tf_op jit(solution)/shard_map/pallas_call | solution.py:555
  (39 shorter events, 0.4 us)
Async XLA Ops:
  0.6 1.0 %copy-start = (bf16[2,12,24,192]{3,2,1,0:T(8,128)(2,1)S(1)}, bf16[2,12,24,192]{3,2,1,0:T(8,128)(2,1)}, u32[]{:S(2)}) copy-start(bf16[2,12,24,192]{3,2,1,0:T(8,128)(2,1)} %tokens_ref.3) | copy-start | bytes 663556
  1.6 1.0 %copy-start.2 = (bf16[2,12,24,192]{3,2,1,0:T(8,128)(2,1)S(1)}, bf16[2,12,24,192]{3,2,1,0:T(8,128)(2,1)}, u32[]{:S(2)}) copy-start(bf16[2,12,24,192]{3,2,1,0:T(8,128)(2,1)} %cots_ref.1) | copy-start | bytes 663556
  2.6 16.6 %copy-start.1 = (bf16[2,12,24,192]{3,2,1,0:T(8,128)(2,1)S(1)}, bf16[2,12,24,192]{3,2,1,0:T(8,128)(2,1)}, u32[]{:S(2)}) copy-start(bf16[2,12,24,192]{3,2,1,0:T(8,128)(2,1)} %tokens_ref.3) | copy-start | bytes 663556
  2.6 16.6 %copy-start.3 = (bf16[2,12,24,192]{3,2,1,0:T(8,128)(2,1)S(1)}, bf16[2,12,24,192]{3,2,1,0:T(8,128)(2,1)}, u32[]{:S(2)}) copy-start(bf16[2,12,24,192]{3,2,1,0:T(8,128)(2,1)} %cots_ref.1) | copy-start | bytes 663556
  2.6 16.6 %copy-start.4 = (bf16[768,192]{0,1:T(8,128)(2,1)S(1)}, bf16[768,192]{0,1:T(8,128)(2,1)}, u32[]{:S(2)}) copy-start(bf16[768,192]{0,1:T(8,128)(2,1)} %param.15) | copy-start | bytes 884740
  2.6 16.6 %copy-start.6 = (bf16[192,576]{1,0:T(8,128)(2,1)S(1)}, bf16[192,576]{1,0:T(8,128)(2,1)}, u32[]{:S(2)}) copy-start(bf16[192,576]{1,0:T(8,128)(2,1)} %qkv_ref.3) | copy-start | bytes 663556
  2.6 16.6 %copy-start.7 = (bf16[576,768]{1,0:T(8,128)(2,1)S(1)}, bf16[576,768]{1,0:T(8,128)(2,1)}, u32[]{:S(2)}) copy-start(bf16[576,768]{1,0:T(8,128)(2,1)} %constant.31.clone.order_ref) | copy-start | bytes 2654212
  2.6 16.5 %collective-permute-start = (bf16[2,2,6,24,192]{4,3,2,1,0:T(8,128)(2,1)S(1)}, bf16[2,2,6,24,192]{4,3,2,1,0:T(8,128)(2,1)S(1)}, u32[]{:S(2)}, u32[]{:S(2)}) collective-permute-start(bf16[2,2,6,24,192]{4,3,2,1,0:T(8,128)(2,1)S(1)} %get-tuple-element.38), channel_id=1, source_target_pairs={{16,0},{32,16},{48,32},{64,48},{80,64},{96,80},{112,96},{128,112},... | collective-permute-start | bytes 663560 | tf_op jit(solution)/shard_map/ppermute | solution.py:466
  5.9 13.2 %collective-permute-start.1 = (bf16[2,2,6,8,192]{4,3,2,1,0:T(8,128)(2,1)S(1)}, bf16[2,2,6,8,192]{4,3,2,1,0:T(8,128)(2,1)S(1)}, u32[]{:S(2)}, u32[]{:S(2)}) collective-permute-start(bf16[2,2,6,8,192]{4,3,2,1,0:T(8,128)(2,1)S(1)} %get-tuple-element.39), channel_id=1, source_target_pairs={{1,0},{2,1},{3,2},{4,3},{5,4},{6,5},{7,6},{8,7},{9,8},{10,9},{11,1... | collective-permute-start | bytes 221192 | tf_op jit(solution)/shard_map/ppermute | solution.py:466
  10.8 8.3 %collective-permute-start.2 = (bf16[2,2,6,8,192]{4,3,2,1,0:T(8,128)(2,1)S(1)}, bf16[2,2,6,8,192]{4,3,2,1,0:T(8,128)(2,1)S(1)}, u32[]{:S(2)}, u32[]{:S(2)}) collective-permute-start(bf16[2,2,6,8,192]{4,3,2,1,0:T(8,128)(2,1)S(1)} %get-tuple-element.40), channel_id=1, source_target_pairs={{17,0},{18,1},{19,2},{20,3},{21,4},{22,5},{23,6},{24,7},{25,8},{26... | collective-permute-start | bytes 221192 | tf_op jit(solution)/shard_map/ppermute | solution.py:466
  16.0 1.0 %copy-start.10 = (f32[1,1,6,24,552]{4,3,2,1,0:T(8,128)S(1)}, f32[1,1,6,24,552]{4,3,2,1,0:T(8,128)}, u32[]{:S(2)}) copy-start(f32[1,1,6,24,552]{4,3,2,1,0:T(8,128)} %table_ref.1) | copy-start | bytes 953860
  16.9 2.3 %copy-start.11 = (bf16[192,768]{1,0:T(8,128)(2,1)S(1)}, bf16[192,768]{1,0:T(8,128)(2,1)}, u32[]{:S(2)}) copy-start(bf16[192,768]{1,0:T(8,128)(2,1)} %up_ref.1) | copy-start | bytes 884740
  16.9 2.3 %copy-start.12 = (bf16[192,192]{1,0:T(8,128)(2,1)S(1)}, bf16[192,192]{1,0:T(8,128)(2,1)}, u32[]{:S(2)}) copy-start(bf16[192,192]{1,0:T(8,128)(2,1)} %proj_ref.1) | copy-start | bytes 221188
  29.3 2.7 %copy-start.9 = (bf16[576,576]{1,0:T(8,128)(2,1)S(1)}, bf16[576,576]{1,0:T(8,128)(2,1)}, u32[]{:S(2)}) copy-start(bf16[576,576]{1,0:T(8,128)(2,1)} %constant.32.clone.order_ref) | copy-start | bytes 1990660
  29.3 6.5 %collective-permute-start.6 = (bf16[1792,128]{1,0:T(8,128)(2,1)S(1)}, bf16[1792,128]{1,0:T(8,128)(2,1)S(1)}, u32[]{:S(2)}, u32[]{:S(2)}) collective-permute-start(bf16[1792,128]{1,0:T(8,128)(2,1)S(1)} %get-tuple-element.56), channel_id=1, source_target_pairs={{0,16},{16,0},{32,48},{48,32},{64,80},{80,64},{96,112},{112,96},{1... | collective-permute-start | bytes 1376264 | tf_op jit(solution)/shard_map/ppermute | solution.py:506
  31.7 4.0 %collective-permute-start.7 = (bf16[352,128]{1,0:T(8,128)(2,1)S(1)}, bf16[352,128]{1,0:T(8,128)(2,1)S(1)}, u32[]{:S(2)}, u32[]{:S(2)}) collective-permute-start(bf16[352,128]{1,0:T(8,128)(2,1)S(1)} %shard_map.167.own_ref), channel_id=1, source_target_pairs={{0,2},{1,3},{2,0},{3,1},{4,6},{5,7},{6,4},{7,5},{8,10},{9,11},{10,... | collective-permute-start | bytes 270344 | tf_op jit(solution)/shard_map/ppermute | solution.py:498
  36.6 50.3 %copy-start.8 = (bf16[576,576]{1,0:T(8,128)(2,1)S(1)}, bf16[576,576]{1,0:T(8,128)(2,1)}, u32[]{:S(2)}) copy-start(bf16[576,576]{1,0:T(8,128)(2,1)} %constant.33.clone.order_ref) | copy-start | bytes 1990660
  36.6 14.2 %all-to-all-start = ((bf16[16,112,128]{2,1,0:T(8,128)(2,1)}), bf16[16,112,128]{2,1,0:T(8,128)(2,1)S(1)}, u32[]{:S(2)}, u32[]{:S(2)}) async-start(bf16[16,112,128]{2,1,0:T(8,128)(2,1)} %bitcast.3), calls=%async_computation | async-start | bytes 917504 | tf_op jit(solution)/shard_map/all_to_all | solution.py:508
  40.6 10.2 %collective-permute-start.8 = (bf16[352,128]{1,0:T(8,128)(2,1)S(1)}, bf16[352,128]{1,0:T(8,128)(2,1)S(1)}, u32[]{:S(2)}, u32[]{:S(2)}) collective-permute-start(bf16[352,128]{1,0:T(8,128)(2,1)S(1)} %get-tuple-element.59.own_ref), channel_id=1, source_target_pairs={{0,4},{1,5},{2,6},{3,7},{4,0},{5,1},{6,2},{7,3},{8,12},{9,13},{10,... | collective-permute-start | bytes 270344 | tf_op jit(solution)/shard_map/ppermute | solution.py:498
  43.3 7.5 %collective-permute-start.5 = (bf16[72,384]{1,0:T(8,128)(2,1)S(1)}, bf16[72,384]{1,0:T(8,128)(2,1)S(1)}, u32[]{:S(2)}, u32[]{:S(2)}) collective-permute-start(bf16[72,384]{1,0:T(8,128)(2,1)S(1)} %get-tuple-element.52), channel_id=1, source_target_pairs={{255,0},{240,1},{241,2},{242,3},{243,4},{244,5},{245,6},{246,7},{2... | collective-permute-start | bytes 165896 | tf_op jit(solution)/shard_map/ppermute | solution.py:466
  51.6 36.8 %copy-start.5 = (bf16[2,384,552]{2,1,0:T(8,128)(2,1)S(1)}, bf16[2,384,552]{2,1,0:T(8,128)(2,1)}, u32[]{:S(2)}) copy-start(bf16[2,384,552]{2,1,0:T(8,128)(2,1)} %constant.34.clone.back_ref) | copy-start | bytes 2543620
  51.6 15.1 %all-to-all-start.1 = ((bf16[8,112,128]{2,1,0:T(8,128)(2,1)}), bf16[8,112,128]{2,1,0:T(8,128)(2,1)S(1)}, u32[]{:S(2)}, u32[]{:S(2)}) async-start(bf16[8,112,128]{2,1,0:T(8,128)(2,1)} %get-tuple-element.60), calls=%async_computation.1 | async-start | bytes 458752 | tf_op jit(solution)/shard_map/all_to_all | solution.py:510
  57.7 4.2 %collective-permute-start.3 = (bf16[216,384]{1,0:T(8,128)(2,1)S(1)}, bf16[216,384]{1,0:T(8,128)(2,1)S(1)}, u32[]{:S(2)}, u32[]{:S(2)}) collective-permute-start(bf16[216,384]{1,0:T(8,128)(2,1)S(1)} %get-tuple-element.50), channel_id=1, source_target_pairs={{240,0},{0,16},{16,32},{32,48},{48,64},{64,80},{80,96},{96,112},{1... | collective-permute-start | bytes 497672 | tf_op jit(solution)/shard_map/ppermute | solution.py:466
  59.6 3.4 %collective-permute-start.9 = (bf16[352,128]{1,0:T(8,128)(2,1)S(1)}, bf16[352,128]{1,0:T(8,128)(2,1)S(1)}, u32[]{:S(2)}, u32[]{:S(2)}) collective-permute-start(bf16[352,128]{1,0:T(8,128)(2,1)S(1)} %get-tuple-element.61.own_ref), channel_id=1, source_target_pairs={{0,1},{1,0},{2,3},{3,2},{4,5},{5,4},{6,7},{7,6},{8,9},{9,8},{10,11... | collective-permute-start | bytes 270344 | tf_op jit(solution)/shard_map/ppermute | solution.py:498
  67.5 15.0 %all-to-all-start.2 = ((bf16[16,112,128]{2,1,0:T(8,128)(2,1)}), bf16[16,112,128]{2,1,0:T(8,128)(2,1)S(1)}, u32[]{:S(2)}, u32[]{:S(2)}) async-start(bf16[16,112,128]{2,1,0:T(8,128)(2,1)} %get-tuple-element.62), calls=%async_computation.2 | async-start | bytes 917504 | tf_op jit(solution)/shard_map/all_to_all | solution.py:513
  73.0 7.5 %collective-permute-start.10 = (bf16[352,128]{1,0:T(8,128)(2,1)S(1)}, bf16[352,128]{1,0:T(8,128)(2,1)S(1)}, u32[]{:S(2)}, u32[]{:S(2)}) collective-permute-start(bf16[352,128]{1,0:T(8,128)(2,1)S(1)} %get-tuple-element.63), channel_id=1, source_target_pairs={{0,8},{1,9},{2,10},{3,11},{4,12},{5,13},{6,14},{7,15},{8,0},{9,1},... | collective-permute-start | bytes 270344 | tf_op jit(solution)/shard_map/ppermute | solution.py:498
  77.1 5.4 %collective-permute-start.4 = (bf16[72,384]{1,0:T(8,128)(2,1)S(1)}, bf16[72,384]{1,0:T(8,128)(2,1)S(1)}, u32[]{:S(2)}, u32[]{:S(2)}) collective-permute-start(bf16[72,384]{1,0:T(8,128)(2,1)S(1)} %get-tuple-element.51), channel_id=1, source_target_pairs={{15,0},{0,1},{1,2},{2,3},{3,4},{4,5},{5,6},{6,7},{7,8},{8,9},{9,10... | collective-permute-start | bytes 165896 | tf_op jit(solution)/shard_map/ppermute | solution.py:466
  82.5 5.9 %collective-permute-start.11 = (bf16[16,112,128]{2,1,0:T(8,128)(2,1)S(1)}, bf16[16,112,128]{2,1,0:T(8,128)(2,1)S(1)}, u32[]{:S(2)}, u32[]{:S(2)}) collective-permute-start(bf16[16,112,128]{2,1,0:T(8,128)(2,1)S(1)} %fusion.1), channel_id=1, source_target_pairs={{0,16},{16,0},{32,48},{48,32},{64,80},{80,64},{96,112},{112,96},{1... | collective-permute-start | bytes 1376264 | tf_op jit(solution)/shard_map/ppermute | solution.py:516

commit v6 on v5

--- a/solution.py
+++ b/solution.py
@@ -165,9 +165,9 @@
 def block_kernel(
     core_ref, tokens_ref, cots_ref, below_ref, beside_ref, corner_ref, order_ref,
     qkv_ref, proj_ref, up_ref, down_ref, bias_ref,
-    mine_ref, other_ref, ds_ref, act_ref, res_ref, gres_ref, dq_ref, dk_ref, dv_ref, unit_ref, inverse_ref,
+    mine_ref, other_ref, gbias_ref, act_ref, res_ref, gres_ref, dq_ref, dk_ref, dv_ref, unit_ref, inverse_ref,
     source_ref, x_ref, cot_ref, normed_ref, q_ref, k_ref, v_ref, prob_ref, att_ref, two_ref, upper_ref, gact_ref,
-    gup_ref, gmix_ref, gatt_ref, turned_ref, unit_two_ref, inverse_two_ref, mean_ref,
+    gup_ref, gmix_ref, gatt_ref, ds_ref, bsum_ref, turned_ref, unit_two_ref, inverse_two_ref, mean_ref,
 ):
     lane = lax.broadcasted_iota(jnp.int32, (1, C), 1) // HEAD
     half_masks = [(lane == head).astype(F32).astype(BF) for head in range(HEADS)]
@@ -317,8 +317,6 @@
     mine_ref[9 * C :, :] = jnp.zeros((PACKED - 9 * C, LANES), F32)
     other_ref[9 * C :, :] = jnp.zeros((PACKED - 9 * C, LANES), BF)
 
-
-def table_kernel(ds_ref, gbias_ref, bsum_ref):
     row = lax.broadcasted_iota(jnp.int32, (2 * WA, WIDE), 0)
 
     def table_grad(level, head):
@@ -534,18 +532,17 @@
     def tokens_of(width, kind=BF):
         return pltpu.VMEM((TOKENS, width), kind)
 
-    outs = [shape(PACKED, LANES), shape(PACKED, LANES, kind=BF), shape(2, HEADS * WIN, WIN)]
+    outs = [shape(PACKED, LANES), shape(PACKED, LANES, kind=BF), shape(2 * BIAS_ROWS, LANES, kind=BF)]
     outs += [shape(TOKENS, HID, kind=BF), shape(TOKENS, C), shape(TOKENS, C)]
     outs += [shape(TOKENS, C, kind=BF)] * 3 + [shape(TOKENS, C)] * 2
     scratch = [pltpu.VMEM((SOURCES, C), F32)] + [tokens_of(C)] * 6
     scratch += [pltpu.VMEM((PARTS, HEADS * WIN, WIN), BF), tokens_of(C), tokens_of(C), tokens_of(HID, F32)]
-    scratch += [tokens_of(HID)] * 2 + [tokens_of(C)] * 2 + [pltpu.VMEM((C, WIN), F32)] + [tokens_of(C, F32)] * 3
-    mine, other, scores, *late = call(block_kernel, outs, 1, 11, scratch, limit=LARGE)(
+    scratch += [tokens_of(HID)] * 2 + [tokens_of(C)] * 2 + [pltpu.VMEM((2, HEADS * WIN, WIN), F32)]
+    scratch += [pltpu.VMEM((2, BIAS_ROWS, LANES), F32), pltpu.VMEM((C, WIN), F32)] + [tokens_of(C, F32)] * 3
+    mine, other, grad_table, *late = call(block_kernel, outs, 1, 11, scratch, limit=LARGE)(
         core, tokens, cotangent, below, beside, corner, jnp.asarray(window_order(), BF),
         w_qkv, w_proj, w_up, w_down.T, bias,
     )
-    scratch = [pltpu.VMEM((2, BIAS_ROWS, LANES), F32)]
-    grad_table = call(table_kernel, [shape(2 * BIAS_ROWS, LANES, kind=BF)], 0, 1, scratch)(scores)[0]
     pieces = roll_back_start(*late, w_qkv, w_down.T)
     sums = gradient_sums(mine, other, grad_table, pieces)
     result, grad_tokens = roll_back_end(pieces)

time: 90.8 us -> 89.1 us (0.981)
  Pallas kernels: 21.9 us -> 20 us
    pallas_call x1 -> x0, Pallas kernels: 2.28 us -> none  [on_device(): call(table_kernel, [shape(2 * BIAS_ROWS, LANES, kind=BF)], 0, 1, scratch)]
  transfers between devices with their start and end apart: 15 -> 15, of which waited for: 8 -> 8; matrix products, arithmetic and copies ran while one was open for 0% -> 0% of each run, Pallas kernels for 8% -> 6%
where the time goes in v6:
time: 89.1 us; the launch traced here: 88.6 us
  starting transfers between devices  47.1 us (53%)
  Pallas kernels  20 us (22%)
  waiting for transfers between devices  17.7 us (20%)
  local copies, waits for them, and re-layouts  2.95 us (3%)
    ppermute x6, starting transfers between devices, from_next(): return lax.ppermute(block, tuple(axes), route)  20 us
    pallas_call x1, Pallas kernels, on_device(): call(block_kernel, outs, 1, 11, scratch, limit=LARGE)  10.4 us
    ppermute x6, waiting for transfers between devices, from_next(): return lax.ppermute(block, tuple(axes), route)  8.08 us
    ppermute x4, starting transfers between devices, partner(): return lax.ppermute(block, 'lon', [(i, i ^ distance) for i in range(lon)])  6.87 us
    all_to_all x1, starting transfers between devices, gradient_sums(): got = lax.all_to_all(wide, 'lon', 0, 0, axis_index_groups=columns)  5.93 us
    all_to_all x1, starting transfers between devices, gradient_sums(): mine = lax.all_to_all(wide, ('lat', 'lon'), 0, 0, axis_index_groups=planes)  5.68 us
    ppermute x4, waiting for transfers between devices, partner(): return lax.ppermute(block, 'lon', [(i, i ^ distance) for i in range(lon)])  5.61 us
    ppermute x1, starting transfers between devices, gradient_sums(): other = lax.ppermute(mine, 'lat', pairs)  4.36 us
  transfers between devices with their start and end apart: 15, of which 8 were waited for; matrix products, arithmetic and copies ran while one was open for 0% of the time, Pallas kernels for 6%

profile of v6, /device:TPU:1, one launch (start us, length us, event | category | flops | bytes accessed | tf_op | source)
XLA Modules:
  0.0 88.6 jit_solution(6936460782714434222)
XLA Ops:
  0.6 1.0 %copy-done = bf16[2,12,24,192]{3,2,1,0:T(8,128)(2,1)S(1)} copy-done((bf16[2,12,24,192]{3,2,1,0:T(8,128)(2,1)S(1)}, bf16[2,12,24,192]{3,2,1,0:T(8,128)(2,1)}, u32[]{:S(2)}) %copy-start) | copy-done | bytes 221208
  1.6 1.0 %copy-done.2 = bf16[2,12,24,192]{3,2,1,0:T(8,128)(2,1)S(1)} copy-done((bf16[2,12,24,192]{3,2,1,0:T(8,128)(2,1)S(1)}, bf16[2,12,24,192]{3,2,1,0:T(8,128)(2,1)}, u32[]{:S(2)}) %copy-start.2) | copy-done | bytes 221208
  2.6 3.3 %collective-permute-start = (bf16[2,2,6,24,192]{4,3,2,1,0:T(8,128)(2,1)S(1)}, bf16[2,2,6,24,192]{4,3,2,1,0:T(8,128)(2,1)S(1)}, u32[]{:S(2)}, u32[]{:S(2)}) collective-permute-start(bf16[2,2,6,24,192]{4,3,2,1,0:T(8,128)(2,1)S(1)} %get-tuple-element.38), channel_id=1, source_target_pairs={{16,0},{32,16},{48,32},{64,48},{80,64},{96,80},{112,96},{128,112},... | collective-permute-start | bytes 663560 | tf_op jit(solution)/shard_map/ppermute | solution.py:464
  5.9 4.9 %collective-permute-start.1 = (bf16[2,2,6,8,192]{4,3,2,1,0:T(8,128)(2,1)S(1)}, bf16[2,2,6,8,192]{4,3,2,1,0:T(8,128)(2,1)S(1)}, u32[]{:S(2)}, u32[]{:S(2)}) collective-permute-start(bf16[2,2,6,8,192]{4,3,2,1,0:T(8,128)(2,1)S(1)} %get-tuple-element.39), channel_id=1, source_target_pairs={{1,0},{2,1},{3,2},{4,3},{5,4},{6,5},{7,6},{8,7},{9,8},{10,9},{11,1... | collective-permute-start | bytes 221192 | tf_op jit(solution)/shard_map/ppermute | solution.py:464
  10.8 5.2 %collective-permute-start.2 = (bf16[2,2,6,8,192]{4,3,2,1,0:T(8,128)(2,1)S(1)}, bf16[2,2,6,8,192]{4,3,2,1,0:T(8,128)(2,1)S(1)}, u32[]{:S(2)}, u32[]{:S(2)}) collective-permute-start(bf16[2,2,6,8,192]{4,3,2,1,0:T(8,128)(2,1)S(1)} %get-tuple-element.40), channel_id=1, source_target_pairs={{17,0},{18,1},{19,2},{20,3},{21,4},{22,5},{23,6},{24,7},{25,8},{26... | collective-permute-start | bytes 221192 | tf_op jit(solution)/shard_map/ppermute | solution.py:464
  16.0 1.0 %copy-done.10 = f32[1,1,6,24,552]{4,3,2,1,0:T(8,128)S(1)} copy-done((f32[1,1,6,24,552]{4,3,2,1,0:T(8,128)S(1)}, f32[1,1,6,24,552]{4,3,2,1,0:T(8,128)}, u32[]{:S(2)}) %copy-start.10) | copy-done | bytes 317976
  17.0 2.2 %shard_map.163.bias_ref = f32[2,864,144]{2,1,0:T(8,128)S(1)} custom-call(s32[1]{0:T(128)} %bitcast.2.last_ref, f32[1,1,6,24,552]{4,3,2,1,0:T(8,128)S(1)} %copy-done.10), custom_call_target="tpu_custom_call" | custom-call | tf_op jit(solution)/shard_map/pallas_call | solution.py:530
  19.2 10.4 %shard_map.164 = (f32[1792,128]{1,0:T(8,128)S(1)}, bf16[1792,128]{1,0:T(8,128)(2,1)S(1)}, bf16[352,128]{1,0:T(8,128)(2,1)S(1)}, bf16[576,768]{1,0:T(8,128)(2,1)S...) custom-call(s32[1]{0:T(128)} %bitcast.core_ref, ...), custom_call_target="tpu_custom_call" | custom-call | tf_op jit(solution)/shard_map/pallas_call | solution.py:542
  29.7 0.2 collective-permute-start.6
  29.8 0.3 collective-permute-start.7
  30.1 1.7 %shard_map.165 = (bf16[216,384]{1,0:T(8,128)(2,1)S(1)}, bf16[216,384]{1,0:T(8,128)(2,1)S(1)}, bf16[72,384]{1,0:T(8,128)(2,1)S(1)}, bf16[72,384]{1,0:T(8,128)(2,1)S(1)}) custom-call(bf16[576,768]{1,0:T(8,128)(2,1)S(1)} %get-tuple-element.41.act_ref, f32[576,192]{1,0:T(8,128)S(1)} %get-tuple-element.42.res_ref, f32[576,192]{1,0:T(8,128)S(1)} %get-tuple-element.43.gres_ref, ...), custom_call_target="tpu_custom_call" | custom-call | tf_op jit(solution)/shard_map/pallas_call | solution.py:470
  31.8 2.3 %collective-permute-done.7.came_ref = bf16[352,128]{1,0:T(8,128)(2,1)S(1)} collective-permute-done((bf16[352,128]{1,0:T(8,128)(2,1)S(1)}, bf16[352,128]{1,0:T(8,128)(2,1)S(1)}, u32[]{:S(2)}, u32[]{:S(2)}) %collective-permute-start.7) | collective-permute-done | bytes 90144 | tf_op jit(solution)/shard_map/ppermute | solution.py:496
  34.1 0.9 shard_map.167
  35.0 4.1 %all-to-all-start = ((bf16[16,112,128]{2,1,0:T(8,128)(2,1)}), bf16[16,112,128]{2,1,0:T(8,128)(2,1)S(1)}, u32[]{:S(2)}, u32[]{:S(2)}) async-start(bf16[16,112,128]{2,1,0:T(8,128)(2,1)} %bitcast.3), calls=%async_computation | async-start | bytes 917504 | tf_op jit(solution)/shard_map/all_to_all | solution.py:506
  39.1 2.7 %collective-permute-start.8 = (bf16[352,128]{1,0:T(8,128)(2,1)S(1)}, bf16[352,128]{1,0:T(8,128)(2,1)S(1)}, u32[]{:S(2)}, u32[]{:S(2)}) collective-permute-start(bf16[352,128]{1,0:T(8,128)(2,1)S(1)} %get-tuple-element.59.own_ref), channel_id=1, source_target_pairs={{0,4},{1,5},{2,6},{3,7},{4,0},{5,1},{6,2},{7,3},{8,12},{9,13},{10,... | collective-permute-start | bytes 270344 | tf_op jit(solution)/shard_map/ppermute | solution.py:496
  41.8 3.6 %collective-permute-start.5 = (bf16[72,384]{1,0:T(8,128)(2,1)S(1)}, bf16[72,384]{1,0:T(8,128)(2,1)S(1)}, u32[]{:S(2)}, u32[]{:S(2)}) collective-permute-start(bf16[72,384]{1,0:T(8,128)(2,1)S(1)} %get-tuple-element.52), channel_id=1, source_target_pairs={{255,0},{240,1},{241,2},{242,3},{243,4},{244,5},{245,6},{246,7},{2... | collective-permute-start | bytes 165896 | tf_op jit(solution)/shard_map/ppermute | solution.py:464
  45.4 3.8 %collective-permute-done.5.corner_ref = bf16[72,384]{1,0:T(8,128)(2,1)S(1)} collective-permute-done((bf16[72,384]{1,0:T(8,128)(2,1)S(1)}, bf16[72,384]{1,0:T(8,128)(2,1)S(1)}, u32[]{:S(2)}, u32[]{:S(2)}) %collective-permute-start.5) | collective-permute-done | bytes 55328 | tf_op jit(solution)/shard_map/ppermute | solution.py:464
  49.2 0.8 shard_map.168
  50.0 5.9 %all-to-all-start.1 = ((bf16[8,112,128]{2,1,0:T(8,128)(2,1)}), bf16[8,112,128]{2,1,0:T(8,128)(2,1)S(1)}, u32[]{:S(2)}, u32[]{:S(2)}) async-start(bf16[8,112,128]{2,1,0:T(8,128)(2,1)} %get-tuple-element.60), calls=%async_computation.1 | async-start | bytes 458752 | tf_op jit(solution)/shard_map/all_to_all | solution.py:508
  55.9 1.8 %collective-permute-start.3 = (bf16[216,384]{1,0:T(8,128)(2,1)S(1)}, bf16[216,384]{1,0:T(8,128)(2,1)S(1)}, u32[]{:S(2)}, u32[]{:S(2)}) collective-permute-start(bf16[216,384]{1,0:T(8,128)(2,1)S(1)} %get-tuple-element.50), channel_id=1, source_target_pairs={{240,0},{0,16},{16,32},{32,48},{48,64},{64,80},{80,96},{96,112},{1... | collective-permute-start | bytes 497672 | tf_op jit(solution)/shard_map/ppermute | solution.py:464
  57.8 2.3 %collective-permute-done.3.above_ref = bf16[216,384]{1,0:T(8,128)(2,1)S(1)} collective-permute-done((bf16[216,384]{1,0:T(8,128)(2,1)S(1)}, bf16[216,384]{1,0:T(8,128)(2,1)S(1)}, u32[]{:S(2)}, u32[]{:S(2)}) %collective-permute-start.3) | collective-permute-done | bytes 165920 | tf_op jit(solution)/shard_map/ppermute | solution.py:464
  60.1 1.1 %collective-permute-done.9.came_ref = bf16[352,128]{1,0:T(8,128)(2,1)S(1)} collective-permute-done((bf16[352,128]{1,0:T(8,128)(2,1)S(1)}, bf16[352,128]{1,0:T(8,128)(2,1)S(1)}, u32[]{:S(2)}, u32[]{:S(2)}) %collective-permute-start.9) | collective-permute-done | bytes 90144 | tf_op jit(solution)/shard_map/ppermute | solution.py:496
  61.1 3.9 %all-to-all-done.1.got_ref = bf16[8,112,128]{2,1,0:T(8,128)(2,1)S(1)} async-done(((bf16[8,112,128]{2,1,0:T(8,128)(2,1)}), bf16[8,112,128]{2,1,0:T(8,128)(2,1)S(1)}, u32[]{:S(2)}, u32[]{:S(2)}) %all-to-all-start.1) | async-done | bytes 229408 | tf_op jit(solution)/shard_map/all_to_all | solution.py:508
  65.1 0.8 shard_map.169
  65.9 5.7 %all-to-all-start.2 = ((bf16[16,112,128]{2,1,0:T(8,128)(2,1)}), bf16[16,112,128]{2,1,0:T(8,128)(2,1)S(1)}, u32[]{:S(2)}, u32[]{:S(2)}) async-start(bf16[16,112,128]{2,1,0:T(8,128)(2,1)} %get-tuple-element.62), calls=%async_computation.2 | async-start | bytes 917504 | tf_op jit(solution)/shard_map/all_to_all | solution.py:511
  71.6 3.9 %collective-permute-start.10 = (bf16[352,128]{1,0:T(8,128)(2,1)S(1)}, bf16[352,128]{1,0:T(8,128)(2,1)S(1)}, u32[]{:S(2)}, u32[]{:S(2)}) collective-permute-start(bf16[352,128]{1,0:T(8,128)(2,1)S(1)} %get-tuple-element.63), channel_id=1, source_target_pairs={{0,8},{1,9},{2,10},{3,11},{4,12},{5,13},{6,14},{7,15},{8,0},{9,1},... | collective-permute-start | bytes 270344 | tf_op jit(solution)/shard_map/ppermute | solution.py:496
  75.5 1.3 %collective-permute-start.4 = (bf16[72,384]{1,0:T(8,128)(2,1)S(1)}, bf16[72,384]{1,0:T(8,128)(2,1)S(1)}, u32[]{:S(2)}, u32[]{:S(2)}) collective-permute-start(bf16[72,384]{1,0:T(8,128)(2,1)S(1)} %get-tuple-element.51), channel_id=1, source_target_pairs={{15,0},{0,1},{1,2},{2,3},{3,4},{4,5},{5,6},{6,7},{7,8},{8,9},{9,10... | collective-permute-start | bytes 165896 | tf_op jit(solution)/shard_map/ppermute | solution.py:464
  76.7 2.2 %collective-permute-done.10 = bf16[352,128]{1,0:T(8,128)(2,1)S(1)} collective-permute-done((bf16[352,128]{1,0:T(8,128)(2,1)S(1)}, bf16[352,128]{1,0:T(8,128)(2,1)S(1)}, u32[]{:S(2)}, u32[]{:S(2)}) %collective-permute-start.10) | collective-permute-done | bytes 90144 | tf_op jit(solution)/shard_map/ppermute | solution.py:496
  79.0 2.0 %collective-permute-done.4.beside_ref = bf16[72,384]{1,0:T(8,128)(2,1)S(1)} collective-permute-done((bf16[72,384]{1,0:T(8,128)(2,1)S(1)}, bf16[72,384]{1,0:T(8,128)(2,1)S(1)}, u32[]{:S(2)}, u32[]{:S(2)}) %collective-permute-start.4) | collective-permute-done | bytes 55328 | tf_op jit(solution)/shard_map/ppermute | solution.py:464
  80.9 4.4 %collective-permute-start.11 = (bf16[16,112,128]{2,1,0:T(8,128)(2,1)S(1)}, bf16[16,112,128]{2,1,0:T(8,128)(2,1)S(1)}, u32[]{:S(2)}, u32[]{:S(2)}) collective-permute-start(bf16[16,112,128]{2,1,0:T(8,128)(2,1)S(1)} %fusion.1), channel_id=1, source_target_pairs={{0,16},{16,0},{32,48},{48,32},{64,80},{80,64},{96,112},{112,96},{1... | collective-permute-start | bytes 1376264 | tf_op jit(solution)/shard_map/ppermute | solution.py:514
  85.3 1.4 %shard_map.166 = (bf16[2,12,24,192]{3,2,1,0:T(8,128)(2,1)}, bf16[2,12,24,192]{3,2,1,0:T(8,128)(2,1)}) custom-call(bf16[216,384]{1,0:T(8,128)(2,1)S(1)} %get-tuple-element.49.own_ref, bf16[216,384]{1,0:T(8,128)(2,1)S(1)} %collective-permute-done.3.above_ref, bf16[72,384]{1,0:T(8,128)(2,1)S(1)} %collective-permute-done.4.beside_ref, ...), custom_call_target="tpu_custom_call" | custom-call | tf_op jit(solution)/shard_map/pallas_call | solution.py:480
  86.7 1.9 %shard_map.170 = (f32[192,576]{1,0:T(8,128)}, f32[192,192]{1,0:T(8,128)}, f32[192,768]{1,0:T(8,128)}, f32[192,768]{1,0:T(8,128)}, f32[1,1,6,24,552]{4,3,2,1,0:T(8,128)}) custom-call(s32[1]{0:T(128)} %bitcast.core_ref, bf16[1792,128]{1,0:T(8,128)(2,1)S(1)} %bitcast.11, bf16[1792,128]{1,0:T(8,128)(2,1)S(1)} %bitcast.14, ...), custom_call_target="tpu_custom_call" | custom-call | tf_op jit(solution)/shard_map/pallas_call | solution.py:552
  (38 shorter events, 0.2 us)
Async XLA Ops:
  0.6 1.0 %copy-start = (bf16[2,12,24,192]{3,2,1,0:T(8,128)(2,1)S(1)}, bf16[2,12,24,192]{3,2,1,0:T(8,128)(2,1)}, u32[]{:S(2)}) copy-start(bf16[2,12,24,192]{3,2,1,0:T(8,128)(2,1)} %tokens_ref.3) | copy-start | bytes 663556
  1.6 1.0 %copy-start.2 = (bf16[2,12,24,192]{3,2,1,0:T(8,128)(2,1)S(1)}, bf16[2,12,24,192]{3,2,1,0:T(8,128)(2,1)}, u32[]{:S(2)}) copy-start(bf16[2,12,24,192]{3,2,1,0:T(8,128)(2,1)} %cots_ref.1) | copy-start | bytes 663556
  2.6 16.6 %copy-start.1 = (bf16[2,12,24,192]{3,2,1,0:T(8,128)(2,1)S(1)}, bf16[2,12,24,192]{3,2,1,0:T(8,128)(2,1)}, u32[]{:S(2)}) copy-start(bf16[2,12,24,192]{3,2,1,0:T(8,128)(2,1)} %tokens_ref.3) | copy-start | bytes 663556
  2.6 16.6 %copy-start.3 = (bf16[2,12,24,192]{3,2,1,0:T(8,128)(2,1)S(1)}, bf16[2,12,24,192]{3,2,1,0:T(8,128)(2,1)}, u32[]{:S(2)}) copy-start(bf16[2,12,24,192]{3,2,1,0:T(8,128)(2,1)} %cots_ref.1) | copy-start | bytes 663556
  2.6 16.6 %copy-start.4 = (bf16[768,192]{0,1:T(8,128)(2,1)S(1)}, bf16[768,192]{0,1:T(8,128)(2,1)}, u32[]{:S(2)}) copy-start(bf16[768,192]{0,1:T(8,128)(2,1)} %param.15) | copy-start | bytes 884740
  2.6 16.6 %copy-start.6 = (bf16[192,576]{1,0:T(8,128)(2,1)S(1)}, bf16[192,576]{1,0:T(8,128)(2,1)}, u32[]{:S(2)}) copy-start(bf16[192,576]{1,0:T(8,128)(2,1)} %qkv_ref.3) | copy-start | bytes 663556
  2.6 16.6 %copy-start.7 = (bf16[576,768]{1,0:T(8,128)(2,1)S(1)}, bf16[576,768]{1,0:T(8,128)(2,1)}, u32[]{:S(2)}) copy-start(bf16[576,768]{1,0:T(8,128)(2,1)} %constant.31.clone.order_ref) | copy-start | bytes 2654212
  2.6 16.5 %collective-permute-start = (bf16[2,2,6,24,192]{4,3,2,1,0:T(8,128)(2,1)S(1)}, bf16[2,2,6,24,192]{4,3,2,1,0:T(8,128)(2,1)S(1)}, u32[]{:S(2)}, u32[]{:S(2)}) collective-permute-start(bf16[2,2,6,24,192]{4,3,2,1,0:T(8,128)(2,1)S(1)} %get-tuple-element.38), channel_id=1, source_target_pairs={{16,0},{32,16},{48,32},{64,48},{80,64},{96,80},{112,96},{128,112},... | collective-permute-start | bytes 663560 | tf_op jit(solution)/shard_map/ppermute | solution.py:464
  5.9 13.2 %collective-permute-start.1 = (bf16[2,2,6,8,192]{4,3,2,1,0:T(8,128)(2,1)S(1)}, bf16[2,2,6,8,192]{4,3,2,1,0:T(8,128)(2,1)S(1)}, u32[]{:S(2)}, u32[]{:S(2)}) collective-permute-start(bf16[2,2,6,8,192]{4,3,2,1,0:T(8,128)(2,1)S(1)} %get-tuple-element.39), channel_id=1, source_target_pairs={{1,0},{2,1},{3,2},{4,3},{5,4},{6,5},{7,6},{8,7},{9,8},{10,9},{11,1... | collective-permute-start | bytes 221192 | tf_op jit(solution)/shard_map/ppermute | solution.py:464
  10.8 8.3 %collective-permute-start.2 = (bf16[2,2,6,8,192]{4,3,2,1,0:T(8,128)(2,1)S(1)}, bf16[2,2,6,8,192]{4,3,2,1,0:T(8,128)(2,1)S(1)}, u32[]{:S(2)}, u32[]{:S(2)}) collective-permute-start(bf16[2,2,6,8,192]{4,3,2,1,0:T(8,128)(2,1)S(1)} %get-tuple-element.40), channel_id=1, source_target_pairs={{17,0},{18,1},{19,2},{20,3},{21,4},{22,5},{23,6},{24,7},{25,8},{26... | collective-permute-start | bytes 221192 | tf_op jit(solution)/shard_map/ppermute | solution.py:464
  16.0 1.0 %copy-start.10 = (f32[1,1,6,24,552]{4,3,2,1,0:T(8,128)S(1)}, f32[1,1,6,24,552]{4,3,2,1,0:T(8,128)}, u32[]{:S(2)}) copy-start(f32[1,1,6,24,552]{4,3,2,1,0:T(8,128)} %table_ref.1) | copy-start | bytes 953860
  16.9 2.3 %copy-start.11 = (bf16[192,768]{1,0:T(8,128)(2,1)S(1)}, bf16[192,768]{1,0:T(8,128)(2,1)}, u32[]{:S(2)}) copy-start(bf16[192,768]{1,0:T(8,128)(2,1)} %up_ref.1) | copy-start | bytes 884740
  16.9 2.3 %copy-start.12 = (bf16[192,192]{1,0:T(8,128)(2,1)S(1)}, bf16[192,192]{1,0:T(8,128)(2,1)}, u32[]{:S(2)}) copy-start(bf16[192,192]{1,0:T(8,128)(2,1)} %proj_ref.1) | copy-start | bytes 221188
  19.2 10.9 %copy-start.9 = (bf16[576,576]{1,0:T(8,128)(2,1)S(1)}, bf16[576,576]{1,0:T(8,128)(2,1)}, u32[]{:S(2)}) copy-start(bf16[576,576]{1,0:T(8,128)(2,1)} %constant.32.clone.order_ref) | copy-start | bytes 1990660
  29.7 4.4 %collective-permute-start.6 = (bf16[1792,128]{1,0:T(8,128)(2,1)S(1)}, bf16[1792,128]{1,0:T(8,128)(2,1)S(1)}, u32[]{:S(2)}, u32[]{:S(2)}) collective-permute-start(bf16[1792,128]{1,0:T(8,128)(2,1)S(1)} %get-tuple-element.56), channel_id=1, source_target_pairs={{0,16},{16,0},{32,48},{48,32},{64,80},{80,64},{96,112},{112,96},{1... | collective-permute-start | bytes 1376264 | tf_op jit(solution)/shard_map/ppermute | solution.py:504
  29.8 4.3 %collective-permute-start.7 = (bf16[352,128]{1,0:T(8,128)(2,1)S(1)}, bf16[352,128]{1,0:T(8,128)(2,1)S(1)}, u32[]{:S(2)}, u32[]{:S(2)}) collective-permute-start(bf16[352,128]{1,0:T(8,128)(2,1)S(1)} %get-tuple-element.57.own_ref), channel_id=1, source_target_pairs={{0,2},{1,3},{2,0},{3,1},{4,6},{5,7},{6,4},{7,5},{8,10},{9,11},{10,... | collective-permute-start | bytes 270344 | tf_op jit(solution)/shard_map/ppermute | solution.py:496
  35.0 50.3 %copy-start.8 = (bf16[576,576]{1,0:T(8,128)(2,1)S(1)}, bf16[576,576]{1,0:T(8,128)(2,1)}, u32[]{:S(2)}) copy-start(bf16[576,576]{1,0:T(8,128)(2,1)} %constant.33.clone.order_ref) | copy-start | bytes 1990660
  35.0 14.2 %all-to-all-start = ((bf16[16,112,128]{2,1,0:T(8,128)(2,1)}), bf16[16,112,128]{2,1,0:T(8,128)(2,1)S(1)}, u32[]{:S(2)}, u32[]{:S(2)}) async-start(bf16[16,112,128]{2,1,0:T(8,128)(2,1)} %bitcast.3), calls=%async_computation | async-start | bytes 917504 | tf_op jit(solution)/shard_map/all_to_all | solution.py:506
  39.1 10.1 %collective-permute-start.8 = (bf16[352,128]{1,0:T(8,128)(2,1)S(1)}, bf16[352,128]{1,0:T(8,128)(2,1)S(1)}, u32[]{:S(2)}, u32[]{:S(2)}) collective-permute-start(bf16[352,128]{1,0:T(8,128)(2,1)S(1)} %get-tuple-element.59.own_ref), channel_id=1, source_target_pairs={{0,4},{1,5},{2,6},{3,7},{4,0},{5,1},{6,2},{7,3},{8,12},{9,13},{10,... | collective-permute-start | bytes 270344 | tf_op jit(solution)/shard_map/ppermute | solution.py:496
  41.8 7.4 %collective-permute-start.5 = (bf16[72,384]{1,0:T(8,128)(2,1)S(1)}, bf16[72,384]{1,0:T(8,128)(2,1)S(1)}, u32[]{:S(2)}, u32[]{:S(2)}) collective-permute-start(bf16[72,384]{1,0:T(8,128)(2,1)S(1)} %get-tuple-element.52), channel_id=1, source_target_pairs={{255,0},{240,1},{241,2},{242,3},{243,4},{244,5},{245,6},{246,7},{2... | collective-permute-start | bytes 165896 | tf_op jit(solution)/shard_map/ppermute | solution.py:464
  50.0 36.8 %copy-start.5 = (bf16[2,384,552]{2,1,0:T(8,128)(2,1)S(1)}, bf16[2,384,552]{2,1,0:T(8,128)(2,1)}, u32[]{:S(2)}) copy-start(bf16[2,384,552]{2,1,0:T(8,128)(2,1)} %constant.34.clone.back_ref) | copy-start | bytes 2543620
  50.0 15.1 %all-to-all-start.1 = ((bf16[8,112,128]{2,1,0:T(8,128)(2,1)}), bf16[8,112,128]{2,1,0:T(8,128)(2,1)S(1)}, u32[]{:S(2)}, u32[]{:S(2)}) async-start(bf16[8,112,128]{2,1,0:T(8,128)(2,1)} %get-tuple-element.60), calls=%async_computation.1 | async-start | bytes 458752 | tf_op jit(solution)/shard_map/all_to_all | solution.py:508
  55.9 4.1 %collective-permute-start.3 = (bf16[216,384]{1,0:T(8,128)(2,1)S(1)}, bf16[216,384]{1,0:T(8,128)(2,1)S(1)}, u32[]{:S(2)}, u32[]{:S(2)}) collective-permute-start(bf16[216,384]{1,0:T(8,128)(2,1)S(1)} %get-tuple-element.50), channel_id=1, source_target_pairs={{240,0},{0,16},{16,32},{32,48},{48,64},{64,80},{80,96},{96,112},{1... | collective-permute-start | bytes 497672 | tf_op jit(solution)/shard_map/ppermute | solution.py:464
  57.8 3.4 %collective-permute-start.9 = (bf16[352,128]{1,0:T(8,128)(2,1)S(1)}, bf16[352,128]{1,0:T(8,128)(2,1)S(1)}, u32[]{:S(2)}, u32[]{:S(2)}) collective-permute-start(bf16[352,128]{1,0:T(8,128)(2,1)S(1)} %get-tuple-element.61.own_ref), channel_id=1, source_target_pairs={{0,1},{1,0},{2,3},{3,2},{4,5},{5,4},{6,7},{7,6},{8,9},{9,8},{10,11... | collective-permute-start | bytes 270344 | tf_op jit(solution)/shard_map/ppermute | solution.py:496
  65.9 15.1 %all-to-all-start.2 = ((bf16[16,112,128]{2,1,0:T(8,128)(2,1)}), bf16[16,112,128]{2,1,0:T(8,128)(2,1)S(1)}, u32[]{:S(2)}, u32[]{:S(2)}) async-start(bf16[16,112,128]{2,1,0:T(8,128)(2,1)} %get-tuple-element.62), calls=%async_computation.2 | async-start | bytes 917504 | tf_op jit(solution)/shard_map/all_to_all | solution.py:511
  71.6 7.4 %collective-permute-start.10 = (bf16[352,128]{1,0:T(8,128)(2,1)S(1)}, bf16[352,128]{1,0:T(8,128)(2,1)S(1)}, u32[]{:S(2)}, u32[]{:S(2)}) collective-permute-start(bf16[352,128]{1,0:T(8,128)(2,1)S(1)} %get-tuple-element.63), channel_id=1, source_target_pairs={{0,8},{1,9},{2,10},{3,11},{4,12},{5,13},{6,14},{7,15},{8,0},{9,1},... | collective-permute-start | bytes 270344 | tf_op jit(solution)/shard_map/ppermute | solution.py:496
  75.5 5.5 %collective-permute-start.4 = (bf16[72,384]{1,0:T(8,128)(2,1)S(1)}, bf16[72,384]{1,0:T(8,128)(2,1)S(1)}, u32[]{:S(2)}, u32[]{:S(2)}) collective-permute-start(bf16[72,384]{1,0:T(8,128)(2,1)S(1)} %get-tuple-element.51), channel_id=1, source_target_pairs={{15,0},{0,1},{1,2},{2,3},{3,4},{4,5},{5,6},{6,7},{7,8},{8,9},{9,10... | collective-permute-start | bytes 165896 | tf_op jit(solution)/shard_map/ppermute | solution.py:464
  80.9 5.8 %collective-permute-start.11 = (bf16[16,112,128]{2,1,0:T(8,128)(2,1)S(1)}, bf16[16,112,128]{2,1,0:T(8,128)(2,1)S(1)}, u32[]{:S(2)}, u32[]{:S(2)}) collective-permute-start(bf16[16,112,128]{2,1,0:T(8,128)(2,1)S(1)} %fusion.1), channel_id=1, source_target_pairs={{0,16},{16,0},{32,48},{48,32},{64,80},{80,64},{96,112},{112,96},{1... | collective-permute-start | bytes 1376264 | tf_op jit(solution)/shard_map/ppermute | solution.py:514
